TPU v7x, 512 devices: a whole 4x8x8 slice. The times are simulated.
512 devices in a mesh: ctx: 64 (over y_lo, z, core), kvh: 8 (over x, y_hi).
Axes of the slice: x: 4, y: 8 (y_hi: 2, y_lo: 4; y = y_hi * 4 + y_lo), z: 8, core: 2. Of those that a mesh axis runs over, the one named last changes fastest.
Arguments:
- hidden: bfloat16 [8192, 4096], P('ctx', 'kvh'), may hold values from -6 to 6
- destination: int32 [8192], P('ctx'), may hold values from 0 to 8191, as said below
- doc_ids: int32 [8192], P('ctx'), may hold values from 0 to 31, never falling along the last dimension, each value on 1 to 1024 neighbouring positions
- w_query: bfloat16 [4096, 2048], P(None, 'kvh'), may hold values from -0.09375 to 0.09375
- w_key: bfloat16 [4096, 1024], P(None, 'kvh'), may hold values from -0.09375 to 0.09375
- w_value: bfloat16 [4096, 1024], P(None, 'kvh'), may hold values from -0.09375 to 0.09375
- q_gain: float32 [128], replicated, may hold values from 0.1 to 1.9
- k_gain: float32 [128], replicated, may hold values from 0.1 to 1.9
Outputs:
- attended: bfloat16 [8192, 2048], P('ctx', 'kvh')
Inputs may be any that keep to these rules, and one draw needn't show every extreme that they name: destination is a permutation of the packed positions; the rows held by one ctx index send at most 4 rows to any one block of 128 consecutive positions, and each ctx index sends exactly 4 to some block. `doc_ids`: documents are numbered in packed order and each covers at most 1024 consecutive positions.
All inputs are finite; a program needn't handle non-finite values.
Results may differ from a plain program's by a relative error of at most 0.009.
Values may be sent and summed in bfloat16 or wider, within the bound.
No kernel may reach another device: no remote copies, remote signals or barrier semaphores. Data moves between devices by JAX's collectives and lax.ppermute only.
A program may use at most 64 MiB of HBM per device.

v0:
```python
import jax
import jax.numpy as jnp
from jax import lax
from jax.sharding import PartitionSpec as P

SPAN = 8


def passed_along(block, axis, distance):
    devices = range(lax.axis_size(axis))
    route = [(i - distance, i) for i in devices if i - distance in devices]
    return lax.ppermute(block, axis, route)


def normalize(tensor, gain_vec):
    return tensor * lax.rsqrt(jnp.mean(tensor * tensor, -1, keepdims=True) + 1e-06) * gain_vec


def rotate(tensor, positions):
    half_dim = tensor.shape[-1] // 2
    exponent = jnp.arange(half_dim, dtype=jnp.float32) * (2.0 / tensor.shape[-1])
    frequency = jnp.power(jnp.float32(1000000.0), -exponent)
    angles = positions.astype(jnp.float32)[:, None] * frequency[None, :]
    cosine = jnp.cos(angles)[:, None, :]
    sine_part = jnp.sin(angles)[:, None, :]
    leading = tensor[..., :half_dim]
    trailing = tensor[..., half_dim:]
    return jnp.concatenate(
        [leading * cosine - trailing * sine_part, trailing * cosine + leading * sine_part], -1
    )


def body(hidden, destination, doc_ids, w_query, w_key, w_value, q_gain, k_gain):
    loop_size = lax.axis_size("ctx")
    ctx_index = lax.axis_index("ctx")
    row_count = destination.shape[0]
    capacity = 2 * row_count // loop_size
    row_ids = jnp.arange(row_count, dtype=jnp.int32)
    target = destination // row_count
    within = destination % row_count
    matches = (target[:, None] == target[None, :]) & (row_ids[None, :] < row_ids[:, None])
    order_in = jnp.sum(matches.astype(jnp.int32), 1)
    owners = jnp.arange(loop_size, dtype=jnp.int32)
    places = jnp.arange(capacity, dtype=jnp.int32)
    picked = (target[None, None, :] == owners[:, None, None]) & (
        order_in[None, None, :] == places[None, :, None]
    )
    picked_flat = picked.reshape(loop_size * capacity, row_count).astype(jnp.bfloat16)
    parcel = jnp.dot(picked_flat, hidden, preferred_element_type=jnp.float32).astype(jnp.bfloat16)
    parcel = parcel.reshape(loop_size, capacity, hidden.shape[1])
    labels = jnp.sum(jnp.where(picked, within[None, None, :] + 1, 0), 2) - 1
    arrived, arrived_at = (
        lax.all_to_all(parcel, "ctx", split_axis=0, concat_axis=0, tiled=True),
        lax.all_to_all(labels, "ctx", split_axis=0, concat_axis=0, tiled=True),
    )
    landing = (arrived_at.reshape(1, -1) == row_ids[:, None]).astype(jnp.bfloat16)
    placed = jnp.dot(
        landing,
        arrived.reshape(loop_size * capacity, hidden.shape[1]),
        preferred_element_type=jnp.float32,
    ).astype(jnp.bfloat16)
    features = lax.all_gather(placed, "kvh", axis=1, tiled=True)
    positions = ctx_index * row_count + row_ids
    doc_count = loop_size // 2
    doc_range = jnp.arange(doc_count, dtype=jnp.int32)
    member = doc_ids[None, :] == doc_range[:, None]
    earliest = jnp.min(jnp.where(member, positions[None, :], loop_size * row_count), 1)
    starts = lax.pmin(earliest, "ctx")
    doc_start = jnp.sum(jnp.where(member, starts[:, None], 0), 0)
    head_dim = q_gain.shape[0]
    queries_raw = jnp.dot(features, w_query, preferred_element_type=jnp.float32).reshape(
        row_count, -1, head_dim
    )
    q_groups = queries_raw.shape[1]
    queries_rot = (rotate(normalize(queries_raw, q_gain), positions) * head_dim ** (-0.5)).astype(
        jnp.bfloat16
    )
    keys_raw = jnp.dot(features, w_key, preferred_element_type=jnp.float32).reshape(
        row_count, 1, head_dim
    )
    key_rows = (
        rotate(normalize(keys_raw, k_gain), positions)
        .astype(jnp.bfloat16)
        .reshape(row_count, head_dim)
    )
    value_rows = jnp.dot(features, w_value, preferred_element_type=jnp.float32).astype(jnp.bfloat16)
    queries = jnp.transpose(queries_rot, (1, 0, 2)).reshape(q_groups * row_count, head_dim)
    q_pos = jnp.tile(positions, q_groups)
    q_first = jnp.tile(doc_start, q_groups)

    def attend(totals, key_block, value_block, begin_at):
        k_pos = begin_at + jnp.arange(key_block.shape[0], dtype=jnp.int32)
        visible = (k_pos[None, :] >= q_first[:, None]) & (k_pos[None, :] <= q_pos[:, None])
        scores = lax.dot_general(
            queries, key_block, (((1,), (1,)), ((), ())), preferred_element_type=jnp.float32
        )
        weights = jnp.where(visible, jnp.exp(scores), jnp.float32(0.0))
        numer = totals[0] + jnp.dot(
            weights.astype(jnp.bfloat16), value_block, preferred_element_type=jnp.float32
        )
        return (numer, totals[1] + jnp.sum(weights, 1))

    def sweep(totals, key_part, value_part, begin_at):
        return attend(totals, key_part, value_part, begin_at)

    initial = (
        jnp.zeros((q_groups * row_count, head_dim), jnp.float32),
        jnp.zeros((q_groups * row_count,), jnp.float32),
    )
    first_totals = sweep(initial, key_rows, value_rows, ctx_index * row_count)

    def advance(state, unused):
        key_block, value_block, begin_at, totals = state
        key_block, value_block = passed_along((key_block, value_block), "ctx", 1)
        begin_at = begin_at - row_count
        return (
            (key_block, value_block, begin_at, sweep(totals, key_block, value_block, begin_at)),
            None,
        )

    state_out, ignored = lax.scan(
        advance, (key_rows, value_rows, ctx_index * row_count, first_totals), None, length=SPAN
    )
    numerator, denominator = state_out[3]
    result = (
        (numerator / denominator[:, None])
        .astype(jnp.bfloat16)
        .reshape(q_groups, row_count, head_dim)
    )
    return jnp.transpose(result, (1, 0, 2)).reshape(row_count, q_groups * head_dim)


def solution(mesh):
    placed = (
        P("ctx", "kvh"),
        P("ctx"),
        P("ctx"),
        P(None, "kvh"),
        P(None, "kvh"),
        P(None, "kvh"),
        P(),
        P(),
    )
    return jax.shard_map(
        body, mesh=mesh, in_specs=placed, out_specs=P("ctx", "kvh"), check_vma=False
    )
```

profile of v0, /device:TPU:8, one launch (start us, length us, event | category | flops | bytes accessed | tf_op | source)
XLA Modules:
  0.0 203.7 jit_solution(8066542704368405383)
XLA Ops:
  6.5 0.8 and_select_fusion.1
  7.6 1.2 select_reduce_fusion
  9.6 14.4 %all-to-all-start = ((s32[64,1,4]{2,1,0:T(1,128)}), s32[64,1,4]{2,1,0:T(1,128)S(1)}, u32[]{:S(2)}, u32[]{:S(2)}) async-start(s32[64,1,4]{2,1,0:T(1,128)} %copy.34), calls=%async_computation | async-start | bytes 65536 | tf_op jit(solution)/shard_map/all_to_all | solution.py:54
  23.9 1.1 convolution_convert_fusion
  25.1 0.8 reshape.249
  25.8 6.9 %all-to-all-done = s32[64,1,4]{2,1,0:T(1,128)S(1)} async-done(((s32[64,1,4]{2,1,0:T(1,128)}), s32[64,1,4]{2,1,0:T(1,128)S(1)}, u32[]{:S(2)}, u32[]{:S(2)}) %all-to-all-start) | async-done | bytes 1056 | tf_op jit(solution)/shard_map/all_to_all | solution.py:54
  32.7 5.5 %all-to-all-start.1 = ((bf16[64,4,512]{2,1,0:T(4,128)(2,1)}), bf16[64,4,512]{2,1,0:T(4,128)(2,1)S(1)}, u32[]{:S(2)}, u32[]{:S(2)}) async-start(bf16[64,4,512]{2,1,0:T(4,128)(2,1)} %reshape.249), calls=%async_computation.1 | async-start | bytes 524288 | tf_op jit(solution)/shard_map/all_to_all | solution.py:53
  38.8 0.7 reduce.5
  39.7 10.6 %all-to-all-done.1 = bf16[64,4,512]{2,1,0:T(4,128)(2,1)S(1)} async-done(((bf16[64,4,512]{2,1,0:T(4,128)(2,1)}), bf16[64,4,512]{2,1,0:T(4,128)(2,1)S(1)}, u32[]{:S(2)}, u32[]{:S(2)}) %all-to-all-start.1) | async-done | bytes 262176 | tf_op jit(solution)/shard_map/all_to_all | solution.py:53
  50.3 0.8 convolution_convert_fusion.1
  51.3 17.0 %pmin.7 = s32[32]{0:T(128)S(1)} all-reduce(s32[32]{0:T(128)S(1)} %select_reduce_fusion.2), channel_id=1, replica_groups=mesh['ctx'=64,'kvh'=8] {'ctx'}, use_global_device_ids=true, to_apply=%region_4.5 | all-reduce | flops 32 | bytes 256 | tf_op jit(solution)/shard_map/pmin | solution.py:68
  69.8 43.0 %all-gather.2.cloned.1.call-done = bf16[128,4096]{1,0:T(8,128)(2,1)} async-done(((bf16[128,512]{1,0:T(8,128)(2,1)}), bf16[128,4096]{1,0:T(8,128)(2,1)}) %all-gather.2.cloned.1.call-update) | async-done | bytes 1048592 | tf_op jit(solution)/shard_map/all_gather | solution.py:62
  112.9 2.2 %multiply_reduce_fusion.1 = (f32[128]{0:T(128)S(1)}, f32[128,128]{0,1:T(8,128)S(1)}) fusion(bf16[128,4096]{1,0:T(8,128)(2,1)} %all-gather.2.cloned.1.call-done, bf16[4096,128]{1,0:T(8,128)(2,1)} %param.14), kind=kOutput, calls=%fused_computation.30 | convolution fusion | flops 134250368 | bytes 2163200 | tf_op jit(solution)/shard_map/dot_general | solution.py:78
  116.9 0.9 multiply_multiply_fusion
  118.4 1.0 fusion.26
  120.0 76.0 %while.21 = (s32[]{:T(128)}, bf16[128,128]{1,0:T(8,128)(2,1)S(1)}, bf16[128,128]{1,0:T(8,128)(2,1)S(1)}, f32[256,128]{1,0:T(8,128)S(1)}, f32[256]{0:T(256)S(1)},...) while((s32[]{:T(128)}, bf16[128,128]{1,0:T(8,128)(2,1)S(1)}, ...), condition=%wide.region_10.11_spmd.clone, body=%wide.region_8.10_spmd.clone.sunk | while | flops 17006724 | bytes 927973 | solution.py:121
  120.0 1.9 collective-permute-start
  121.9 3.7 %collective-permute-start.1 = (bf16[128,128]{1,0:T(8,128)(2,1)S(1)}, bf16[128,128]{1,0:T(8,128)(2,1)S(1)}, u32[]{:S(2)}, u32[]{:S(2)}) collective-permute-start(bf16[128,128]{1,0:T(8,128)(2,1)S(1)} %get-tuple-element.391), channel_id=1, source_target_pairs={{0,8},{8,16},{16,24},{24,32},{32,40},{40,48},{48,56},{56,64},{64,7... | collective-permute-start | bytes 98312 | tf_op jit(solution)/shard_map/while/body/eval_jaxpr/ppermute | solution.py:12
  125.6 1.7 collective-permute-done
  127.6 1.7 collective-permute-done.1
  129.5 1.9 collective-permute-start
  131.4 1.9 collective-permute-start.1
  133.4 3.5 %collective-permute-done = bf16[128,128]{1,0:T(8,128)(2,1)S(1)} collective-permute-done((bf16[128,128]{1,0:T(8,128)(2,1)S(1)}, bf16[128,128]{1,0:T(8,128)(2,1)S(1)}, u32[]{:S(2)}, u32[]{:S(2)}) %collective-permute-start) | collective-permute-done | bytes 32800 | tf_op jit(solution)/shard_map/while/body/eval_jaxpr/ppermute | solution.py:12
  137.1 1.7 collective-permute-done.1
  139.0 1.9 collective-permute-start
  140.9 1.9 collective-permute-start.1
  142.9 3.5 %collective-permute-done = bf16[128,128]{1,0:T(8,128)(2,1)S(1)} collective-permute-done((bf16[128,128]{1,0:T(8,128)(2,1)S(1)}, bf16[128,128]{1,0:T(8,128)(2,1)S(1)}, u32[]{:S(2)}, u32[]{:S(2)}) %collective-permute-start) | collective-permute-done | bytes 32800 | tf_op jit(solution)/shard_map/while/body/eval_jaxpr/ppermute | solution.py:12
  146.6 1.7 collective-permute-done.1
  148.5 1.9 collective-permute-start
  150.4 1.9 collective-permute-start.1
  152.4 3.5 %collective-permute-done = bf16[128,128]{1,0:T(8,128)(2,1)S(1)} collective-permute-done((bf16[128,128]{1,0:T(8,128)(2,1)S(1)}, bf16[128,128]{1,0:T(8,128)(2,1)S(1)}, u32[]{:S(2)}, u32[]{:S(2)}) %collective-permute-start) | collective-permute-done | bytes 32800 | tf_op jit(solution)/shard_map/while/body/eval_jaxpr/ppermute | solution.py:12
  156.1 1.7 collective-permute-done.1
  158.0 1.9 collective-permute-start
  159.9 1.9 collective-permute-start.1
  161.9 3.5 %collective-permute-done = bf16[128,128]{1,0:T(8,128)(2,1)S(1)} collective-permute-done((bf16[128,128]{1,0:T(8,128)(2,1)S(1)}, bf16[128,128]{1,0:T(8,128)(2,1)S(1)}, u32[]{:S(2)}, u32[]{:S(2)}) %collective-permute-start) | collective-permute-done | bytes 32800 | tf_op jit(solution)/shard_map/while/body/eval_jaxpr/ppermute | solution.py:12
  165.6 1.7 collective-permute-done.1
  167.5 1.9 collective-permute-start
  169.4 1.9 collective-permute-start.1
  171.4 3.5 %collective-permute-done = bf16[128,128]{1,0:T(8,128)(2,1)S(1)} collective-permute-done((bf16[128,128]{1,0:T(8,128)(2,1)S(1)}, bf16[128,128]{1,0:T(8,128)(2,1)S(1)}, u32[]{:S(2)}, u32[]{:S(2)}) %collective-permute-start) | collective-permute-done | bytes 32800 | tf_op jit(solution)/shard_map/while/body/eval_jaxpr/ppermute | solution.py:12
  175.1 1.7 collective-permute-done.1
  177.0 1.9 collective-permute-start
  178.9 1.9 collective-permute-start.1
  180.9 3.5 %collective-permute-done = bf16[128,128]{1,0:T(8,128)(2,1)S(1)} collective-permute-done((bf16[128,128]{1,0:T(8,128)(2,1)S(1)}, bf16[128,128]{1,0:T(8,128)(2,1)S(1)}, u32[]{:S(2)}, u32[]{:S(2)}) %collective-permute-start) | collective-permute-done | bytes 32800 | tf_op jit(solution)/shard_map/while/body/eval_jaxpr/ppermute | solution.py:12
  184.6 1.7 collective-permute-done.1
  186.5 1.9 collective-permute-start
  188.4 1.9 collective-permute-start.1
  190.4 3.5 %collective-permute-done = bf16[128,128]{1,0:T(8,128)(2,1)S(1)} collective-permute-done((bf16[128,128]{1,0:T(8,128)(2,1)S(1)}, bf16[128,128]{1,0:T(8,128)(2,1)S(1)}, u32[]{:S(2)}, u32[]{:S(2)}) %collective-permute-start) | collective-permute-done | bytes 32800 | tf_op jit(solution)/shard_map/while/body/eval_jaxpr/ppermute | solution.py:12
  194.1 1.7 collective-permute-done.1
  (114 shorter events, 10.5 us)
Async XLA Ops:
  6.5 109.6 %copy-start = (bf16[4096,256]{1,0:T(8,128)(2,1)S(1)}, bf16[4096,256]{1,0:T(8,128)(2,1)}, u32[]{:S(2)}) copy-start(bf16[4096,256]{1,0:T(8,128)(2,1)} %param.13) | copy-start | bytes 6291460
  6.5 44.7 %copy-start.10 = (s32[128]{0:T(128)S(1)}, s32[128]{0:T(128)}, u32[]{:S(2)}) copy-start(s32[128]{0:T(128)} %param.12) | copy-start | bytes 1540
  9.6 23.2 %all-to-all-start = ((s32[64,1,4]{2,1,0:T(1,128)}), s32[64,1,4]{2,1,0:T(1,128)S(1)}, u32[]{:S(2)}, u32[]{:S(2)}) async-start(s32[64,1,4]{2,1,0:T(1,128)} %copy.34), calls=%async_computation | async-start | bytes 65536 | tf_op jit(solution)/shard_map/all_to_all | solution.py:54
  25.8 89.2 %copy-start.9 = (f32[128]{0:T(128)S(1)}, f32[128]{0:T(128)}, u32[]{:S(2)}) copy-start(f32[128]{0:T(128)} %param.17) | copy-start | bytes 1540
  32.7 17.5 %all-to-all-start.1 = ((bf16[64,4,512]{2,1,0:T(4,128)(2,1)}), bf16[64,4,512]{2,1,0:T(4,128)(2,1)S(1)}, u32[]{:S(2)}, u32[]{:S(2)}) async-start(bf16[64,4,512]{2,1,0:T(4,128)(2,1)} %reshape.249), calls=%async_computation.1 | async-start | bytes 524288 | tf_op jit(solution)/shard_map/all_to_all | solution.py:53
  38.3 74.6 %all-gather.2.cloned.1.call-start = ((), (), s32[]{:S(2)}) async-start(), calls=%async_computation.2 | async-start | bytes 1179648 | tf_op jit(solution)/shard_map/all_gather | solution.py:62
  51.2 18.6 %copy-start.5 = (s32[128]{0:T(128)}, s32[128]{0:T(128)S(1)}, u32[]{:S(2)}) copy-start(s32[128]{0:T(128)S(1)} %iota_add_fusion.1) | copy-start | bytes 1540
  68.4 0.6 copy-start.7
  112.9 3.2 %copy-start.1 = (bf16[128,4096]{1,0:T(8,128)(2,1)S(1)}, bf16[128,4096]{1,0:T(8,128)(2,1)}, u32[]{:S(2)}) copy-start(bf16[128,4096]{1,0:T(8,128)(2,1)} %all-gather.2.cloned.1.call-done) | copy-start | bytes 3145732
  115.3 0.7 copy-start.3
  116.6 2.7 %copy-start.2 = (bf16[4096,128]{1,0:T(8,128)(2,1)S(1)}, bf16[4096,128]{1,0:T(8,128)(2,1)}, u32[]{:S(2)}) copy-start(bf16[4096,128]{1,0:T(8,128)(2,1)} %param.15) | copy-start | bytes 3145732
  116.9 3.1 %copy-start.4 = (bf16[128,128]{1,0:T(8,128)(2,1)S(1)}, bf16[128,128]{1,0:T(8,128)(2,1)}, u32[]{:S(2)}) copy-start(bf16[128,128]{1,0:T(8,128)(2,1)} %copy.38) | copy-start | bytes 98308
  116.9 3.1 %copy-start.6 = (s32[128]{0:T(128)S(1)}, s32[128]{0:T(128)}, u32[]{:S(2)}) copy-start(s32[128]{0:T(128)} %copy-done.5) | copy-start | bytes 1540
  116.9 3.1 %copy-start.8 = (s32[128]{0:T(128)S(1)}, s32[128]{0:T(128)}, u32[]{:S(2)}) copy-start(s32[128]{0:T(128)} %copy-done.7) | copy-start | bytes 1540
  120.0 7.3 %collective-permute-start = (bf16[128,128]{1,0:T(8,128)(2,1)S(1)}, bf16[128,128]{1,0:T(8,128)(2,1)S(1)}, u32[]{:S(2)}, u32[]{:S(2)}) collective-permute-start(bf16[128,128]{1,0:T(8,128)(2,1)S(1)} %get-tuple-element.390), channel_id=1, source_target_pairs={{0,8},{8,16},{16,24},{24,32},{32,40},{40,48},{48,56},{56,64},{64,7... | collective-permute-start | bytes 98312 | tf_op jit(solution)/shard_map/while/body/eval_jaxpr/ppermute | solution.py:12
  121.9 7.3 %collective-permute-start.1 = (bf16[128,128]{1,0:T(8,128)(2,1)S(1)}, bf16[128,128]{1,0:T(8,128)(2,1)S(1)}, u32[]{:S(2)}, u32[]{:S(2)}) collective-permute-start(bf16[128,128]{1,0:T(8,128)(2,1)S(1)} %get-tuple-element.391), channel_id=1, source_target_pairs={{0,8},{8,16},{16,24},{24,32},{32,40},{40,48},{48,56},{56,64},{64,7... | collective-permute-start | bytes 98312 | tf_op jit(solution)/shard_map/while/body/eval_jaxpr/ppermute | solution.py:12
  129.5 7.3 %collective-permute-start = (bf16[128,128]{1,0:T(8,128)(2,1)S(1)}, bf16[128,128]{1,0:T(8,128)(2,1)S(1)}, u32[]{:S(2)}, u32[]{:S(2)}) collective-permute-start(bf16[128,128]{1,0:T(8,128)(2,1)S(1)} %get-tuple-element.390), channel_id=1, source_target_pairs={{0,8},{8,16},{16,24},{24,32},{32,40},{40,48},{48,56},{56,64},{64,7... | collective-permute-start | bytes 98312 | tf_op jit(solution)/shard_map/while/body/eval_jaxpr/ppermute | solution.py:12
  131.4 7.3 %collective-permute-start.1 = (bf16[128,128]{1,0:T(8,128)(2,1)S(1)}, bf16[128,128]{1,0:T(8,128)(2,1)S(1)}, u32[]{:S(2)}, u32[]{:S(2)}) collective-permute-start(bf16[128,128]{1,0:T(8,128)(2,1)S(1)} %get-tuple-element.391), channel_id=1, source_target_pairs={{0,8},{8,16},{16,24},{24,32},{32,40},{40,48},{48,56},{56,64},{64,7... | collective-permute-start | bytes 98312 | tf_op jit(solution)/shard_map/while/body/eval_jaxpr/ppermute | solution.py:12
  139.0 7.3 %collective-permute-start = (bf16[128,128]{1,0:T(8,128)(2,1)S(1)}, bf16[128,128]{1,0:T(8,128)(2,1)S(1)}, u32[]{:S(2)}, u32[]{:S(2)}) collective-permute-start(bf16[128,128]{1,0:T(8,128)(2,1)S(1)} %get-tuple-element.390), channel_id=1, source_target_pairs={{0,8},{8,16},{16,24},{24,32},{32,40},{40,48},{48,56},{56,64},{64,7... | collective-permute-start | bytes 98312 | tf_op jit(solution)/shard_map/while/body/eval_jaxpr/ppermute | solution.py:12
  140.9 7.3 %collective-permute-start.1 = (bf16[128,128]{1,0:T(8,128)(2,1)S(1)}, bf16[128,128]{1,0:T(8,128)(2,1)S(1)}, u32[]{:S(2)}, u32[]{:S(2)}) collective-permute-start(bf16[128,128]{1,0:T(8,128)(2,1)S(1)} %get-tuple-element.391), channel_id=1, source_target_pairs={{0,8},{8,16},{16,24},{24,32},{32,40},{40,48},{48,56},{56,64},{64,7... | collective-permute-start | bytes 98312 | tf_op jit(solution)/shard_map/while/body/eval_jaxpr/ppermute | solution.py:12
  148.5 7.3 %collective-permute-start = (bf16[128,128]{1,0:T(8,128)(2,1)S(1)}, bf16[128,128]{1,0:T(8,128)(2,1)S(1)}, u32[]{:S(2)}, u32[]{:S(2)}) collective-permute-start(bf16[128,128]{1,0:T(8,128)(2,1)S(1)} %get-tuple-element.390), channel_id=1, source_target_pairs={{0,8},{8,16},{16,24},{24,32},{32,40},{40,48},{48,56},{56,64},{64,7... | collective-permute-start | bytes 98312 | tf_op jit(solution)/shard_map/while/body/eval_jaxpr/ppermute | solution.py:12
  150.4 7.3 %collective-permute-start.1 = (bf16[128,128]{1,0:T(8,128)(2,1)S(1)}, bf16[128,128]{1,0:T(8,128)(2,1)S(1)}, u32[]{:S(2)}, u32[]{:S(2)}) collective-permute-start(bf16[128,128]{1,0:T(8,128)(2,1)S(1)} %get-tuple-element.391), channel_id=1, source_target_pairs={{0,8},{8,16},{16,24},{24,32},{32,40},{40,48},{48,56},{56,64},{64,7... | collective-permute-start | bytes 98312 | tf_op jit(solution)/shard_map/while/body/eval_jaxpr/ppermute | solution.py:12
  158.0 7.3 %collective-permute-start = (bf16[128,128]{1,0:T(8,128)(2,1)S(1)}, bf16[128,128]{1,0:T(8,128)(2,1)S(1)}, u32[]{:S(2)}, u32[]{:S(2)}) collective-permute-start(bf16[128,128]{1,0:T(8,128)(2,1)S(1)} %get-tuple-element.390), channel_id=1, source_target_pairs={{0,8},{8,16},{16,24},{24,32},{32,40},{40,48},{48,56},{56,64},{64,7... | collective-permute-start | bytes 98312 | tf_op jit(solution)/shard_map/while/body/eval_jaxpr/ppermute | solution.py:12
  159.9 7.3 %collective-permute-start.1 = (bf16[128,128]{1,0:T(8,128)(2,1)S(1)}, bf16[128,128]{1,0:T(8,128)(2,1)S(1)}, u32[]{:S(2)}, u32[]{:S(2)}) collective-permute-start(bf16[128,128]{1,0:T(8,128)(2,1)S(1)} %get-tuple-element.391), channel_id=1, source_target_pairs={{0,8},{8,16},{16,24},{24,32},{32,40},{40,48},{48,56},{56,64},{64,7... | collective-permute-start | bytes 98312 | tf_op jit(solution)/shard_map/while/body/eval_jaxpr/ppermute | solution.py:12
  167.5 7.3 %collective-permute-start = (bf16[128,128]{1,0:T(8,128)(2,1)S(1)}, bf16[128,128]{1,0:T(8,128)(2,1)S(1)}, u32[]{:S(2)}, u32[]{:S(2)}) collective-permute-start(bf16[128,128]{1,0:T(8,128)(2,1)S(1)} %get-tuple-element.390), channel_id=1, source_target_pairs={{0,8},{8,16},{16,24},{24,32},{32,40},{40,48},{48,56},{56,64},{64,7... | collective-permute-start | bytes 98312 | tf_op jit(solution)/shard_map/while/body/eval_jaxpr/ppermute | solution.py:12
  169.4 7.3 %collective-permute-start.1 = (bf16[128,128]{1,0:T(8,128)(2,1)S(1)}, bf16[128,128]{1,0:T(8,128)(2,1)S(1)}, u32[]{:S(2)}, u32[]{:S(2)}) collective-permute-start(bf16[128,128]{1,0:T(8,128)(2,1)S(1)} %get-tuple-element.391), channel_id=1, source_target_pairs={{0,8},{8,16},{16,24},{24,32},{32,40},{40,48},{48,56},{56,64},{64,7... | collective-permute-start | bytes 98312 | tf_op jit(solution)/shard_map/while/body/eval_jaxpr/ppermute | solution.py:12
  177.0 7.3 %collective-permute-start = (bf16[128,128]{1,0:T(8,128)(2,1)S(1)}, bf16[128,128]{1,0:T(8,128)(2,1)S(1)}, u32[]{:S(2)}, u32[]{:S(2)}) collective-permute-start(bf16[128,128]{1,0:T(8,128)(2,1)S(1)} %get-tuple-element.390), channel_id=1, source_target_pairs={{0,8},{8,16},{16,24},{24,32},{32,40},{40,48},{48,56},{56,64},{64,7... | collective-permute-start | bytes 98312 | tf_op jit(solution)/shard_map/while/body/eval_jaxpr/ppermute | solution.py:12
  178.9 7.3 %collective-permute-start.1 = (bf16[128,128]{1,0:T(8,128)(2,1)S(1)}, bf16[128,128]{1,0:T(8,128)(2,1)S(1)}, u32[]{:S(2)}, u32[]{:S(2)}) collective-permute-start(bf16[128,128]{1,0:T(8,128)(2,1)S(1)} %get-tuple-element.391), channel_id=1, source_target_pairs={{0,8},{8,16},{16,24},{24,32},{32,40},{40,48},{48,56},{56,64},{64,7... | collective-permute-start | bytes 98312 | tf_op jit(solution)/shard_map/while/body/eval_jaxpr/ppermute | solution.py:12
  186.5 7.3 %collective-permute-start = (bf16[128,128]{1,0:T(8,128)(2,1)S(1)}, bf16[128,128]{1,0:T(8,128)(2,1)S(1)}, u32[]{:S(2)}, u32[]{:S(2)}) collective-permute-start(bf16[128,128]{1,0:T(8,128)(2,1)S(1)} %get-tuple-element.390), channel_id=1, source_target_pairs={{0,8},{8,16},{16,24},{24,32},{32,40},{40,48},{48,56},{56,64},{64,7... | collective-permute-start | bytes 98312 | tf_op jit(solution)/shard_map/while/body/eval_jaxpr/ppermute | solution.py:12
  188.4 7.3 %collective-permute-start.1 = (bf16[128,128]{1,0:T(8,128)(2,1)S(1)}, bf16[128,128]{1,0:T(8,128)(2,1)S(1)}, u32[]{:S(2)}, u32[]{:S(2)}) collective-permute-start(bf16[128,128]{1,0:T(8,128)(2,1)S(1)} %get-tuple-element.391), channel_id=1, source_target_pairs={{0,8},{8,16},{16,24},{24,32},{32,40},{40,48},{48,56},{56,64},{64,7... | collective-permute-start | bytes 98312 | tf_op jit(solution)/shard_map/while/body/eval_jaxpr/ppermute | solution.py:12
Sparse Core Ops, SparseCore 0:
  51.3 61.5 all-gather.1
where the time goes:
time: 205 us; the launch traced here: 204 us
  waiting for transfers between devices  100 us (49%)
  starting transfers between devices  52.4 us (26%)
  blocking collectives  17 us (8%)
  between operations  13.7 us (7%)
  matrix products  9.32 us (5%)
  other arithmetic  5.63 us (3%)
  local copies, waits for them, and re-layouts  4.99 us (2%)
    all_gather x1, waiting for transfers between devices, body(): features = lax.all_gather(placed, 'kvh', axis=1, tiled=True)  43 us
    ppermute x16, waiting for transfers between devices, passed_along(): return lax.ppermute(block, axis, route)  39.5 us
    ppermute x16, starting transfers between devices, passed_along(): return lax.ppermute(block, axis, route)  32.5 us
    pmin x1, blocking collectives, body(): starts = lax.pmin(earliest, 'ctx')  17 us
    all_to_all x1, starting transfers between devices, body(): lax.all_to_all(labels, 'ctx', split_axis=0, concat_axis=0, tiled=True)  14.4 us
    all_to_all x1, waiting for transfers between devices, body(): lax.all_to_all(parcel, 'ctx', split_axis=0, concat_axis=0, tiled=True)  10.6 us
    all_to_all x1, waiting for transfers between devices, body(): lax.all_to_all(labels, 'ctx', split_axis=0, concat_axis=0, tiled=True)  6.91 us
    all_to_all x1, starting transfers between devices, body(): lax.all_to_all(parcel, 'ctx', split_axis=0, concat_axis=0, tiled=True)  5.53 us
  transfers between devices with their start and end apart: 19, of which 19 were waited for; matrix products, arithmetic and copies ran while one was open for 3% of the time, Pallas kernels for 0%

commit v1 on v0

v1 whole, which is shorter than its diff:
```python
import functools

import jax
import jax.numpy as jnp
from jax import lax
from jax.experimental import pallas as pl
from jax.experimental.pallas import tpu as pltpu
from jax.sharding import PartitionSpec as P

SPAN = 8
SLOTS = 4
CHUNK = 2 * SLOTS
F32, BF16 = jnp.float32, jnp.bfloat16


def along_kvh(block, shift):
    n = lax.axis_size("kvh")
    return lax.ppermute(block, "kvh", [(i, (i + 2 * shift) % n) for i in range(n)])


def along_ctx(block, distance):
    n = lax.axis_size("ctx")
    return lax.ppermute(block, "ctx", [(i, i + distance) for i in range(n - distance)])


def rotation(positions, head_dim):
    half_dim = head_dim // 2
    exponent = jnp.arange(half_dim, dtype=F32) * (2.0 / head_dim)
    frequency = jnp.power(jnp.float32(1000000.0), -exponent)
    angles = positions.astype(F32)[:, None] * frequency[None, :]
    cosine, sine = jnp.cos(angles), jnp.sin(angles)
    return jnp.concatenate([cosine, cosine], 1), jnp.concatenate([-sine, sine], 1)


def project_kernel(shifts, me_ref, *refs):
    pieces, refs = refs[: len(shifts)], refs[len(shifts) :]
    wq, wk, wv, cosine, sine, q_gain, k_gain, slot, within, docs, out = refs
    rows, width = pieces[0].shape[0] // 2, pieces[0].shape[1]
    groups = wq.shape[0] // width
    me = me_ref[0]
    totals = [jnp.zeros((rows, w.shape[1]), F32) for w in (wq, wk, wv)]
    for piece, shift in zip(pieces, shifts):
        source = lax.rem(me + (groups - 2 * shift), groups)
        for half in range(2):
            owner = source if half == 0 else source + 1 - 2 * lax.rem(source, 2)
            span = pl.ds(pl.multiple_of(owner * width, width), width)
            block = piece[half * rows : (half + 1) * rows, :]
            totals = [
                total + jnp.dot(block, w[span, :], preferred_element_type=F32)
                for total, w in zip(totals, (wq, wk, wv))
            ]
    raw_q, raw_k, raw_v = totals
    head_dim = raw_k.shape[1]

    def turned(raw, gain):
        unit = raw * lax.rsqrt(jnp.mean(raw * raw, -1, keepdims=True) + 1e-06) * gain[...]
        return unit * cosine[...] + pltpu.roll(unit, head_dim // 2, 1) * sine[...]

    heads = [
        turned(raw_q[:, h : h + head_dim], q_gain) * head_dim ** (-0.5)
        for h in range(0, raw_q.shape[1], head_dim)
    ]
    top = jnp.concatenate([h.astype(BF16) for h in heads] + [within[...]], 1)
    low = jnp.concatenate(
        [turned(raw_k, k_gain).astype(BF16), raw_v.astype(BF16), within[...]], 1
    )
    wanted = lax.broadcasted_iota(jnp.int32, (out.shape[0], 2 * rows), 0)
    picked = jnp.where(wanted == slot[...], 1.0, 0.0).astype(BF16)
    parcel = jnp.dot(picked, jnp.concatenate([top, low], 0), preferred_element_type=F32)
    body = out.shape[1] - docs.shape[1]
    out[:, :body] = parcel[:, :body].astype(BF16)
    out[:, body:] = (parcel[:, body:] + docs[...]).astype(BF16)


def land_kernel(me_ref, arrived, queries, keyvalues, key_docs, doc_rows):
    me = me_ref[0]
    rows = keyvalues.shape[0]
    body = arrived.shape[1] - rows
    coded = arrived[:, body:].astype(F32).astype(jnp.int32)
    doc_rows[...] = lax.shift_right_logical(coded, 1)
    hot = lax.bitwise_and(coded, 1)
    kind = lax.rem(lax.broadcasted_iota(jnp.int32, hot.shape, 0), CHUNK)
    first = jnp.where(kind < SLOTS, hot, 0).astype(F32).astype(BF16)
    second = jnp.where(kind >= SLOTS, hot, 0).astype(F32).astype(BF16)
    landing = jnp.concatenate([first, second], 1)
    placed = lax.dot_general(
        landing, arrived[:, :body], (((0,), (0,)), ((), ())), preferred_element_type=F32
    ).astype(BF16)
    head_dim = body // 2
    for h in range(2):
        queries[h * rows : (h + 1) * rows, :] = placed[:rows, h * head_dim : (h + 1) * head_dim]
    keyvalues[...] = placed[rows:, :]
    for back in range(SPAN + 1):
        owner = jnp.maximum(me - back, 0)
        row = doc_rows[pl.ds(pl.multiple_of(owner * CHUNK, CHUNK), CHUNK), :][:1, :]
        key_docs[back : back + 1, :] = jnp.where(me >= back, row, -1)


def attend_kernel(backs, queries, query_docs, key_docs, *refs):
    pieces, out = refs[:-1], refs[-1]
    rows = out.shape[0]
    head_dim = queries.shape[1]
    q = queries[...]
    q_doc = query_docs[...]
    numer = jnp.zeros((q.shape[0], head_dim), F32)
    denom = jnp.zeros((q.shape[0], 1), F32)
    for piece, held in zip(pieces, backs):
        scores = lax.dot_general(
            q, piece[:, :head_dim], (((1,), (1,)), ((), ())), preferred_element_type=F32
        )
        docs = jnp.concatenate([key_docs[back : back + 1, :] for back in held], 1)
        visible = q_doc == docs
        if held == (0,):
            t = lax.rem(lax.broadcasted_iota(jnp.int32, scores.shape, 0), rows)
            u = lax.broadcasted_iota(jnp.int32, scores.shape, 1)
            visible = visible & (u <= t)
        weights = jnp.where(visible, jnp.exp(scores), 0.0)
        denom = denom + jnp.sum(weights, 1, keepdims=True)
        numer = numer + jnp.dot(
            weights.astype(BF16), piece[:, head_dim:], preferred_element_type=F32
        )
    result = (numer / denom).astype(BF16)
    for h in range(out.shape[1] // head_dim):
        out[:, h * head_dim : (h + 1) * head_dim] = result[h * rows : (h + 1) * rows, :]


VMEM = pl.BlockSpec(memory_space=pltpu.VMEM)
SMEM = pl.BlockSpec(memory_space=pltpu.SMEM)


def call(kernel, out_shape, operands, scratch=(), flops=0, size=0, limit=24):
    return pl.pallas_call(
        kernel,
        out_shape=out_shape,
        in_specs=[SMEM if x.shape == (1,) else VMEM for x in operands],
        out_specs=jax.tree.map(lambda _: VMEM, out_shape),
        scratch_shapes=scratch,
        cost_estimate=pl.CostEstimate(flops=flops, bytes_accessed=size, transcendentals=0),
        compiler_params=pltpu.CompilerParams(vmem_limit_bytes=limit * 2**20),
    )(*operands)


def body(hidden, destination, doc_ids, w_query, w_key, w_value, q_gain, k_gain):
    blocks = lax.axis_size("ctx")
    ctx_index = lax.axis_index("ctx")
    kvh_index = lax.axis_index("kvh")
    rows, width = hidden.shape
    head_dim = q_gain.shape[0]

    n = lax.axis_size("kvh")
    across = lax.ppermute(hidden, "kvh", [(i, i ^ 1) for i in range(n)])
    own = jnp.concatenate([hidden, across], 0)
    shifts = (0, 1, 3, 2)
    pieces = [own] + [along_kvh(own, s) for s in shifts[1:]]

    target, inside = destination // rows, destination % rows
    index = jnp.arange(rows, dtype=jnp.int32)
    earlier = (target[:, None] == target[None, :]) & (index[:, None] < index[None, :])
    slot = target * CHUNK + jnp.sum(earlier.astype(jnp.int32), 0)
    slot = jnp.concatenate([slot, slot + SLOTS]).reshape(1, 2 * rows)
    within = (inside[:, None] == index[None, :]).astype(BF16)
    cosine, sine = rotation(destination, head_dim)
    docs = (2 * doc_ids).astype(F32).reshape(1, rows)
    query_docs = jnp.tile(doc_ids, w_query.shape[1] // head_dim).reshape(-1, 1)

    me_kvh = kvh_index.astype(jnp.int32).reshape(1)
    me_ctx = ctx_index.astype(jnp.int32).reshape(1)
    parcel = call(
        functools.partial(project_kernel, shifts),
        jax.ShapeDtypeStruct((blocks * CHUNK, 2 * head_dim + rows), BF16),
        [me_kvh, *pieces, w_query, w_key, w_value, cosine, sine]
        + [q_gain.reshape(1, -1), k_gain.reshape(1, -1), slot, within, docs],
    )
    arrived = lax.all_to_all(
        parcel.reshape(blocks, CHUNK, -1), "ctx", split_axis=0, concat_axis=0, tiled=True
    ).reshape(parcel.shape)
    queries, near, key_docs = call(
        land_kernel,
        (
            jax.ShapeDtypeStruct((2 * rows, head_dim), BF16),
            jax.ShapeDtypeStruct((rows, 2 * head_dim), BF16),
            jax.ShapeDtypeStruct((16, rows), jnp.int32),
        ),
        [me_ctx, arrived],
        scratch=[pltpu.VMEM((blocks * CHUNK, rows), jnp.int32)],
    )

    back8 = along_ctx(near, 8)
    back2 = along_ctx(near, 2)
    back02 = jnp.concatenate([near, back2], 0)
    back46 = along_ctx(back02, 4)
    held = jnp.concatenate([back02, back46, back8], 0)
    odd = lax.rem(ctx_index, 2) == 1
    swapped = lax.ppermute(
        jnp.where(odd, held[rows:], held[: 4 * rows]),
        "ctx",
        [(i, i ^ 1) for i in range(blocks)],
    )
    return call(
        functools.partial(attend_kernel, ((0,), (2,), (4, 6), (8,), (1, 3, 5, 7))),
        jax.ShapeDtypeStruct((rows, w_query.shape[1]), BF16),
        [queries, query_docs, key_docs, near, back2, back46, back8, swapped],
    )


def solution(mesh):
    placed = (
        P("ctx", "kvh"),
        P("ctx"),
        P("ctx"),
        P(None, "kvh"),
        P(None, "kvh"),
        P(None, "kvh"),
        P(),
        P(),
    )
    return jax.shard_map(
        body, mesh=mesh, in_specs=placed, out_specs=P("ctx", "kvh"), check_vma=False
    )
```

time: 205 us -> 96.8 us (0.47)
  the two profiles are of different devices: /device:TPU:8 before, /device:TPU:11 now
where the time goes in v1:
time: 96.8 us; the launch traced here: 96.3 us
  starting transfers between devices  48.8 us (50%)
  waiting for transfers between devices  35 us (36%)
  local copies, waits for them, and re-layouts  6.41 us (7%)
  Pallas kernels  3.81 us (4%)
  other arithmetic  2.08 us (2%)
    all_to_all x1, starting transfers between devices, body(): lax.all_to_all(parcel.reshape(blocks, CHUNK, -1), 'ctx', split_axis=0, co...  22.1 us
    all_to_all x1, waiting for transfers between devices, body(): lax.all_to_all(parcel.reshape(blocks, CHUNK, -1), 'ctx', split_axis=0, co...  14.6 us
    ppermute x3, waiting for transfers between devices, along_ctx(): lax.ppermute(block, 'ctx', [(i, i + distance) for i in range(n - distance)])  12.8 us
    ppermute x3, starting transfers between devices, along_kvh(): lax.ppermute(block, 'kvh', [(i, (i + 2 * shift) % n) for i in range(n)])  9.04 us
    ppermute x3, starting transfers between devices, along_ctx(): lax.ppermute(block, 'ctx', [(i, i + distance) for i in range(n - distance)])  7.19 us
    ppermute x1, starting transfers between devices, body(): across = lax.ppermute(hidden, 'kvh', [(i, i ^ 1) for i in range(n)])  6.54 us
    unnamed x13, local copies, waits for them, and re-layouts  6.27 us
    ppermute x3, waiting for transfers between devices, along_kvh(): lax.ppermute(block, 'kvh', [(i, (i + 2 * shift) % n) for i in range(n)])  5.58 us
  transfers between devices with their start and end apart: 9, of which 7 were waited for; matrix products, arithmetic and copies ran while one was open for 3% of the time, Pallas kernels for 0%

profile of v1, /device:TPU:11, one launch (start us, length us, event | category | flops | bytes accessed | tf_op | source)
XLA Modules:
  0.0 96.3 jit_solution(17748425767749738131)
XLA Ops:
  0.0 6.5 %collective-permute-start = (bf16[128,512]{1,0:T(8,128)(2,1)}, bf16[128,512]{1,0:T(8,128)(2,1)S(1)}, u32[]{:S(2)}, u32[]{:S(2)}) collective-permute-start(bf16[128,512]{1,0:T(8,128)(2,1)} %param.8), channel_id=1, source_target_pairs={{0,1},{1,0},{2,3},{3,2},{4,5},{5,4},{6,7},{7,6},{8,9},{9,8},{10,11... | collective-permute-start | bytes 393224 | tf_op jit(solution)/shard_map/ppermute | solution.py:151
  6.6 0.7 and_select_fusion
  7.3 0.1 convert_reduce_fusion
  7.4 0.7 convert_bitcast_fusion.refs_13_
  8.1 0.3 fusion.2
  8.4 0.9 constant_dynamic-update-slice_fusion.1
  9.3 0.1 pad_maximum_fusion.1
  9.4 0.9 collective-permute-done
  10.4 3.1 %collective-permute-start.1 = (bf16[256,512]{1,0:T(8,128)(2,1)S(1)}, bf16[256,512]{1,0:T(8,128)(2,1)S(1)}, u32[]{:S(2)}, u32[]{:S(2)}) collective-permute-start(bf16[256,512]{1,0:T(8,128)(2,1)S(1)} %constant_dynamic-update-slice_fusion.refs_0_), channel_id=1, source_target_pairs={{0,2},{1,3},{2,4},{3,5},{4,6},{5,7},{6,0},{7,1},{8,10},{9,11},{10,... | collective-permute-start | bytes 786440 | tf_op jit(solution)/shard_map/ppermute | solution.py:18
  13.5 2.2 %collective-permute-start.2 = (bf16[256,512]{1,0:T(8,128)(2,1)S(1)}, bf16[256,512]{1,0:T(8,128)(2,1)S(1)}, u32[]{:S(2)}, u32[]{:S(2)}) collective-permute-start(bf16[256,512]{1,0:T(8,128)(2,1)S(1)} %constant_dynamic-update-slice_fusion.refs_0_), channel_id=1, source_target_pairs={{0,6},{1,7},{2,0},{3,1},{4,2},{5,3},{6,4},{7,5},{8,14},{9,15},{10,... | collective-permute-start | bytes 786440 | tf_op jit(solution)/shard_map/ppermute | solution.py:18
  15.7 3.8 %collective-permute-start.3 = (bf16[256,512]{1,0:T(8,128)(2,1)S(1)}, bf16[256,512]{1,0:T(8,128)(2,1)S(1)}, u32[]{:S(2)}, u32[]{:S(2)}) collective-permute-start(bf16[256,512]{1,0:T(8,128)(2,1)S(1)} %constant_dynamic-update-slice_fusion.refs_0_), channel_id=1, source_target_pairs={{0,4},{1,5},{2,6},{3,7},{4,0},{5,1},{6,2},{7,3},{8,12},{9,13},{10,... | collective-permute-start | bytes 786440 | tf_op jit(solution)/shard_map/ppermute | solution.py:18
  19.5 0.1 fusion.1.refs_12_
  19.5 0.0 collective-permute-done.1.refs_1_
  19.6 1.4 %collective-permute-done.2.refs_2_ = bf16[256,512]{1,0:T(8,128)(2,1)S(1)} collective-permute-done((bf16[256,512]{1,0:T(8,128)(2,1)S(1)}, bf16[256,512]{1,0:T(8,128)(2,1)S(1)}, u32[]{:S(2)}, u32[]{:S(2)}) %collective-permute-start.2) | collective-permute-done | bytes 262176 | tf_op jit(solution)/shard_map/ppermute | solution.py:18
  20.9 4.2 %collective-permute-done.3.refs_3_ = bf16[256,512]{1,0:T(8,128)(2,1)S(1)} collective-permute-done((bf16[256,512]{1,0:T(8,128)(2,1)S(1)}, bf16[256,512]{1,0:T(8,128)(2,1)S(1)}, u32[]{:S(2)}, u32[]{:S(2)}) %collective-permute-start.3) | collective-permute-done | bytes 262176 | tf_op jit(solution)/shard_map/ppermute | solution.py:18
  25.1 0.0 copy-start
  25.1 1.6 %copy-done = bf16[4096,256]{1,0:T(8,128)(2,1)S(1)} copy-done((bf16[4096,256]{1,0:T(8,128)(2,1)S(1)}, bf16[4096,256]{1,0:T(8,128)(2,1)}, u32[]{:S(2)}) %copy-start) | copy-done | bytes 2097176
  26.7 0.0 copy-start.1
  26.7 1.2 %copy-done.1 = bf16[4096,128]{1,0:T(8,128)(2,1)S(1)} copy-done((bf16[4096,128]{1,0:T(8,128)(2,1)S(1)}, bf16[4096,128]{1,0:T(8,128)(2,1)}, u32[]{:S(2)}) %copy-start.1) | copy-done | bytes 1048600
  28.0 0.0 copy-start.2
  28.0 1.2 %copy-done.2 = bf16[4096,128]{1,0:T(8,128)(2,1)S(1)} copy-done((bf16[4096,128]{1,0:T(8,128)(2,1)S(1)}, bf16[4096,128]{1,0:T(8,128)(2,1)}, u32[]{:S(2)}) %copy-start.2) | copy-done | bytes 1048600
  29.2 0.0 copy-start.3
  29.2 0.7 copy-done.3
  29.8 0.0 copy-start.4
  29.8 0.7 copy-done.4
  30.5 0.0 copy-start.5
  30.5 2.2 %shard_map.82 = bf16[512,384]{1,0:T(8,128)(2,1)} custom-call(s32[1]{0:T(128)} %bitcast.1.me_ref, bf16[256,512]{1,0:T(8,128)(2,1)S(1)} %constant_dynamic-update-slice_fusion.refs_0_, bf16[256,512]{1,0:T(8,128)(2,1)S(1)} %collective-permute-done.1.refs_1_, bf16[256,512]{1,0:T(8,128)(2,1)S(1)} %collective-permute-done.2.refs_2_, ...), custom_call_target="tpu_custom_call" | custom-call | tf_op jit(solution)/shard_map/pallas_call | solution.py:132
  32.7 22.1 %all-to-all-start = ((bf16[64,8,384]{2,1,0:T(8,128)(2,1)}), bf16[64,8,384]{2,1,0:T(8,128)(2,1)S(1)}, u32[]{:S(2)}, u32[]{:S(2)}) async-start(bf16[64,8,384]{2,1,0:T(8,128)(2,1)} %bitcast.6), calls=%async_computation | async-start | bytes 786432 | tf_op jit(solution)/shard_map/all_to_all | solution.py:174
  54.7 14.6 %all-to-all-done = bf16[64,8,384]{2,1,0:T(8,128)(2,1)S(1)} async-done(((bf16[64,8,384]{2,1,0:T(8,128)(2,1)}), bf16[64,8,384]{2,1,0:T(8,128)(2,1)S(1)}, u32[]{:S(2)}, u32[]{:S(2)}) %all-to-all-start) | async-done | bytes 393248 | tf_op jit(solution)/shard_map/all_to_all | solution.py:174
  69.4 0.3 shard_map.83
  69.7 2.8 %collective-permute-start.4 = (bf16[128,256]{1,0:T(8,128)(2,1)S(1)}, bf16[128,256]{1,0:T(8,128)(2,1)S(1)}, u32[]{:S(2)}, u32[]{:S(2)}) collective-permute-start(bf16[128,256]{1,0:T(8,128)(2,1)S(1)} %get-tuple-element.10.refs_0_), channel_id=1, source_target_pairs={{0,16},{8,24},{16,32},{24,40},{32,48},{40,56},{48,64},{56,72},{64,... | collective-permute-start | bytes 196616 | tf_op jit(solution)/shard_map/ppermute | solution.py:23
  72.5 4.7 %collective-permute-done.4.refs_1_ = bf16[128,256]{1,0:T(8,128)(2,1)S(1)} collective-permute-done((bf16[128,256]{1,0:T(8,128)(2,1)S(1)}, bf16[128,256]{1,0:T(8,128)(2,1)S(1)}, u32[]{:S(2)}, u32[]{:S(2)}) %collective-permute-start.4) | collective-permute-done | bytes 65568 | tf_op jit(solution)/shard_map/ppermute | solution.py:23
  77.3 1.9 %collective-permute-start.5 = (bf16[256,256]{1,0:T(8,128)(2,1)S(1)}, bf16[256,256]{1,0:T(8,128)(2,1)S(1)}, u32[]{:S(2)}, u32[]{:S(2)}) collective-permute-start(bf16[256,256]{1,0:T(8,128)(2,1)S(1)} %pad_maximum_fusion), channel_id=1, source_target_pairs={{0,32},{8,40},{16,48},{24,56},{32,64},{40,72},{48,80},{56,88},{64,... | collective-permute-start | bytes 393224 | tf_op jit(solution)/shard_map/ppermute | solution.py:23
  79.2 2.5 %collective-permute-start.6 = (bf16[128,256]{1,0:T(8,128)(2,1)S(1)}, bf16[128,256]{1,0:T(8,128)(2,1)S(1)}, u32[]{:S(2)}, u32[]{:S(2)}) collective-permute-start(bf16[128,256]{1,0:T(8,128)(2,1)S(1)} %get-tuple-element.10.refs_0_), channel_id=1, source_target_pairs={{0,64},{8,72},{16,80},{24,88},{32,96},{40,104},{48,112},{56,120},{... | collective-permute-start | bytes 196616 | tf_op jit(solution)/shard_map/ppermute | solution.py:23
  81.6 8.1 %collective-permute-done.6.refs_3_ = bf16[128,256]{1,0:T(8,128)(2,1)S(1)} collective-permute-done((bf16[128,256]{1,0:T(8,128)(2,1)S(1)}, bf16[128,256]{1,0:T(8,128)(2,1)S(1)}, u32[]{:S(2)}, u32[]{:S(2)}) %collective-permute-start.6) | collective-permute-done | bytes 65568 | tf_op jit(solution)/shard_map/ppermute | solution.py:23
  89.8 0.0 collective-permute-done.5.refs_2_
  89.8 0.1 maximum_select_fusion
  89.8 4.0 %collective-permute-start.7 = (bf16[512,256]{1,0:T(8,128)(2,1)S(1)}, bf16[512,256]{1,0:T(8,128)(2,1)S(1)}, u32[]{:S(2)}, u32[]{:S(2)}) collective-permute-start(bf16[512,256]{1,0:T(8,128)(2,1)S(1)} %maximum_select_fusion), channel_id=1, source_target_pairs={{0,8},{8,0},{16,24},{24,16},{32,40},{40,32},{48,56},{56,48},{64,72... | collective-permute-start | bytes 786440 | tf_op jit(solution)/shard_map/ppermute | solution.py:194
  93.8 0.0 copy-done.5
  93.8 0.1 copy.10.query_docs
  94.0 1.0 %collective-permute-done.7.refs_4_ = bf16[512,256]{1,0:T(8,128)(2,1)S(1)} collective-permute-done((bf16[512,256]{1,0:T(8,128)(2,1)S(1)}, bf16[512,256]{1,0:T(8,128)(2,1)S(1)}, u32[]{:S(2)}, u32[]{:S(2)}) %collective-permute-start.7) | collective-permute-done | bytes 262176 | tf_op jit(solution)/shard_map/ppermute | solution.py:194
  95.0 1.3 %shard_map.84 = bf16[128,256]{1,0:T(8,128)(2,1)} custom-call(bf16[256,128]{1,0:T(8,128)(2,1)S(1)} %get-tuple-element.8.queries, s32[256,1]{1,0:T(8,128)S(1)} %copy.10.query_docs, s32[16,128]{1,0:T(8,128)S(1)} %get-tuple-element.9.key_docs, bf16[128,256]{1,0:T(8,128)(2,1)S(1)} %get-tuple-element.10.refs_0_, ...), custom_call_target="tpu_custom_call" | custom-call | tf_op jit(solution)/shard_map/pallas_call | solution.py:132
  (6 shorter events, 0.0 us)
Async XLA Ops:
  0.0 10.4 %collective-permute-start = (bf16[128,512]{1,0:T(8,128)(2,1)}, bf16[128,512]{1,0:T(8,128)(2,1)S(1)}, u32[]{:S(2)}, u32[]{:S(2)}) collective-permute-start(bf16[128,512]{1,0:T(8,128)(2,1)} %param.8), channel_id=1, source_target_pairs={{0,1},{1,0},{2,3},{3,2},{4,5},{5,4},{6,7},{7,6},{8,9},{9,8},{10,11... | collective-permute-start | bytes 393224 | tf_op jit(solution)/shard_map/ppermute | solution.py:151
  10.4 9.2 %collective-permute-start.1 = (bf16[256,512]{1,0:T(8,128)(2,1)S(1)}, bf16[256,512]{1,0:T(8,128)(2,1)S(1)}, u32[]{:S(2)}, u32[]{:S(2)}) collective-permute-start(bf16[256,512]{1,0:T(8,128)(2,1)S(1)} %constant_dynamic-update-slice_fusion.refs_0_), channel_id=1, source_target_pairs={{0,2},{1,3},{2,4},{3,5},{4,6},{5,7},{6,0},{7,1},{8,10},{9,11},{10,... | collective-permute-start | bytes 786440 | tf_op jit(solution)/shard_map/ppermute | solution.py:18
  13.5 7.4 %collective-permute-start.2 = (bf16[256,512]{1,0:T(8,128)(2,1)S(1)}, bf16[256,512]{1,0:T(8,128)(2,1)S(1)}, u32[]{:S(2)}, u32[]{:S(2)}) collective-permute-start(bf16[256,512]{1,0:T(8,128)(2,1)S(1)} %constant_dynamic-update-slice_fusion.refs_0_), channel_id=1, source_target_pairs={{0,6},{1,7},{2,0},{3,1},{4,2},{5,3},{6,4},{7,5},{8,14},{9,15},{10,... | collective-permute-start | bytes 786440 | tf_op jit(solution)/shard_map/ppermute | solution.py:18
  15.7 9.5 %collective-permute-start.3 = (bf16[256,512]{1,0:T(8,128)(2,1)S(1)}, bf16[256,512]{1,0:T(8,128)(2,1)S(1)}, u32[]{:S(2)}, u32[]{:S(2)}) collective-permute-start(bf16[256,512]{1,0:T(8,128)(2,1)S(1)} %constant_dynamic-update-slice_fusion.refs_0_), channel_id=1, source_target_pairs={{0,4},{1,5},{2,6},{3,7},{4,0},{5,1},{6,2},{7,3},{8,12},{9,13},{10,... | collective-permute-start | bytes 786440 | tf_op jit(solution)/shard_map/ppermute | solution.py:18
  25.1 1.6 %copy-start = (bf16[4096,256]{1,0:T(8,128)(2,1)S(1)}, bf16[4096,256]{1,0:T(8,128)(2,1)}, u32[]{:S(2)}) copy-start(bf16[4096,256]{1,0:T(8,128)(2,1)} %refs_4_.1) | copy-start | bytes 6291460
  26.7 1.2 %copy-start.1 = (bf16[4096,128]{1,0:T(8,128)(2,1)S(1)}, bf16[4096,128]{1,0:T(8,128)(2,1)}, u32[]{:S(2)}) copy-start(bf16[4096,128]{1,0:T(8,128)(2,1)} %refs_5_.1) | copy-start | bytes 3145732
  28.0 1.2 %copy-start.2 = (bf16[4096,128]{1,0:T(8,128)(2,1)S(1)}, bf16[4096,128]{1,0:T(8,128)(2,1)}, u32[]{:S(2)}) copy-start(bf16[4096,128]{1,0:T(8,128)(2,1)} %refs_6_.1) | copy-start | bytes 3145732
  29.2 0.7 copy-start.3
  29.8 0.7 copy-start.4
  30.5 63.3 %copy-start.5 = (s32[128]{0:T(128)S(1)}, s32[128]{0:T(128)}, u32[]{:S(2)}) copy-start(s32[128]{0:T(128)} %param.10) | copy-start | bytes 1540
  32.7 36.7 %all-to-all-start = ((bf16[64,8,384]{2,1,0:T(8,128)(2,1)}), bf16[64,8,384]{2,1,0:T(8,128)(2,1)S(1)}, u32[]{:S(2)}, u32[]{:S(2)}) async-start(bf16[64,8,384]{2,1,0:T(8,128)(2,1)} %bitcast.6), calls=%async_computation | async-start | bytes 786432 | tf_op jit(solution)/shard_map/all_to_all | solution.py:174
  69.7 7.5 %collective-permute-start.4 = (bf16[128,256]{1,0:T(8,128)(2,1)S(1)}, bf16[128,256]{1,0:T(8,128)(2,1)S(1)}, u32[]{:S(2)}, u32[]{:S(2)}) collective-permute-start(bf16[128,256]{1,0:T(8,128)(2,1)S(1)} %get-tuple-element.10.refs_0_), channel_id=1, source_target_pairs={{0,16},{8,24},{16,32},{24,40},{32,48},{40,56},{48,64},{56,72},{64,... | collective-permute-start | bytes 196616 | tf_op jit(solution)/shard_map/ppermute | solution.py:23
  77.3 12.5 %collective-permute-start.5 = (bf16[256,256]{1,0:T(8,128)(2,1)S(1)}, bf16[256,256]{1,0:T(8,128)(2,1)S(1)}, u32[]{:S(2)}, u32[]{:S(2)}) collective-permute-start(bf16[256,256]{1,0:T(8,128)(2,1)S(1)} %pad_maximum_fusion), channel_id=1, source_target_pairs={{0,32},{8,40},{16,48},{24,56},{32,64},{40,72},{48,80},{56,88},{64,... | collective-permute-start | bytes 393224 | tf_op jit(solution)/shard_map/ppermute | solution.py:23
  79.2 10.6 %collective-permute-start.6 = (bf16[128,256]{1,0:T(8,128)(2,1)S(1)}, bf16[128,256]{1,0:T(8,128)(2,1)S(1)}, u32[]{:S(2)}, u32[]{:S(2)}) collective-permute-start(bf16[128,256]{1,0:T(8,128)(2,1)S(1)} %get-tuple-element.10.refs_0_), channel_id=1, source_target_pairs={{0,64},{8,72},{16,80},{24,88},{32,96},{40,104},{48,112},{56,120},{... | collective-permute-start | bytes 196616 | tf_op jit(solution)/shard_map/ppermute | solution.py:23
  89.8 5.1 %collective-permute-start.7 = (bf16[512,256]{1,0:T(8,128)(2,1)S(1)}, bf16[512,256]{1,0:T(8,128)(2,1)S(1)}, u32[]{:S(2)}, u32[]{:S(2)}) collective-permute-start(bf16[512,256]{1,0:T(8,128)(2,1)S(1)} %maximum_select_fusion), channel_id=1, source_target_pairs={{0,8},{8,0},{16,24},{24,16},{32,40},{40,32},{48,56},{56,48},{64,72... | collective-permute-start | bytes 786440 | tf_op jit(solution)/shard_map/ppermute | solution.py:194

commit v2 on v0

v2 whole, which is shorter than its diff:
```python
import functools

import jax
import jax.numpy as jnp
from jax import lax
from jax.experimental import pallas as pl
from jax.experimental.pallas import tpu as pltpu
from jax.sharding import PartitionSpec as P

SPAN = 8
SLOTS = 4
PARTS = 1 + SPAN // 2 + 1
CHUNK = PARTS * SLOTS
PAIRS = PARTS // 2
LABEL = 256
F32, BF16, I32 = jnp.float32, jnp.bfloat16, jnp.int32


def along_kvh(block, shift):
    n = lax.axis_size("kvh")
    return lax.ppermute(block, "kvh", [(i, (i + 2 * shift) % n) for i in range(n)])


def iota(shape, dim):
    return lax.broadcasted_iota(I32, shape, dim)


def hot(mask):
    return jnp.where(mask, 1.0, 0.0).astype(BF16)


def column(row):
    square = (row.shape[1], row.shape[1])
    return jnp.sum(jnp.where(iota(square, 0) == iota(square, 1), row, 0), 1, keepdims=True)


def fetch(pairs, sems):
    copies = [pltpu.make_async_copy(a, b, sems.at[i]) for i, (a, b) in enumerate(pairs)]
    for copy in copies:
        copy.start()
    for copy in copies:
        copy.wait()


def notes_kernel(destination, doc_ids, hidden, notes, slot, query_docs, own, place_ref, docs_ref, sems):
    rows = destination.shape[1]
    fetch([(destination, place_ref), (doc_ids, docs_ref)], sems)
    place, docs = place_ref[...], docs_ref[...]
    target, inside = lax.div(place, rows), lax.rem(place, rows)
    square = (rows, rows)
    earlier = (column(target) == target) & (iota(square, 0) < iota(square, 1))
    order = jnp.sum(jnp.where(earlier, 1, 0), 0, keepdims=True)
    slot[...] = target * SLOTS + order
    blocks = notes.shape[0]
    order_col, label_col = column(order), column(inside) + 1
    label = jnp.zeros((blocks, rows), F32)
    for k in range(PARTS - 1):
        sent = hot(iota((blocks, rows), 0) == target + 2 * k)
        at = jnp.where(order_col + k * SLOTS == iota(square, 1), label_col, 0)
        label += jnp.dot(sent, at.astype(F32).astype(BF16), preferred_element_type=F32)
    notes[...] = (label.astype(I32) + LABEL * docs).reshape(notes.shape)
    docs_col = column(docs)
    for h in range(query_docs.shape[0] // rows):
        query_docs[h * rows : (h + 1) * rows, :] = docs_col
    own[...] = hidden[...]


def tables_kernel(
    slot, q_gain, k_gain, cosine, sine, picked, q_cos, q_sin, k_cos, k_sin, q_ref, k_ref, sems
):
    fetch([(q_gain, q_ref), (k_gain, k_ref)], sems)
    rows = slot.shape[1]
    shape = (picked.shape[0] // CHUNK, CHUNK, rows)
    block, line = iota(shape, 0), iota(shape, 1)
    wanted = block * SLOTS + line
    for p in range(PARTS):
        mine = (line >= p * SLOTS) & (line < (p + 1) * SLOTS)
        wanted = jnp.where(mine, wanted - p * SLOTS - 2 * max(p - 1, 0) * SLOTS, wanted)
    found = wanted == slot[...].reshape(1, 1, rows)
    flat = (picked.shape[0], rows)
    picked[:, :rows] = jnp.where(found & (line < SLOTS), 1.0, 0.0).reshape(flat).astype(BF16)
    picked[:, rows:] = jnp.where(found & (line >= SLOTS), 1.0, 0.0).reshape(flat).astype(BF16)
    c, s = cosine[...], sine[...]
    half = c.shape[1] // 2
    for gain, scale, turn_cos, turn_sin in (
        (q_ref[...], c.shape[1] ** (-0.5), q_cos, q_sin),
        (k_ref[...], 1.0, k_cos, k_sin),
    ):
        turn_cos[...] = c * (gain * scale)
        turn_sin[...] = s * (jnp.concatenate([gain[:, half:], gain[:, :half]], 1) * scale)


def project_kernel(shifts, me_ref, *refs):
    pieces, refs = refs[: len(shifts)], refs[len(shifts) :]
    q_cos, q_sin, k_cos, k_sin, picked, wq, wk, wv, out, held, sems = refs
    rows, width = pieces[0].shape[0] // 2, pieces[0].shape[1]
    groups = wq.shape[0] // width
    me = me_ref[0]
    steps = []
    for piece, shift in zip(pieces, shifts):
        source = lax.rem(me + (groups - 2 * shift), groups)
        for half in range(2):
            owner = source if half == 0 else source + 1 - 2 * lax.rem(source, 2)
            span = pl.ds(pl.multiple_of(owner * width, width), width)
            n, begin, copies = len(steps), 0, []
            for i, w in enumerate((wq, wk, wv)):
                to = held.at[n, :, begin : begin + w.shape[1]]
                copies.append(pltpu.make_async_copy(w.at[span, :], to, sems.at[n, i]))
                copies[-1].start()
                begin += w.shape[1]
            steps.append((copies, piece, half))
    total = jnp.zeros((rows, held.shape[2]), F32)
    for n, (copies, piece, half) in enumerate(steps):
        for copy in copies:
            copy.wait()
        block = piece[half * rows : (half + 1) * rows, :]
        total = total + jnp.dot(block, held[n], preferred_element_type=F32)
    head_dim = q_cos.shape[1]

    def turned(raw, turn_cos, turn_sin):
        scale = lax.rsqrt(jnp.mean(raw * raw, -1, keepdims=True) + 1e-06)
        return (
            (raw * turn_cos[...] + pltpu.roll(raw, head_dim // 2, 1) * turn_sin[...]) * scale
        ).astype(BF16)

    heads = [total[:, h : h + head_dim] for h in range(0, total.shape[1], head_dim)]
    top = jnp.concatenate([turned(h, q_cos, q_sin) for h in heads[:-2]], 1)
    low = jnp.concatenate([turned(heads[-2], k_cos, k_sin), heads[-1].astype(BF16)], 1)
    out[...] = jnp.dot(
        picked[...], jnp.concatenate([top, low], 0), preferred_element_type=F32
    ).astype(BF16)


def read_notes_kernel(me_ref, notes, landing, key_docs, doc_rows):
    me = me_ref[0]
    blocks, rows = notes.shape[0], notes.shape[2]
    got = notes[...].reshape(blocks, rows)
    doc_rows[...] = lax.div(got, LABEL)
    pair = 2 * SLOTS
    shape = (blocks * pair, rows)
    mixing = (blocks * pair, blocks)
    spread = hot(iota(mixing, 1) == lax.div(iota(mixing, 0), pair))
    labels = lax.rem(got, LABEL).astype(F32).astype(BF16)
    labels = jnp.dot(spread, labels, preferred_element_type=F32)
    place = lax.rem(iota(shape, 0), pair)
    lane = iota(shape, 1)
    for g in range(PAIRS):
        at = place + (2 * g - 1) * SLOTS
        if g == 0:
            at = jnp.where(at < 0, at + SLOTS, at)
        label = jnp.sum(jnp.where(lane == at, labels, 0.0), 1, keepdims=True).astype(I32)
        lands = lane + 1 == label
        for part, wanted in enumerate((place < SLOTS, place >= SLOTS)):
            part_hot = jnp.where(lands & wanted, 1.0, 0.0)
            landing[g, part * rows : (part + 1) * rows, :] = part_hot.T.astype(BF16)
    for back in range(SPAN + 1):
        row = doc_rows[pl.ds(jnp.maximum(me - back, 0), 1), :]
        key_docs[back : back + 1, :] = jnp.where(me >= back, row, -1)
    key_docs[SPAN + 1 :, :] = jnp.full((key_docs.shape[0] - SPAN - 1, rows), -1, I32)


def land_kernel(me_ref, landing, arrived, queries, keyvalues, sent):
    rows = landing.shape[1] // 2
    head_dim = queries.shape[1]
    pair = 2 * SLOTS
    for g in range(PAIRS):
        lines = arrived[:, g * pair : (g + 1) * pair, :].reshape(landing.shape[2], -1)
        placed = jnp.dot(landing[g], lines, preferred_element_type=F32).astype(BF16)
        if g == 0:
            for h in range(queries.shape[0] // rows):
                queries[h * rows : (h + 1) * rows, :] = placed[
                    :rows, h * head_dim : (h + 1) * head_dim
                ]
            keyvalues[:rows, :] = placed[rows:, :]
        else:
            keyvalues[(2 * g - 1) * rows : (2 * g + 1) * rows, :] = placed
    begin = pl.multiple_of(lax.rem(me_ref[0], 2) * rows, rows)
    sent[...] = keyvalues[pl.ds(begin, sent.shape[0]), :]


def attend(backs, rows, queries, query_docs, key_docs, keyvalues):
    head_dim = queries.shape[1]
    q = queries[...]
    q_doc = query_docs[...]
    scores = lax.dot_general(
        q, keyvalues[:, :head_dim], (((1,), (1,)), ((), ())), preferred_element_type=F32
    )
    docs = jnp.concatenate([key_docs[back : back + 1, :] for back in backs], 1)
    visible = q_doc == docs
    if 0 in backs:
        t, u = lax.rem(iota(scores.shape, 0), rows), iota(scores.shape, 1)
        visible = visible & ((u <= t) | (u >= rows))
    weights = jnp.where(visible, jnp.exp(scores), 0.0)
    denom = jnp.sum(weights, 1, keepdims=True)
    numer = jnp.dot(weights.astype(BF16), keyvalues[:, head_dim:], preferred_element_type=F32)
    return numer, denom


def attend_first_kernel(backs, queries, query_docs, key_docs, keyvalues, numer, denom):
    rows = key_docs.shape[1]
    n, d = attend(backs, rows, queries, query_docs, key_docs, keyvalues)
    numer[...] = n
    denom[...] = jnp.broadcast_to(d, denom.shape)


def attend_last_kernel(backs, queries, query_docs, key_docs, keyvalues, numer, denom, out):
    rows = out.shape[0]
    head_dim = queries.shape[1]
    n, d = attend(backs, rows, queries, query_docs, key_docs, keyvalues)
    result = ((numer[...] + n) / (denom[...] + d)).astype(BF16)
    for h in range(out.shape[1] // head_dim):
        out[:, h * head_dim : (h + 1) * head_dim] = result[h * rows : (h + 1) * rows, :]


VMEM = pl.BlockSpec(memory_space=pltpu.VMEM)
SMEM = pl.BlockSpec(memory_space=pltpu.SMEM)
HBM = pl.BlockSpec(memory_space=pltpu.HBM)


def call(kernel, outs, operands, scratch=(), flops=0, size=0, limit=24, away=()):
    specs = [SMEM if x.shape == (1,) else VMEM for x in operands]
    for i in away:
        specs[i] = HBM
    shapes = [jax.ShapeDtypeStruct(s, t) for s, t in outs]
    return pl.pallas_call(
        kernel,
        out_shape=shapes,
        in_specs=specs,
        out_specs=[VMEM] * len(shapes),
        scratch_shapes=scratch,
        cost_estimate=pl.CostEstimate(flops=flops, bytes_accessed=size, transcendentals=0),
        compiler_params=pltpu.CompilerParams(vmem_limit_bytes=limit * 2**20),
    )(*operands)


def rotation(positions, head_dim):
    half_dim = head_dim // 2
    exponent = jnp.arange(half_dim, dtype=F32) * (2.0 / head_dim)
    frequency = jnp.power(jnp.float32(1000000.0), -exponent)
    angles = positions.astype(F32)[:, None] * frequency[None, :]
    cosine, sine = jnp.cos(angles), jnp.sin(angles)
    return jnp.concatenate([cosine, cosine], 1), jnp.concatenate([-sine, sine], 1)


def body(hidden, destination, doc_ids, w_query, w_key, w_value, q_gain, k_gain):
    blocks = lax.axis_size("ctx")
    rows, width = hidden.shape
    q_width = w_query.shape[1]
    head_dim = q_gain.shape[0]
    q_rows = q_width // head_dim * rows
    me_kvh = lax.axis_index("kvh").astype(I32).reshape(1)
    me_ctx = lax.axis_index("ctx").astype(I32).reshape(1)

    n = lax.axis_size("kvh")
    across = lax.ppermute(hidden, "kvh", [(i, i ^ 1) for i in range(n)])
    notes, slot, query_docs, own = call(
        notes_kernel,
        [((blocks, 1, rows), I32), ((1, rows), I32), ((q_rows, 1), I32), (hidden.shape, BF16)],
        [destination.reshape(1, -1), doc_ids.reshape(1, -1), hidden],
        scratch=[pltpu.VMEM((1, rows), I32)] * 2 + [pltpu.SemaphoreType.DMA((2,))],
        away=(0, 1),
    )
    notes = lax.all_to_all(notes, "ctx", split_axis=0, concat_axis=0, tiled=True)
    own = jnp.concatenate([own, across], 0)
    shifts = (0, 1, 3, 2)
    pieces = [own] + [along_kvh(own, s) for s in shifts[1:]]
    landing, key_docs = call(
        read_notes_kernel,
        [((PAIRS, 2 * rows, blocks * 2 * SLOTS), BF16), ((16, rows), I32)],
        [me_ctx, notes],
        scratch=[pltpu.VMEM((blocks, rows), I32)],
    )
    cosine, sine = rotation(destination, head_dim)
    picked, q_cos, q_sin, k_cos, k_sin = call(
        tables_kernel,
        [((blocks * CHUNK, 2 * rows), BF16)] + [((rows, head_dim), F32)] * 4,
        [slot, q_gain.reshape(1, -1), k_gain.reshape(1, -1), cosine, sine],
        scratch=[pltpu.VMEM((1, head_dim), F32)] * 2 + [pltpu.SemaphoreType.DMA((2,))],
        away=(1, 2),
    )

    features = 2 * len(pieces)
    (parcel,) = call(
        functools.partial(project_kernel, shifts),
        [((blocks * CHUNK, 2 * head_dim), BF16)],
        [me_kvh, *pieces, q_cos, q_sin, k_cos, k_sin, picked, w_query, w_key, w_value],
        scratch=[
            pltpu.VMEM((features, width, q_width + 2 * head_dim), BF16),
            pltpu.SemaphoreType.DMA((features, 3)),
        ],
        away=(10, 11, 12),
    )
    arrived = lax.all_to_all(
        parcel.reshape(blocks, CHUNK, -1), "ctx", split_axis=0, concat_axis=0, tiled=True
    )
    held = SPAN // 2 + 1
    queries, keyvalues, sent = call(
        land_kernel,
        [
            ((q_rows, head_dim), BF16),
            ((held * rows, 2 * head_dim), BF16),
            (((held - 1) * rows, 2 * head_dim), BF16),
        ],
        [me_ctx, landing, arrived],
    )

    swapped = lax.ppermute(sent, "ctx", [(i, i ^ 1) for i in range(blocks)])
    numer, denom = call(
        functools.partial(attend_first_kernel, tuple(range(0, SPAN + 1, 2))),
        [((q_rows, head_dim), F32)] * 2,
        [queries, query_docs, key_docs, keyvalues],
    )
    (out,) = call(
        functools.partial(attend_last_kernel, tuple(range(1, SPAN + 1, 2))),
        [((rows, q_width), BF16)],
        [queries, query_docs, key_docs, swapped, numer, denom],
    )
    return out


def solution(mesh):
    placed = (
        P("ctx", "kvh"),
        P("ctx"),
        P("ctx"),
        P(None, "kvh"),
        P(None, "kvh"),
        P(None, "kvh"),
        P(),
        P(),
    )
    return jax.shard_map(
        body, mesh=mesh, in_specs=placed, out_specs=P("ctx", "kvh"), check_vma=False
    )
```

time: 205 us -> 88.9 us (0.43)
  the two profiles are of different devices: /device:TPU:8 before, /device:TPU:1 now
where the time goes in v2:
time: 88.9 us; the launch traced here: 87.9 us
  starting transfers between devices  45 us (51%)
  waiting for transfers between devices  27.5 us (31%)
  Pallas kernels  7.76 us (9%)
  local copies, waits for them, and re-layouts  6.36 us (7%)
  other arithmetic  1.08 us (1%)
    all_to_all x1, waiting for transfers between devices, body(): lax.all_to_all(parcel.reshape(blocks, CHUNK, -1), 'ctx', split_axis=0, co...  22.1 us
    all_to_all x1, starting transfers between devices, body(): lax.all_to_all(parcel.reshape(blocks, CHUNK, -1), 'ctx', split_axis=0, co...  12.3 us
    all_to_all x1, starting transfers between devices, body(): lax.all_to_all(notes, 'ctx', split_axis=0, concat_axis=0, tiled=True)  12.2 us
    ppermute x3, starting transfers between devices, along_kvh(): lax.ppermute(block, 'kvh', [(i, (i + 2 * shift) % n) for i in range(n)])  9.93 us
    ppermute x1, starting transfers between devices, body(): across = lax.ppermute(hidden, 'kvh', [(i, i ^ 1) for i in range(n)])  8.4 us
    pallas_call x7, Pallas kernels, call(): pl.pallas_call(kernel, out_shape=shapes, in_specs=specs, out_specs=[VMEM]...  7.76 us
    unnamed x17, local copies, waits for them, and re-layouts  6.35 us
    ppermute x3, waiting for transfers between devices, along_kvh(): lax.ppermute(block, 'kvh', [(i, (i + 2 * shift) % n) for i in range(n)])  4.53 us
  transfers between devices with their start and end apart: 7, of which 3 were waited for; matrix products, arithmetic and copies ran while one was open for 1% of the time, Pallas kernels for 7%

profile of v2, /device:TPU:1, one launch (start us, length us, event | category | flops | bytes accessed | tf_op | source)
XLA Modules:
  0.0 87.9 jit_solution(16336905013988294159)
XLA Ops:
  0.0 0.0 copy-start.1
  0.0 8.4 %collective-permute-start = (bf16[128,512]{1,0:T(8,128)(2,1)}, bf16[128,512]{1,0:T(8,128)(2,1)S(1)}, u32[]{:S(2)}, u32[]{:S(2)}) collective-permute-start(bf16[128,512]{1,0:T(8,128)(2,1)} %hidden.1), channel_id=1, source_target_pairs={{0,1},{1,0},{2,3},{3,2},{4,5},{5,4},{6,7},{7,6},{8,9},{9,8},{10,11... | collective-permute-start | bytes 393224 | tf_op jit(solution)/shard_map/ppermute | solution.py:255
  8.4 0.0 copy-start.3
  8.4 0.9 %copy-done.3 = bf16[128,512]{1,0:T(8,128)(2,1)S(1)} copy-done((bf16[128,512]{1,0:T(8,128)(2,1)S(1)}, bf16[128,512]{1,0:T(8,128)(2,1)}, u32[]{:S(2)}) %copy-start.3) | copy-done | bytes 131096
  9.3 0.0 copy-start.4
  9.3 0.7 copy-done.4
  10.0 0.0 copy-start.5
  10.0 0.7 copy-done.5
  10.6 1.1 %shard_map.82 = (s32[64,1,128]{2,1,0:T(1,128)}, s32[1,128]{1,0:T(1,128)S(1)}, s32[256,1]{1,0:T(8,128)S(1)}, bf16[128,512]{1,0:T(8,128)(2,1)S(1)}) custom-call(s32[1,128]{1,0:T(1,128)S(1)} %bitcast.8, s32[1,128]{1,0:T(1,128)S(1)} %bitcast.7, bf16[128,512]{1,0:T(8,128)(2,1)S(1)} %copy-done.3), custom_call_target="tpu_custom_call" | custom-call | tf_op jit(solution)/shard_map/pallas_call | solution.py:225
  11.7 12.2 %all-to-all-start = ((s32[64,1,128]{2,1,0:T(1,128)}), s32[64,1,128]{2,1,0:T(1,128)S(1)}, u32[]{:S(2)}, u32[]{:S(2)}) async-start(s32[64,1,128]{2,1,0:T(1,128)} %get-tuple-element.21), calls=%async_computation | async-start | bytes 65536 | tf_op jit(solution)/shard_map/all_to_all | solution.py:263
  23.9 0.7 convert_element_type.3
  24.6 0.0 collective-permute-done
  24.6 3.1 %collective-permute-start.1 = (bf16[256,512]{1,0:T(8,128)(2,1)S(1)}, bf16[256,512]{1,0:T(8,128)(2,1)S(1)}, u32[]{:S(2)}, u32[]{:S(2)}) collective-permute-start(bf16[256,512]{1,0:T(8,128)(2,1)S(1)} %constant_dynamic-update-slice_fusion.refs_0_), channel_id=1, source_target_pairs={{0,2},{1,3},{2,4},{3,5},{4,6},{5,7},{6,0},{7,1},{8,10},{9,11},{10,... | collective-permute-start | bytes 786440 | tf_op jit(solution)/shard_map/ppermute | solution.py:21
  27.8 3.4 %collective-permute-start.2 = (bf16[256,512]{1,0:T(8,128)(2,1)S(1)}, bf16[256,512]{1,0:T(8,128)(2,1)S(1)}, u32[]{:S(2)}, u32[]{:S(2)}) collective-permute-start(bf16[256,512]{1,0:T(8,128)(2,1)S(1)} %constant_dynamic-update-slice_fusion.refs_0_), channel_id=1, source_target_pairs={{0,6},{1,7},{2,0},{3,1},{4,2},{5,3},{6,4},{7,5},{8,14},{9,15},{10,... | collective-permute-start | bytes 786440 | tf_op jit(solution)/shard_map/ppermute | solution.py:21
  31.1 3.4 %collective-permute-start.3 = (bf16[256,512]{1,0:T(8,128)(2,1)S(1)}, bf16[256,512]{1,0:T(8,128)(2,1)S(1)}, u32[]{:S(2)}, u32[]{:S(2)}) collective-permute-start(bf16[256,512]{1,0:T(8,128)(2,1)S(1)} %constant_dynamic-update-slice_fusion.refs_0_), channel_id=1, source_target_pairs={{0,4},{1,5},{2,6},{3,7},{4,0},{5,1},{6,2},{7,3},{8,12},{9,13},{10,... | collective-permute-start | bytes 786440 | tf_op jit(solution)/shard_map/ppermute | solution.py:21
  34.6 0.3 fusion
  34.9 0.1 pad_maximum_fusion
  35.0 0.0 copy-start.6
  35.0 0.6 copy-done.6
  35.7 0.0 copy-start.7
  35.7 0.7 copy-done.7
  36.3 0.4 shard_map.84
  36.8 0.0 collective-permute-done.1.refs_1_
  36.8 0.0 collective-permute-done.2.refs_2_
  36.8 4.5 %collective-permute-done.3.refs_3_ = bf16[256,512]{1,0:T(8,128)(2,1)S(1)} collective-permute-done((bf16[256,512]{1,0:T(8,128)(2,1)S(1)}, bf16[256,512]{1,0:T(8,128)(2,1)S(1)}, u32[]{:S(2)}, u32[]{:S(2)}) %collective-permute-start.3) | collective-permute-done | bytes 262176 | tf_op jit(solution)/shard_map/ppermute | solution.py:21
  41.3 0.0 copy-done.1
  41.3 0.0 copy-start
  41.3 1.6 %copy-done = bf16[4096,256]{1,0:T(8,128)(2,1)S(1)} copy-done((bf16[4096,256]{1,0:T(8,128)(2,1)S(1)}, bf16[4096,256]{1,0:T(8,128)(2,1)}, u32[]{:S(2)}) %copy-start) | copy-done | bytes 2097176
  42.9 0.0 copy-start.2
  42.9 1.2 %copy-done.2 = bf16[4096,128]{1,0:T(8,128)(2,1)S(1)} copy-done((bf16[4096,128]{1,0:T(8,128)(2,1)S(1)}, bf16[4096,128]{1,0:T(8,128)(2,1)}, u32[]{:S(2)}) %copy-start.2) | copy-done | bytes 1048600
  44.1 3.5 %shard_map.85 = bf16[1536,256]{1,0:T(8,128)(2,1)} custom-call(s32[1]{0:T(128)} %bitcast.3.me_ref, bf16[256,512]{1,0:T(8,128)(2,1)S(1)} %constant_dynamic-update-slice_fusion.refs_0_, bf16[256,512]{1,0:T(8,128)(2,1)S(1)} %collective-permute-done.1.refs_1_, bf16[256,512]{1,0:T(8,128)(2,1)S(1)} %collective-permute-done.2.refs_2_, ...), custom_call_target="tpu_custom_call" | custom-call | tf_op jit(solution)/shard_map/pallas_call | solution.py:225
  47.7 0.0 all-to-all-done.notes
  47.7 12.3 %all-to-all-start.1 = ((bf16[64,24,256]{2,1,0:T(8,128)(2,1)}), bf16[64,24,256]{2,1,0:T(8,128)(2,1)S(1)}, u32[]{:S(2)}, u32[]{:S(2)}) async-start(bf16[64,24,256]{2,1,0:T(8,128)(2,1)} %bitcast.6), calls=%async_computation.1 | async-start | bytes 1572864 | tf_op jit(solution)/shard_map/all_to_all | solution.py:293
  60.0 0.9 shard_map.83
  60.9 22.1 %all-to-all-done.1.arrived = bf16[64,24,256]{2,1,0:T(8,128)(2,1)S(1)} async-done(((bf16[64,24,256]{2,1,0:T(8,128)(2,1)}), bf16[64,24,256]{2,1,0:T(8,128)(2,1)S(1)}, u32[]{:S(2)}, u32[]{:S(2)}) %all-to-all-start.1) | async-done | bytes 786464 | tf_op jit(solution)/shard_map/all_to_all | solution.py:293
  83.0 0.4 shard_map.86
  83.4 2.1 %collective-permute-start.4 = (bf16[512,256]{1,0:T(8,128)(2,1)S(1)}, bf16[512,256]{1,0:T(8,128)(2,1)S(1)}, u32[]{:S(2)}, u32[]{:S(2)}) collective-permute-start(bf16[512,256]{1,0:T(8,128)(2,1)S(1)} %get-tuple-element.33), channel_id=1, source_target_pairs={{0,8},{8,0},{16,24},{24,16},{32,40},{40,32},{48,56},{56,48},{64,72... | collective-permute-start | bytes 786440 | tf_op jit(solution)/shard_map/ppermute | solution.py:307
  85.6 0.4 shard_map.87
  86.0 0.8 collective-permute-done.4.keyvalues
  86.9 1.0 %shard_map.88 = bf16[128,256]{1,0:T(8,128)(2,1)} custom-call(bf16[256,128]{1,0:T(8,128)(2,1)S(1)} %get-tuple-element.30.queries, s32[256,1]{1,0:T(8,128)S(1)} %get-tuple-element.31.query_docs, s32[16,128]{1,0:T(8,128)S(1)} %get-tuple-element.32.key_docs, bf16[512,256]{1,0:T(8,128)(2,1)S(1)} %collective-permute-done.4.keyvalues, ...), custom_call_target="tpu_custom_call" | custom-call | tf_op jit(solution)/shard_map/pallas_call | solution.py:225
  (3 shorter events, 0.0 us)
Async XLA Ops:
  0.0 41.3 %copy-start.1 = (bf16[4096,128]{1,0:T(8,128)(2,1)S(1)}, bf16[4096,128]{1,0:T(8,128)(2,1)}, u32[]{:S(2)}) copy-start(bf16[4096,128]{1,0:T(8,128)(2,1)} %refs_10_.1) | copy-start | bytes 3145732
  0.0 24.6 %collective-permute-start = (bf16[128,512]{1,0:T(8,128)(2,1)}, bf16[128,512]{1,0:T(8,128)(2,1)S(1)}, u32[]{:S(2)}, u32[]{:S(2)}) collective-permute-start(bf16[128,512]{1,0:T(8,128)(2,1)} %hidden.1), channel_id=1, source_target_pairs={{0,1},{1,0},{2,3},{3,2},{4,5},{5,4},{6,7},{7,6},{8,9},{9,8},{10,11... | collective-permute-start | bytes 393224 | tf_op jit(solution)/shard_map/ppermute | solution.py:255
  8.4 0.9 %copy-start.3 = (bf16[128,512]{1,0:T(8,128)(2,1)S(1)}, bf16[128,512]{1,0:T(8,128)(2,1)}, u32[]{:S(2)}) copy-start(bf16[128,512]{1,0:T(8,128)(2,1)} %hidden.1) | copy-start | bytes 393220
  9.3 0.7 copy-start.4
  10.0 0.7 copy-start.5
  11.7 36.0 %all-to-all-start = ((s32[64,1,128]{2,1,0:T(1,128)}), s32[64,1,128]{2,1,0:T(1,128)S(1)}, u32[]{:S(2)}, u32[]{:S(2)}) async-start(s32[64,1,128]{2,1,0:T(1,128)} %get-tuple-element.21), calls=%async_computation | async-start | bytes 65536 | tf_op jit(solution)/shard_map/all_to_all | solution.py:263
  24.6 12.1 %collective-permute-start.1 = (bf16[256,512]{1,0:T(8,128)(2,1)S(1)}, bf16[256,512]{1,0:T(8,128)(2,1)S(1)}, u32[]{:S(2)}, u32[]{:S(2)}) collective-permute-start(bf16[256,512]{1,0:T(8,128)(2,1)S(1)} %constant_dynamic-update-slice_fusion.refs_0_), channel_id=1, source_target_pairs={{0,2},{1,3},{2,4},{3,5},{4,6},{5,7},{6,0},{7,1},{8,10},{9,11},{10,... | collective-permute-start | bytes 786440 | tf_op jit(solution)/shard_map/ppermute | solution.py:21
  27.8 9.0 %collective-permute-start.2 = (bf16[256,512]{1,0:T(8,128)(2,1)S(1)}, bf16[256,512]{1,0:T(8,128)(2,1)S(1)}, u32[]{:S(2)}, u32[]{:S(2)}) collective-permute-start(bf16[256,512]{1,0:T(8,128)(2,1)S(1)} %constant_dynamic-update-slice_fusion.refs_0_), channel_id=1, source_target_pairs={{0,6},{1,7},{2,0},{3,1},{4,2},{5,3},{6,4},{7,5},{8,14},{9,15},{10,... | collective-permute-start | bytes 786440 | tf_op jit(solution)/shard_map/ppermute | solution.py:21
  31.1 10.2 %collective-permute-start.3 = (bf16[256,512]{1,0:T(8,128)(2,1)S(1)}, bf16[256,512]{1,0:T(8,128)(2,1)S(1)}, u32[]{:S(2)}, u32[]{:S(2)}) collective-permute-start(bf16[256,512]{1,0:T(8,128)(2,1)S(1)} %constant_dynamic-update-slice_fusion.refs_0_), channel_id=1, source_target_pairs={{0,4},{1,5},{2,6},{3,7},{4,0},{5,1},{6,2},{7,3},{8,12},{9,13},{10,... | collective-permute-start | bytes 786440 | tf_op jit(solution)/shard_map/ppermute | solution.py:21
  35.0 0.7 copy-start.6
  35.7 0.7 copy-start.7
  41.3 1.6 %copy-start = (bf16[4096,256]{1,0:T(8,128)(2,1)S(1)}, bf16[4096,256]{1,0:T(8,128)(2,1)}, u32[]{:S(2)}) copy-start(bf16[4096,256]{1,0:T(8,128)(2,1)} %refs_9_.1) | copy-start | bytes 6291460
  42.9 1.2 %copy-start.2 = (bf16[4096,128]{1,0:T(8,128)(2,1)S(1)}, bf16[4096,128]{1,0:T(8,128)(2,1)}, u32[]{:S(2)}) copy-start(bf16[4096,128]{1,0:T(8,128)(2,1)} %refs_11_.1) | copy-start | bytes 3145732
  47.7 35.3 %all-to-all-start.1 = ((bf16[64,24,256]{2,1,0:T(8,128)(2,1)}), bf16[64,24,256]{2,1,0:T(8,128)(2,1)S(1)}, u32[]{:S(2)}, u32[]{:S(2)}) async-start(bf16[64,24,256]{2,1,0:T(8,128)(2,1)} %bitcast.6), calls=%async_computation.1 | async-start | bytes 1572864 | tf_op jit(solution)/shard_map/all_to_all | solution.py:293
  83.4 3.4 %collective-permute-start.4 = (bf16[512,256]{1,0:T(8,128)(2,1)S(1)}, bf16[512,256]{1,0:T(8,128)(2,1)S(1)}, u32[]{:S(2)}, u32[]{:S(2)}) collective-permute-start(bf16[512,256]{1,0:T(8,128)(2,1)S(1)} %get-tuple-element.33), channel_id=1, source_target_pairs={{0,8},{8,0},{16,24},{24,16},{32,40},{40,32},{48,56},{56,48},{64,72... | collective-permute-start | bytes 786440 | tf_op jit(solution)/shard_map/ppermute | solution.py:307

commit v3 on v2

v3 whole, which is shorter than its diff:
```python
import functools

import jax
import jax.numpy as jnp
from jax import lax
from jax.experimental import pallas as pl
from jax.experimental.pallas import tpu as pltpu
from jax.sharding import PartitionSpec as P

SPAN = 8
SLOTS = 4
PARTS = 1 + SPAN // 2 + 1
PAIRS = PARTS // 2
LINES = 2 * SLOTS
NOTED = 64
F32, BF16, I32 = jnp.float32, jnp.bfloat16, jnp.int32


def block_back(part):
    return 2 * max(part - 1, 0)


def iota(shape, dim):
    return lax.broadcasted_iota(I32, shape, dim)


def hot(mask):
    return jnp.where(mask, 1.0, 0.0).astype(BF16)


def column(row):
    square = (row.shape[1], row.shape[1])
    return jnp.sum(jnp.where(iota(square, 0) == iota(square, 1), row, 0), 1, keepdims=True)


def fetch(pairs, sems):
    copies = [pltpu.make_async_copy(a, b, sems.at[i]) for i, (a, b) in enumerate(pairs)]
    for copy in copies:
        copy.start()
    for copy in copies:
        copy.wait()


def spread_own_kernel(hidden, spread, sems):
    fetch([(hidden, spread.at[0])], sems)
    for i in range(1, spread.shape[0]):
        spread[i] = spread[0]


def spread_kernel(across, table, spread):
    for i in range(spread.shape[0]):
        spread[i] = across[...]


def tables_kernel(
    cosine, sine, destination, doc_ids, q_gain, k_gain,
    own, later, notes, query_docs, q_cos, q_sin, k_cos, k_sin,
    place_ref, docs_ref, q_ref, k_ref, sems,
):
    small = [(destination, place_ref), (doc_ids, docs_ref), (q_gain, q_ref), (k_gain, k_ref)]
    fetch(small, sems)
    place, docs = place_ref[...], docs_ref[...]
    rows = place.shape[1]
    target, inside = lax.div(place, rows), lax.rem(place, rows)
    square = (rows, rows)
    earlier = (column(target) == target) & (iota(square, 0) < iota(square, 1))
    order = jnp.sum(jnp.where(earlier, 1, 0), 0, keepdims=True)
    slot = (target * SLOTS + order).reshape(1, 1, rows)
    label = column(inside) + 1
    shape = (own.shape[0] // LINES, LINES, rows)
    flat = (own.shape[0], rows)
    block, line = iota(shape, 0), iota(shape, 1)
    noted = jnp.zeros(flat, F32)
    for g in range(PAIRS):
        back = jnp.where(line < SLOTS, block_back(2 * g), block_back(2 * g + 1))
        at = jnp.where(line < SLOTS, line, line - SLOTS)
        found = (block - back) * SLOTS + at == slot
        picked = jnp.where(found, 1.0, 0.0).reshape(flat).astype(BF16)
        if g == 0:
            own[:, :rows] = jnp.where(found & (line < SLOTS), 1.0, 0.0).reshape(flat).astype(BF16)
            own[:, rows:] = jnp.where(found & (line >= SLOTS), 1.0, 0.0).reshape(flat).astype(BF16)
        else:
            later[g - 1] = picked
        lane = jnp.where(iota(square, 1) == g, label, 0).astype(F32).astype(BF16)
        noted += jnp.dot(picked, lane, preferred_element_type=F32)
    kept = docs.astype(F32)
    halves = [jnp.concatenate([jnp.zeros((1, rows - NOTED), F32), kept[:, h : h + NOTED]], 1) for h in range(0, rows, NOTED)]
    doc_lines = sum(
        jnp.where(line == h, half.reshape(1, 1, rows), 0.0) for h, half in enumerate(halves)
    )
    notes[...] = (noted + doc_lines.reshape(flat)).astype(BF16)
    docs_col = column(docs)
    for h in range(query_docs.shape[0] // rows):
        query_docs[h * rows : (h + 1) * rows, :] = docs_col
    c, s = cosine[...], sine[...]
    half = c.shape[1] // 2
    for gain, scale, turn_cos, turn_sin in (
        (q_ref[...], c.shape[1] ** (-0.5), q_cos, q_sin),
        (k_ref[...], 1.0, k_cos, k_sin),
    ):
        turn_cos[...] = c * (gain * scale)
        turn_sin[...] = s * (jnp.concatenate([gain[:, half:], gain[:, :half]], 1) * scale)


def partial_projection(pieces, side, weights, held, sems):
    width = pieces[0].shape[1]
    steps = []
    for k in range(len(pieces)):
        span = pl.ds(pl.multiple_of((2 * k + side) * width, width), width)
        steps.append(
            [
                pltpu.make_async_copy(w.at[span, :], to.at[k], sems.at[k, i])
                for i, (w, to) in enumerate(zip(weights, held))
            ]
        )
        for copy in steps[-1]:
            copy.start()
    total = jnp.zeros((pieces[0].shape[0], sum(w.shape[1] for w in weights)), F32)
    for k, (piece, copies) in enumerate(zip(pieces, steps)):
        for copy in copies:
            copy.wait()
        block = jnp.concatenate([to[k] for to in held], 1)
        total = total + jnp.dot(piece[...], block, preferred_element_type=F32)
    return total


def project_first_kernel(me_ref, mine, wq, wk, wv, first, *room):
    pieces = [mine.at[k] for k in range(mine.shape[0])]
    side = lax.rem(me_ref[0], 2)
    first[...] = partial_projection(pieces, side, (wq, wk, wv), room[:-1], room[-1])


def project_kernel(
    me_ref, first, other, q_cos, q_sin, k_cos, k_sin, own, later, notes, wq, wk, wv,
    out, *room,
):
    pieces = [other.at[k] for k in range(other.shape[0])]
    side = 1 - lax.rem(me_ref[0], 2)
    total = first[...] + partial_projection(pieces, side, (wq, wk, wv), room[:-1], room[-1])
    head_dim = q_cos.shape[1]

    def turned(raw, turn_cos, turn_sin):
        scale = lax.rsqrt(jnp.mean(raw * raw, -1, keepdims=True) + 1e-06)
        return (
            (raw * turn_cos[...] + pltpu.roll(raw, head_dim // 2, 1) * turn_sin[...]) * scale
        ).astype(BF16)

    heads = [total[:, h : h + head_dim] for h in range(0, total.shape[1], head_dim)]
    top = jnp.concatenate([turned(h, q_cos, q_sin) for h in heads[:-2]], 1)
    low = jnp.concatenate([turned(heads[-2], k_cos, k_sin), heads[-1].astype(BF16)], 1)
    both = jnp.concatenate([top, low], 0)
    width = low.shape[1]
    for g in range(PAIRS):
        picked, lines = (own[...], both) if g == 0 else (later[g - 1], low)
        out[:, g * width : (g + 1) * width] = jnp.dot(
            picked, lines, preferred_element_type=F32
        ).astype(BF16)
    out[:, PAIRS * width :] = notes[...]


def land_kernel(me_ref, arrived, queries, keyvalues, sent, key_docs, doc_lines):
    me = me_ref[0]
    rows = key_docs.shape[1]
    width = keyvalues.shape[1]
    head_dim = queries.shape[1]
    noted = arrived[:, PAIRS * width :].astype(F32)
    doc_lines[...] = noted
    shape = noted.shape
    first = lax.rem(iota(shape, 0), LINES) < SLOTS
    spot = (iota(shape, 1) + 1).astype(F32)
    for g in range(PAIRS):
        lands = noted[:, g : g + 1] == spot
        landing = jnp.concatenate([hot(lands & first), hot(lands & ~first)], 1)
        placed = lax.dot_general(
            landing,
            arrived[:, g * width : (g + 1) * width],
            (((0,), (0,)), ((), ())),
            preferred_element_type=F32,
        ).astype(BF16)
        if g == 0:
            for h in range(queries.shape[0] // rows):
                queries[h * rows : (h + 1) * rows, :] = placed[
                    :rows, h * head_dim : (h + 1) * head_dim
                ]
            keyvalues[:rows, :] = placed[rows:, :]
        else:
            keyvalues[(2 * g - 1) * rows : (2 * g + 1) * rows, :] = placed
    begin = pl.multiple_of(lax.rem(me, 2) * rows, rows)
    sent[...] = keyvalues[pl.ds(begin, sent.shape[0]), :]
    for back in range(SPAN + 1):
        owner = pl.multiple_of(jnp.maximum(me - back, 0) * LINES, LINES)
        lines = doc_lines[pl.ds(owner, LINES), :]
        docs = jnp.concatenate([lines[h : h + 1, NOTED:] for h in range(rows // NOTED)], 1)
        key_docs[back : back + 1, :] = jnp.where(me >= back, docs.astype(I32), -1)
    key_docs[SPAN + 1 :, :] = jnp.full((key_docs.shape[0] - SPAN - 1, rows), -1, I32)


def attend(backs, rows, queries, query_docs, key_docs, keyvalues):
    head_dim = queries.shape[1]
    q = queries[...]
    q_doc = query_docs[...]
    scores = lax.dot_general(
        q, keyvalues[:, :head_dim], (((1,), (1,)), ((), ())), preferred_element_type=F32
    )
    docs = jnp.concatenate([key_docs[back : back + 1, :] for back in backs], 1)
    visible = q_doc == docs
    if 0 in backs:
        t, u = lax.rem(iota(scores.shape, 0), rows), iota(scores.shape, 1)
        visible = visible & ((u <= t) | (u >= rows))
    weights = jnp.where(visible, jnp.exp(scores), 0.0)
    denom = jnp.sum(weights, 1, keepdims=True)
    numer = jnp.dot(weights.astype(BF16), keyvalues[:, head_dim:], preferred_element_type=F32)
    return numer, denom


def attend_first_kernel(backs, queries, query_docs, key_docs, keyvalues, numer, denom):
    rows = key_docs.shape[1]
    n, d = attend(backs, rows, queries, query_docs, key_docs, keyvalues)
    numer[...] = n
    denom[...] = jnp.broadcast_to(d, denom.shape)


def attend_last_kernel(backs, queries, query_docs, key_docs, keyvalues, numer, denom, out):
    rows = out.shape[0]
    head_dim = queries.shape[1]
    n, d = attend(backs, rows, queries, query_docs, key_docs, keyvalues)
    result = ((numer[...] + n) / (denom[...] + d)).astype(BF16)
    for h in range(out.shape[1] // head_dim):
        out[:, h * head_dim : (h + 1) * head_dim] = result[h * rows : (h + 1) * rows, :]


TABLES_COST = 3 * 10**9
VMEM = pl.BlockSpec(memory_space=pltpu.VMEM)
SMEM = pl.BlockSpec(memory_space=pltpu.SMEM)
HBM = pl.BlockSpec(memory_space=pltpu.HBM)


def call(kernel, outs, operands, away=(), scratch=(), limit=24, near=(), cost=None):
    shapes = [
        pltpu.VMEM(s, t) if i in near else jax.ShapeDtypeStruct(s, t)
        for i, (s, t) in enumerate(outs)
    ]
    return pl.pallas_call(
        kernel,
        out_shape=shapes,
        in_specs=[SMEM if x.shape == (1,) else VMEM for x in operands] + [HBM] * len(away),
        out_specs=[VMEM] * len(shapes),
        scratch_shapes=scratch,
        cost_estimate=cost and pl.CostEstimate(flops=cost, bytes_accessed=0, transcendentals=0),
        compiler_params=pltpu.CompilerParams(vmem_limit_bytes=limit * 2**20),
    )(*operands, *[pltpu.with_memory_space_constraint(x, pltpu.HBM) for x in away])


def rotation(positions, head_dim):
    half_dim = head_dim // 2
    exponent = jnp.arange(half_dim, dtype=F32) * (2.0 / head_dim)
    frequency = jnp.power(jnp.float32(1000000.0), -exponent)
    angles = positions.astype(F32)[:, None] * frequency[None, :]
    cosine, sine = jnp.cos(angles), jnp.sin(angles)
    return jnp.concatenate([cosine, cosine], 1), jnp.concatenate([-sine, sine], 1)


def body(hidden, destination, doc_ids, w_query, w_key, w_value, q_gain, k_gain):
    blocks = lax.axis_size("ctx")
    rows, width = hidden.shape
    q_width = w_query.shape[1]
    head_dim = q_gain.shape[0]
    q_rows = q_width // head_dim * rows
    me_kvh = lax.axis_index("kvh").astype(I32).reshape(1)
    me_ctx = lax.axis_index("ctx").astype(I32).reshape(1)

    n = lax.axis_size("kvh")
    along_x = [list(range(side, n, 2)) for side in range(2)]
    members = len(along_x[0])
    across = lax.ppermute(hidden, "kvh", [(i, i ^ 1) for i in range(n)])
    (spread,) = call(
        spread_own_kernel,
        [((members, rows, width), BF16)],
        [],
        [hidden],
        scratch=[pltpu.SemaphoreType.DMA((1,))],
    )
    mine = lax.all_to_all(spread, "kvh", 0, 0, tiled=True, axis_index_groups=along_x)
    cosine, sine = rotation(destination, head_dim)
    lines = blocks * LINES
    own, later, notes, query_docs, q_cos, q_sin, k_cos, k_sin = call(
        tables_kernel,
        [
            ((lines, 2 * rows), BF16),
            ((PAIRS - 1, lines, rows), BF16),
            ((lines, rows), BF16),
            ((q_rows, 1), I32),
        ]
        + [((rows, head_dim), F32)] * 4,
        [cosine, sine],
        [destination.reshape(1, -1), doc_ids.reshape(1, -1)]
        + [q_gain.reshape(1, -1), k_gain.reshape(1, -1)],
        scratch=[pltpu.VMEM((1, rows), I32)] * 2
        + [pltpu.VMEM((1, head_dim), F32)] * 2
        + [pltpu.SemaphoreType.DMA((4,))],
        cost=TABLES_COST,
    )
    (spread,) = call(spread_kernel, [((members, rows, width), BF16)], [across, q_cos])
    other = lax.all_to_all(spread, "kvh", 0, 0, tiled=True, axis_index_groups=along_x)

    columns = PAIRS * 2 * head_dim + rows
    weights = [w_query, w_key, w_value]
    all_heads = q_width + 2 * head_dim
    room = [pltpu.VMEM((members, width, w.shape[1]), BF16) for w in weights]
    room.append(pltpu.SemaphoreType.DMA((members, len(weights))))
    (first,) = call(
        project_first_kernel, [((rows, all_heads), F32)], [me_kvh, mine], weights, scratch=room
    )
    (parcel,) = call(
        project_kernel,
        [((lines, columns), BF16)],
        [me_kvh, first, other, q_cos, q_sin, k_cos, k_sin, own, later, notes],
        weights,
        scratch=room,
    )
    arrived = lax.all_to_all(
        parcel.reshape(blocks, LINES, columns), "ctx", split_axis=0, concat_axis=0, tiled=True
    ).reshape(lines, columns)
    held = SPAN // 2 + 1
    queries, keyvalues, sent, key_docs = call(
        land_kernel,
        [
            ((q_rows, head_dim), BF16),
            ((held * rows, 2 * head_dim), BF16),
            (((held - 1) * rows, 2 * head_dim), BF16),
            ((16, rows), I32),
        ],
        [me_ctx, arrived],
        scratch=[pltpu.VMEM((lines, rows), F32)],
    )

    swapped = lax.ppermute(sent, "ctx", [(i, i ^ 1) for i in range(blocks)])
    numer, denom = call(
        functools.partial(attend_first_kernel, tuple(range(0, SPAN + 1, 2))),
        [((q_rows, head_dim), F32)] * 2,
        [queries, query_docs, key_docs, keyvalues],
    )
    (out,) = call(
        functools.partial(attend_last_kernel, tuple(range(1, SPAN + 1, 2))),
        [((rows, q_width), BF16)],
        [queries, query_docs, key_docs, swapped, numer, denom],
    )
    return out


def solution(mesh):
    placed = (
        P("ctx", "kvh"),
        P("ctx"),
        P("ctx"),
        P(None, "kvh"),
        P(None, "kvh"),
        P(None, "kvh"),
        P(),
        P(),
    )
    return jax.shard_map(
        body, mesh=mesh, in_specs=placed, out_specs=P("ctx", "kvh"), check_vma=False
    )
```

time: 88.9 us -> 82.3 us (0.926)
  starting transfers between devices: 45 us -> 32.6 us
  waiting for transfers between devices: 27.5 us -> 36.7 us
  local copies, waits for them, and re-layouts: 6.36 us -> 0 us
  Pallas kernels: 7.76 us -> 11.4 us
    all_to_all x2 -> x3, waiting for transfers between devices: 22.1 us -> 35.7 us  [the longest x1 25.8 us: body(): lax.all_to_all(parcel.reshape(blocks, LINES, columns), 'ctx', split_axis=...]
    ppermute x3 -> x0, starting transfers between devices: 9.93 us -> none  [along_kvh(): lax.ppermute(block, 'kvh', [(i, (i + 2 * shift) % n) for i in range(n)])]
    unnamed x17 -> x0, local copies, waits for them, and re-layouts: 6.35 us -> none
    ppermute x3 -> x0, waiting for transfers between devices: 4.53 us -> none  [along_kvh(): lax.ppermute(block, 'kvh', [(i, (i + 2 * shift) % n) for i in range(n)])]
    pallas_call x7 -> x8, Pallas kernels: 7.76 us -> 11.4 us  [call(): pl.pallas_call(kernel, out_shape=shapes, in_specs=[SMEM if x.shape == (1,...]
    all_to_all x2 -> x3, starting transfers between devices: 24.5 us -> 22.3 us  [the longest x1 14.8 us: body(): lax.all_to_all(parcel.reshape(blocks, LINES, columns), 'ctx', split_axis=...]
  transfers between devices with their start and end apart: 7 -> 5, of which waited for: 3 -> 4; matrix products, arithmetic and copies ran while one was open for 1% -> 1% of each run, Pallas kernels for 7% -> 7%
where the time goes in v3:
time: 82.3 us; the launch traced here: 81.9 us
  waiting for transfers between devices  36.7 us (45%)
  starting transfers between devices  32.6 us (40%)
  Pallas kernels  11.4 us (14%)
  other arithmetic  1.08 us (1%)
    all_to_all x1, waiting for transfers between devices, body(): lax.all_to_all(parcel.reshape(blocks, LINES, columns), 'ctx', split_axis=...  25.8 us
    all_to_all x1, starting transfers between devices, body(): lax.all_to_all(parcel.reshape(blocks, LINES, columns), 'ctx', split_axis=...  14.8 us
    pallas_call x8, Pallas kernels, call(): pl.pallas_call(kernel, out_shape=shapes, in_specs=[SMEM if x.shape == (1,...  11.4 us
    all_to_all x2, waiting for transfers between devices, body(): lax.all_to_all(spread, 'kvh', 0, 0, tiled=True, axis_index_groups=along_x)  9.87 us
    ppermute x1, starting transfers between devices, body(): across = lax.ppermute(hidden, 'kvh', [(i, i ^ 1) for i in range(n)])  8.27 us
    all_to_all x2, starting transfers between devices, body(): lax.all_to_all(spread, 'kvh', 0, 0, tiled=True, axis_index_groups=along_x)  7.49 us
    ppermute x1, starting transfers between devices, body(): swapped = lax.ppermute(sent, 'ctx', [(i, i ^ 1) for i in range(blocks)])  2.04 us
  transfers between devices with their start and end apart: 5, of which 4 were waited for; matrix products, arithmetic and copies ran while one was open for 1% of the time, Pallas kernels for 7%

profile of v3, /device:TPU:1, one launch (start us, length us, event | category | flops | bytes accessed | tf_op | source)
XLA Modules:
  0.0 81.9 jit_solution(17981487682058367342)
XLA Ops:
  0.0 8.3 %collective-permute-start = (bf16[128,512]{1,0:T(8,128)(2,1)}, bf16[128,512]{1,0:T(8,128)(2,1)S(1)}, u32[]{:S(2)}, u32[]{:S(2)}) collective-permute-start(bf16[128,512]{1,0:T(8,128)(2,1)} %hidden.1), channel_id=1, source_target_pairs={{0,1},{1,0},{2,3},{3,2},{4,5},{5,4},{6,7},{7,6},{8,9},{9,8},{10,11... | collective-permute-start | bytes 393224 | tf_op jit(solution)/shard_map/ppermute | solution.py:275
  8.3 1.8 %shard_map.82 = bf16[4,128,512]{2,1,0:T(8,128)(2,1)} custom-call(bf16[128,512]{1,0:T(8,128)(2,1)} %hidden.1), custom_call_target="tpu_custom_call" | custom-call | tf_op jit(solution)/shard_map/pallas_call | solution.py:243
  10.0 4.0 %all-to-all-start = ((bf16[4,128,512]{2,1,0:T(8,128)(2,1)}), bf16[4,128,512]{2,1,0:T(8,128)(2,1)S(1)}, u32[]{:S(2)}, u32[]{:S(2)}) async-start(bf16[4,128,512]{2,1,0:T(8,128)(2,1)} %shard_map.82), calls=%async_computation | async-start | bytes 1048576 | tf_op jit(solution)/shard_map/all_to_all | solution.py:283
  14.1 0.7 convert_element_type.3
  14.7 0.3 fusion
  15.1 0.1 pad_maximum_fusion
  15.2 1.2 %shard_map.84 = (bf16[512,256]{1,0:T(8,128)(2,1)S(1)}, bf16[2,512,128]{2,1,0:T(8,128)(2,1)S(1)}, bf16[512,128]{1,0:T(8,128)(2,1)S(1)}, s32[256,1]{1,0:T(8,128)S(...) custom-call(f32[128,128]{1,0:T(8,128)S(1)} %get-tuple-element.36.cosine, ...), custom_call_target="tpu_custom_call" | custom-call | flops 3000000000 | tf_op jit(solution)/shard_map/pallas_call | solution.py:243
  16.3 0.0 collective-permute-done.across
  16.4 0.8 %shard_map.85 = bf16[4,128,512]{2,1,0:T(8,128)(2,1)} custom-call(bf16[128,512]{1,0:T(8,128)(2,1)S(1)} %collective-permute-done.across, f32[128,128]{1,0:T(8,128)S(1)} %get-tuple-element.19.table.q_cos), custom_call_target="tpu_custom_call" | custom-call | tf_op jit(solution)/shard_map/pallas_call | solution.py:243
  17.2 4.9 %all-to-all-done.mine = bf16[4,128,512]{2,1,0:T(8,128)(2,1)S(1)} async-done(((bf16[4,128,512]{2,1,0:T(8,128)(2,1)}), bf16[4,128,512]{2,1,0:T(8,128)(2,1)S(1)}, u32[]{:S(2)}, u32[]{:S(2)}) %all-to-all-start) | async-done | bytes 524320 | tf_op jit(solution)/shard_map/all_to_all | solution.py:283
  22.0 3.5 %all-to-all-start.1 = ((bf16[4,128,512]{2,1,0:T(8,128)(2,1)}), bf16[4,128,512]{2,1,0:T(8,128)(2,1)S(1)}, u32[]{:S(2)}, u32[]{:S(2)}) async-start(bf16[4,128,512]{2,1,0:T(8,128)(2,1)} %shard_map.85), calls=%async_computation.1 | async-start | bytes 1048576 | tf_op jit(solution)/shard_map/all_to_all | solution.py:304
  25.5 1.9 %shard_map.83.first = f32[128,512]{1,0:T(8,128)S(1)} custom-call(s32[1]{0:T(128)} %bitcast.1.me_ref, bf16[4,128,512]{2,1,0:T(8,128)(2,1)S(1)} %all-to-all-done.mine, bf16[4096,256]{1,0:T(8,128)(2,1)} %wq.3, bf16[4096,128]{1,0:T(8,128)(2,1)} %wk.3, bf16[4096,128]{1,0:T(8,128)(2,1)} %wv.3), custom_call_target="tpu_custom_call" | custom-call | tf_op jit(solution)/shard_map/pallas_call | solution.py:243
  27.4 5.0 %all-to-all-done.1.other = bf16[4,128,512]{2,1,0:T(8,128)(2,1)S(1)} async-done(((bf16[4,128,512]{2,1,0:T(8,128)(2,1)}), bf16[4,128,512]{2,1,0:T(8,128)(2,1)S(1)}, u32[]{:S(2)}, u32[]{:S(2)}) %all-to-all-start.1) | async-done | bytes 524320 | tf_op jit(solution)/shard_map/all_to_all | solution.py:304
  32.4 3.6 %shard_map.86 = bf16[512,896]{1,0:T(8,128)(2,1)} custom-call(s32[1]{0:T(128)} %bitcast.1.me_ref, f32[128,512]{1,0:T(8,128)S(1)} %shard_map.83.first, bf16[4,128,512]{2,1,0:T(8,128)(2,1)S(1)} %all-to-all-done.1.other, f32[128,128]{1,0:T(8,128)S(1)} %get-tuple-element.19.table.q_cos, f32[128,128]{1,0:T(8,128)S(1)} %get-tuple-element.20.q_sin, ...), custom_call_target="tpu_custom_call" | custom-call | tf_op jit(solution)/shard_map/pallas_call | solution.py:243
  36.0 14.8 %all-to-all-start.2 = ((bf16[64,8,896]{2,1,0:T(8,128)(2,1)}), bf16[64,8,896]{2,1,0:T(8,128)(2,1)S(1)}, u32[]{:S(2)}, u32[]{:S(2)}) async-start(bf16[64,8,896]{2,1,0:T(8,128)(2,1)} %bitcast.6), calls=%async_computation.2 | async-start | bytes 1835008 | tf_op jit(solution)/shard_map/all_to_all | solution.py:321
  50.9 25.8 %all-to-all-done.2 = bf16[64,8,896]{2,1,0:T(8,128)(2,1)S(1)} async-done(((bf16[64,8,896]{2,1,0:T(8,128)(2,1)}), bf16[64,8,896]{2,1,0:T(8,128)(2,1)S(1)}, u32[]{:S(2)}, u32[]{:S(2)}) %all-to-all-start.2) | async-done | bytes 917536 | tf_op jit(solution)/shard_map/all_to_all | solution.py:321
  76.7 0.7 shard_map.87
  77.5 2.0 %collective-permute-start.1 = (bf16[512,256]{1,0:T(8,128)(2,1)S(1)}, bf16[512,256]{1,0:T(8,128)(2,1)S(1)}, u32[]{:S(2)}, u32[]{:S(2)}) collective-permute-start(bf16[512,256]{1,0:T(8,128)(2,1)S(1)} %get-tuple-element.29), channel_id=1, source_target_pairs={{0,8},{8,0},{16,24},{24,16},{32,40},{40,32},{48,56},{56,48},{64,72... | collective-permute-start | bytes 786440 | tf_op jit(solution)/shard_map/ppermute | solution.py:337
  79.5 0.4 shard_map.88
  79.9 0.9 %collective-permute-done.1.keyvalues = bf16[512,256]{1,0:T(8,128)(2,1)S(1)} collective-permute-done((bf16[512,256]{1,0:T(8,128)(2,1)S(1)}, bf16[512,256]{1,0:T(8,128)(2,1)S(1)}, u32[]{:S(2)}, u32[]{:S(2)}) %collective-permute-start.1) | collective-permute-done | bytes 262176 | tf_op jit(solution)/shard_map/ppermute | solution.py:337
  80.9 1.0 %shard_map.89 = bf16[128,256]{1,0:T(8,128)(2,1)} custom-call(bf16[256,128]{1,0:T(8,128)(2,1)S(1)} %get-tuple-element.26.queries, s32[256,1]{1,0:T(8,128)S(1)} %get-tuple-element.27.query_docs, s32[16,128]{1,0:T(8,128)S(1)} %get-tuple-element.28.key_docs, bf16[512,256]{1,0:T(8,128)(2,1)S(1)} %collective-permute-done.1.keyvalues, ...), custom_call_target="tpu_custom_call" | custom-call | tf_op jit(solution)/shard_map/pallas_call | solution.py:243
  (1 shorter events, 0.0 us)
Async XLA Ops:
  0.0 16.3 %collective-permute-start = (bf16[128,512]{1,0:T(8,128)(2,1)}, bf16[128,512]{1,0:T(8,128)(2,1)S(1)}, u32[]{:S(2)}, u32[]{:S(2)}) collective-permute-start(bf16[128,512]{1,0:T(8,128)(2,1)} %hidden.1), channel_id=1, source_target_pairs={{0,1},{1,0},{2,3},{3,2},{4,5},{5,4},{6,7},{7,6},{8,9},{9,8},{10,11... | collective-permute-start | bytes 393224 | tf_op jit(solution)/shard_map/ppermute | solution.py:275
  10.0 12.0 %all-to-all-start = ((bf16[4,128,512]{2,1,0:T(8,128)(2,1)}), bf16[4,128,512]{2,1,0:T(8,128)(2,1)S(1)}, u32[]{:S(2)}, u32[]{:S(2)}) async-start(bf16[4,128,512]{2,1,0:T(8,128)(2,1)} %shard_map.82), calls=%async_computation | async-start | bytes 1048576 | tf_op jit(solution)/shard_map/all_to_all | solution.py:283
  22.0 10.4 %all-to-all-start.1 = ((bf16[4,128,512]{2,1,0:T(8,128)(2,1)}), bf16[4,128,512]{2,1,0:T(8,128)(2,1)S(1)}, u32[]{:S(2)}, u32[]{:S(2)}) async-start(bf16[4,128,512]{2,1,0:T(8,128)(2,1)} %shard_map.85), calls=%async_computation.1 | async-start | bytes 1048576 | tf_op jit(solution)/shard_map/all_to_all | solution.py:304
  36.0 40.7 %all-to-all-start.2 = ((bf16[64,8,896]{2,1,0:T(8,128)(2,1)}), bf16[64,8,896]{2,1,0:T(8,128)(2,1)S(1)}, u32[]{:S(2)}, u32[]{:S(2)}) async-start(bf16[64,8,896]{2,1,0:T(8,128)(2,1)} %bitcast.6), calls=%async_computation.2 | async-start | bytes 1835008 | tf_op jit(solution)/shard_map/all_to_all | solution.py:321
  77.5 3.4 %collective-permute-start.1 = (bf16[512,256]{1,0:T(8,128)(2,1)S(1)}, bf16[512,256]{1,0:T(8,128)(2,1)S(1)}, u32[]{:S(2)}, u32[]{:S(2)}) collective-permute-start(bf16[512,256]{1,0:T(8,128)(2,1)S(1)} %get-tuple-element.29), channel_id=1, source_target_pairs={{0,8},{8,0},{16,24},{24,16},{32,40},{40,32},{48,56},{56,48},{64,72... | collective-permute-start | bytes 786440 | tf_op jit(solution)/shard_map/ppermute | solution.py:337

commit v4 on v3

--- a/solution.py
+++ b/solution.py
@@ -41,24 +41,16 @@
         copy.wait()
 
 
-def spread_own_kernel(hidden, spread, sems):
-    fetch([(hidden, spread.at[0])], sems)
-    for i in range(1, spread.shape[0]):
-        spread[i] = spread[0]
-
-
-def spread_kernel(across, table, spread):
+def spread_own_kernel(hidden, spread):
     for i in range(spread.shape[0]):
-        spread[i] = across[...]
+        spread[i] = hidden[...]
 
 
 def tables_kernel(
-    cosine, sine, destination, doc_ids, q_gain, k_gain,
-    own, later, notes, query_docs, q_cos, q_sin, k_cos, k_sin,
-    place_ref, docs_ref, q_ref, k_ref, sems,
+    destination, doc_ids, q_gain, k_gain, picks, notes, gains, place_ref, docs_ref, sems
 ):
-    small = [(destination, place_ref), (doc_ids, docs_ref), (q_gain, q_ref), (k_gain, k_ref)]
-    fetch(small, sems)
+    gain_rows = [(g, gains.at[i : i + 1]) for i, g in enumerate((q_gain, k_gain))]
+    fetch([(destination, place_ref), (doc_ids, docs_ref)] + gain_rows, sems)
     place, docs = place_ref[...], docs_ref[...]
     rows = place.shape[1]
     target, inside = lax.div(place, rows), lax.rem(place, rows)
@@ -67,8 +59,8 @@
     order = jnp.sum(jnp.where(earlier, 1, 0), 0, keepdims=True)
     slot = (target * SLOTS + order).reshape(1, 1, rows)
     label = column(inside) + 1
-    shape = (own.shape[0] // LINES, LINES, rows)
-    flat = (own.shape[0], rows)
+    shape = (notes.shape[0] // LINES, LINES, rows)
+    flat = notes.shape
     block, line = iota(shape, 0), iota(shape, 1)
     noted = jnp.zeros(flat, F32)
     for g in range(PAIRS):
@@ -76,11 +68,7 @@
         at = jnp.where(line < SLOTS, line, line - SLOTS)
         found = (block - back) * SLOTS + at == slot
         picked = jnp.where(found, 1.0, 0.0).reshape(flat).astype(BF16)
-        if g == 0:
-            own[:, :rows] = jnp.where(found & (line < SLOTS), 1.0, 0.0).reshape(flat).astype(BF16)
-            own[:, rows:] = jnp.where(found & (line >= SLOTS), 1.0, 0.0).reshape(flat).astype(BF16)
-        else:
-            later[g - 1] = picked
+        picks[g] = picked
         lane = jnp.where(iota(square, 1) == g, label, 0).astype(F32).astype(BF16)
         noted += jnp.dot(picked, lane, preferred_element_type=F32)
     kept = docs.astype(F32)
@@ -89,76 +77,90 @@
         jnp.where(line == h, half.reshape(1, 1, rows), 0.0) for h, half in enumerate(halves)
     )
     notes[...] = (noted + doc_lines.reshape(flat)).astype(BF16)
-    docs_col = column(docs)
-    for h in range(query_docs.shape[0] // rows):
-        query_docs[h * rows : (h + 1) * rows, :] = docs_col
-    c, s = cosine[...], sine[...]
-    half = c.shape[1] // 2
-    for gain, scale, turn_cos, turn_sin in (
-        (q_ref[...], c.shape[1] ** (-0.5), q_cos, q_sin),
-        (k_ref[...], 1.0, k_cos, k_sin),
-    ):
-        turn_cos[...] = c * (gain * scale)
-        turn_sin[...] = s * (jnp.concatenate([gain[:, half:], gain[:, :half]], 1) * scale)
-
-
-def partial_projection(pieces, side, weights, held, sems):
-    width = pieces[0].shape[1]
-    steps = []
-    for k in range(len(pieces)):
-        span = pl.ds(pl.multiple_of((2 * k + side) * width, width), width)
-        steps.append(
+
+
+def weight_copies(weights, held, sems, owners):
+    width = held[0].shape[1]
+    copies = []
+    for k, owner in enumerate(owners):
+        span = pl.ds(pl.multiple_of(owner * width, width), width)
+        copies.append(
             [
                 pltpu.make_async_copy(w.at[span, :], to.at[k], sems.at[k, i])
                 for i, (w, to) in enumerate(zip(weights, held))
             ]
         )
-        for copy in steps[-1]:
+        for copy in copies[-1]:
             copy.start()
-    total = jnp.zeros((pieces[0].shape[0], sum(w.shape[1] for w in weights)), F32)
-    for k, (piece, copies) in enumerate(zip(pieces, steps)):
+    return copies
+
+
+def project_first_kernel(me_ref, mine, wq, wk, wv, first, *room):
+    held, sems = room[:-1], room[-1]
+    total = 0.0
+    side = lax.rem(me_ref[0], 2)
+    owners = [2 * k + side for k in range(mine.shape[0])]
+    for k, copies in enumerate(weight_copies((wq, wk, wv), held, sems, owners)):
         for copy in copies:
             copy.wait()
         block = jnp.concatenate([to[k] for to in held], 1)
+        total = total + jnp.dot(mine[k], block, preferred_element_type=F32)
+    first[...] = total
+
+
+def ahead_kernel(shifts, me_ref, first, wq, wk, wv, *refs):
+    held, sems = refs[:-1], refs[-1]
+    groups = wq.shape[0] // held[0].shape[1]
+    partner = me_ref[0] + 1 - 2 * lax.rem(me_ref[0], 2)
+    owners = [lax.rem(partner + groups - 2 * d, groups) for d in shifts]
+    for copies in weight_copies((wq, wk, wv), held, sems, owners):
+        for copy in copies:
+            copy.wait()
+
+
+def project_kernel(
+    first, cosine, sine, gains, picks, notes, wq, wk, wv, *refs
+):
+    other, out = refs[:-1], refs[-1]
+    total = first[...]
+    for k, piece in enumerate(other):
+        block = jnp.concatenate([w[k] for w in (wq, wk, wv)], 1)
         total = total + jnp.dot(piece[...], block, preferred_element_type=F32)
-    return total
-
-
-def project_first_kernel(me_ref, mine, wq, wk, wv, first, *room):
-    pieces = [mine.at[k] for k in range(mine.shape[0])]
-    side = lax.rem(me_ref[0], 2)
-    first[...] = partial_projection(pieces, side, (wq, wk, wv), room[:-1], room[-1])
-
-
-def project_kernel(
-    me_ref, first, other, q_cos, q_sin, k_cos, k_sin, own, later, notes, wq, wk, wv,
-    out, *room,
-):
-    pieces = [other.at[k] for k in range(other.shape[0])]
-    side = 1 - lax.rem(me_ref[0], 2)
-    total = first[...] + partial_projection(pieces, side, (wq, wk, wv), room[:-1], room[-1])
-    head_dim = q_cos.shape[1]
+    head_dim = cosine.shape[1]
+    c, s = cosine[...], sine[...]
+    half = head_dim // 2
+    turns = []
+    for i, scale in enumerate((head_dim ** (-0.5), 1.0)):
+        gain = gains[i : i + 1, :] * scale
+        turns.append((c * gain, s * jnp.concatenate([gain[:, half:], gain[:, :half]], 1)))
+    (q_cos, q_sin), (k_cos, k_sin) = turns
 
     def turned(raw, turn_cos, turn_sin):
         scale = lax.rsqrt(jnp.mean(raw * raw, -1, keepdims=True) + 1e-06)
         return (
-            (raw * turn_cos[...] + pltpu.roll(raw, head_dim // 2, 1) * turn_sin[...]) * scale
+            (raw * turn_cos + pltpu.roll(raw, half, 1) * turn_sin) * scale
         ).astype(BF16)
 
     heads = [total[:, h : h + head_dim] for h in range(0, total.shape[1], head_dim)]
     top = jnp.concatenate([turned(h, q_cos, q_sin) for h in heads[:-2]], 1)
     low = jnp.concatenate([turned(heads[-2], k_cos, k_sin), heads[-1].astype(BF16)], 1)
-    both = jnp.concatenate([top, low], 0)
     width = low.shape[1]
+    first_half = lax.rem(iota(picks.shape[1:], 0), LINES) < SLOTS
     for g in range(PAIRS):
-        picked, lines = (own[...], both) if g == 0 else (later[g - 1], low)
+        picked, lines = picks[g], low
+        if g == 0:
+            zero = jnp.zeros_like(picked)
+            parts = [jnp.where(first_half, picked, zero), jnp.where(first_half, zero, picked)]
+            picked, lines = jnp.concatenate(parts, 1), jnp.concatenate([top, low], 0)
         out[:, g * width : (g + 1) * width] = jnp.dot(
             picked, lines, preferred_element_type=F32
         ).astype(BF16)
     out[:, PAIRS * width :] = notes[...]
 
 
-def land_kernel(me_ref, arrived, queries, keyvalues, sent, key_docs, doc_lines):
+def land_kernel(
+    me_ref, arrived, queries, keyvalues, sent, key_docs, query_docs, doc_lines
+):
     me = me_ref[0]
     rows = key_docs.shape[1]
     width = keyvalues.shape[1]
@@ -192,6 +194,10 @@
         lines = doc_lines[pl.ds(owner, LINES), :]
         docs = jnp.concatenate([lines[h : h + 1, NOTED:] for h in range(rows // NOTED)], 1)
         key_docs[back : back + 1, :] = jnp.where(me >= back, docs.astype(I32), -1)
+        if back == 0:
+            own_docs = column(docs)
+            for h in range(queries.shape[0] // rows):
+                query_docs[h * rows : (h + 1) * rows, :] = own_docs.astype(I32)
     key_docs[SPAN + 1 :, :] = jnp.full((key_docs.shape[0] - SPAN - 1, rows), -1, I32)
 
 
@@ -229,7 +235,7 @@
         out[:, h * head_dim : (h + 1) * head_dim] = result[h * rows : (h + 1) * rows, :]
 
 
-TABLES_COST = 3 * 10**9
+TABLES_COST = 2 * 10**10
 VMEM = pl.BlockSpec(memory_space=pltpu.VMEM)
 SMEM = pl.BlockSpec(memory_space=pltpu.SMEM)
 HBM = pl.BlockSpec(memory_space=pltpu.HBM)
@@ -276,59 +282,55 @@
     (spread,) = call(
         spread_own_kernel,
         [((members, rows, width), BF16)],
-        [],
         [hidden],
-        scratch=[pltpu.SemaphoreType.DMA((1,))],
     )
     mine = lax.all_to_all(spread, "kvh", 0, 0, tiled=True, axis_index_groups=along_x)
     cosine, sine = rotation(destination, head_dim)
     lines = blocks * LINES
-    own, later, notes, query_docs, q_cos, q_sin, k_cos, k_sin = call(
+    picks, notes, gains = call(
         tables_kernel,
-        [
-            ((lines, 2 * rows), BF16),
-            ((PAIRS - 1, lines, rows), BF16),
-            ((lines, rows), BF16),
-            ((q_rows, 1), I32),
-        ]
-        + [((rows, head_dim), F32)] * 4,
-        [cosine, sine],
+        [((PAIRS, lines, rows), BF16), ((lines, rows), BF16), ((2, head_dim), F32)],
+        [],
         [destination.reshape(1, -1), doc_ids.reshape(1, -1)]
         + [q_gain.reshape(1, -1), k_gain.reshape(1, -1)],
-        scratch=[pltpu.VMEM((1, rows), I32)] * 2
-        + [pltpu.VMEM((1, head_dim), F32)] * 2
-        + [pltpu.SemaphoreType.DMA((4,))],
+        scratch=[pltpu.VMEM((1, rows), I32)] * 2 + [pltpu.SemaphoreType.DMA((4,))],
         cost=TABLES_COST,
     )
-    (spread,) = call(spread_kernel, [((members, rows, width), BF16)], [across, q_cos])
-    other = lax.all_to_all(spread, "kvh", 0, 0, tiled=True, axis_index_groups=along_x)
+    shifts = (0, 1, 3, 2)
+    other = [across] + [
+        lax.ppermute(across, "kvh", [(i, (i + 2 * d) % n) for i in range(n)]) for d in shifts[1:]
+    ]
 
     columns = PAIRS * 2 * head_dim + rows
     weights = [w_query, w_key, w_value]
     all_heads = q_width + 2 * head_dim
-    room = [pltpu.VMEM((members, width, w.shape[1]), BF16) for w in weights]
-    room.append(pltpu.SemaphoreType.DMA((members, len(weights))))
+    held = [((members, width, w.shape[1]), BF16) for w in weights]
+    sems = pltpu.SemaphoreType.DMA((members, len(weights)))
     (first,) = call(
-        project_first_kernel, [((rows, all_heads), F32)], [me_kvh, mine], weights, scratch=room
-    )
+        project_first_kernel,
+        [((rows, all_heads), F32)],
+        [me_kvh, mine],
+        weights,
+        scratch=[pltpu.VMEM(*h) for h in held] + [sems],
+    )
+    ahead = call(functools.partial(ahead_kernel, shifts), held, [me_kvh, first], weights, scratch=[sems])
     (parcel,) = call(
         project_kernel,
         [((lines, columns), BF16)],
-        [me_kvh, first, other, q_cos, q_sin, k_cos, k_sin, own, later, notes],
-        weights,
-        scratch=room,
+        [first, cosine, sine, gains, picks, notes, *ahead, *other],
     )
     arrived = lax.all_to_all(
         parcel.reshape(blocks, LINES, columns), "ctx", split_axis=0, concat_axis=0, tiled=True
     ).reshape(lines, columns)
     held = SPAN // 2 + 1
-    queries, keyvalues, sent, key_docs = call(
+    queries, keyvalues, sent, key_docs, query_docs = call(
         land_kernel,
         [
             ((q_rows, head_dim), BF16),
             ((held * rows, 2 * head_dim), BF16),
             (((held - 1) * rows, 2 * head_dim), BF16),
             ((16, rows), I32),
+            ((q_rows, 1), I32),
         ],
         [me_ctx, arrived],
         scratch=[pltpu.VMEM((lines, rows), F32)],

time: 82.3 us -> 79 us (0.960)
  waiting for transfers between devices: 36.7 us -> 27.2 us
  starting transfers between devices: 32.6 us -> 39.8 us
  Pallas kernels: 11.4 us -> 10 us
  local copies, waits for them, and re-layouts: 0 us -> 0.91 us
    ppermute x0 -> x3, starting transfers between devices: none -> 10.2 us  [body(): lax.ppermute(across, 'kvh', [(i, (i + 2 * d) % n) for i in range(n)])]
    all_to_all x2 -> x1, waiting for transfers between devices: 9.87 us -> 0.01 us  [body(): lax.all_to_all(spread, 'kvh', 0, 0, tiled=True, axis_index_groups=along_x)]
    all_to_all x2 -> x1, starting transfers between devices: 7.49 us -> 4.01 us  [body(): lax.all_to_all(spread, 'kvh', 0, 0, tiled=True, axis_index_groups=along_x)]
    pallas_call x8, Pallas kernels: 11.4 us -> 10 us  [call(): pl.pallas_call(kernel, out_shape=shapes, in_specs=[SMEM if x.shape == (1,...]
    unnamed x0 -> x4, local copies, waits for them, and re-layouts: none -> 0.91 us
  transfers between devices with their start and end apart: 5 -> 7, of which waited for: 4 -> 3; matrix products, arithmetic and copies ran while one was open for 1% -> 1% of each run, Pallas kernels for 7% -> 8%
where the time goes in v4:
time: 79 us; the launch traced here: 78.5 us
  starting transfers between devices  39.8 us (50%)
  waiting for transfers between devices  27.2 us (34%)
  Pallas kernels  10 us (13%)
  local copies, waits for them, and re-layouts  0.91 us (1%)
    all_to_all x1, waiting for transfers between devices, body(): lax.all_to_all(parcel.reshape(blocks, LINES, columns), 'ctx', split_axis=...  25.8 us
    all_to_all x1, starting transfers between devices, body(): lax.all_to_all(parcel.reshape(blocks, LINES, columns), 'ctx', split_axis=...  15.3 us
    ppermute x3, starting transfers between devices, body(): lax.ppermute(across, 'kvh', [(i, (i + 2 * d) % n) for i in range(n)])  10.2 us
    pallas_call x8, Pallas kernels, call(): pl.pallas_call(kernel, out_shape=shapes, in_specs=[SMEM if x.shape == (1,...  10 us
    ppermute x1, starting transfers between devices, body(): across = lax.ppermute(hidden, 'kvh', [(i, i ^ 1) for i in range(n)])  8.27 us
    all_to_all x1, starting transfers between devices, body(): lax.all_to_all(spread, 'kvh', 0, 0, tiled=True, axis_index_groups=along_x)  4.01 us
    ppermute x1, starting transfers between devices, body(): swapped = lax.ppermute(sent, 'ctx', [(i, i ^ 1) for i in range(blocks)])  2.01 us
  transfers between devices with their start and end apart: 7, of which 3 were waited for; matrix products, arithmetic and copies ran while one was open for 1% of the time, Pallas kernels for 8%

profile of v4, /device:TPU:1, one launch (start us, length us, event | category | flops | bytes accessed | tf_op | source)
XLA Modules:
  0.0 78.5 jit_solution(3857973160997780728)
XLA Ops:
  0.0 8.3 %collective-permute-start = (bf16[128,512]{1,0:T(8,128)(2,1)}, bf16[128,512]{1,0:T(8,128)(2,1)S(1)}, u32[]{:S(2)}, u32[]{:S(2)}) collective-permute-start(bf16[128,512]{1,0:T(8,128)(2,1)} %hidden.1), channel_id=1, source_target_pairs={{0,1},{1,0},{2,3},{3,2},{4,5},{5,4},{6,7},{7,6},{8,9},{9,8},{10,11... | collective-permute-start | bytes 393224 | tf_op jit(solution)/shard_map/ppermute | solution.py:281
  8.3 0.0 copy-start
  8.3 0.9 %copy-done = bf16[128,512]{1,0:T(8,128)(2,1)S(1)} copy-done((bf16[128,512]{1,0:T(8,128)(2,1)S(1)}, bf16[128,512]{1,0:T(8,128)(2,1)}, u32[]{:S(2)}) %copy-start) | copy-done | bytes 131096
  9.2 0.8 %shard_map.82 = bf16[4,128,512]{2,1,0:T(8,128)(2,1)} custom-call(bf16[128,512]{1,0:T(8,128)(2,1)S(1)} %copy-done), custom_call_target="tpu_custom_call" | custom-call | tf_op jit(solution)/shard_map/pallas_call | solution.py:249
  10.0 4.0 %all-to-all-start = ((bf16[4,128,512]{2,1,0:T(8,128)(2,1)}), bf16[4,128,512]{2,1,0:T(8,128)(2,1)S(1)}, u32[]{:S(2)}, u32[]{:S(2)}) async-start(bf16[4,128,512]{2,1,0:T(8,128)(2,1)} %shard_map.82), calls=%async_computation | async-start | bytes 1048576 | tf_op jit(solution)/shard_map/all_to_all | solution.py:287
  14.0 0.0 copy-start.1
  14.0 1.2 %shard_map.84 = (bf16[3,512,128]{2,1,0:T(8,128)(2,1)S(1)}, bf16[512,128]{1,0:T(8,128)(2,1)S(1)}, f32[2,128]{1,0:T(2,128)S(1)}) custom-call(s32[1,128]{1,0:T(1,128)} %bitcast.12, s32[1,128]{1,0:T(1,128)} %bitcast.9, f32[1,128]{1,0:T(1,128)} %bitcast.10, f32[1,128]{1,0:T(1,128)} %bitcast.11), custom_call_target="tpu_custom_call" | custom-call | flops 20000000000 | tf_op jit(solution)/shard_map/pallas_call | solution.py:249
  15.2 0.0 copy-done.1
  15.3 0.0 collective-permute-done.refs_0_
  15.3 4.9 %collective-permute-start.3 = (bf16[128,512]{1,0:T(8,128)(2,1)S(1)}, bf16[128,512]{1,0:T(8,128)(2,1)S(1)}, u32[]{:S(2)}, u32[]{:S(2)}) collective-permute-start(bf16[128,512]{1,0:T(8,128)(2,1)S(1)} %collective-permute-done.refs_0_), channel_id=1, source_target_pairs={{0,4},{1,5},{2,6},{3,7},{4,0},{5,1},{6,2},{7,3},{8,12},{9,13},{10,... | collective-permute-start | bytes 393224 | tf_op jit(solution)/shard_map/ppermute | solution.py:301
  20.2 2.8 %collective-permute-start.2 = (bf16[128,512]{1,0:T(8,128)(2,1)S(1)}, bf16[128,512]{1,0:T(8,128)(2,1)S(1)}, u32[]{:S(2)}, u32[]{:S(2)}) collective-permute-start(bf16[128,512]{1,0:T(8,128)(2,1)S(1)} %collective-permute-done.refs_0_), channel_id=1, source_target_pairs={{0,6},{1,7},{2,0},{3,1},{4,2},{5,3},{6,4},{7,5},{8,14},{9,15},{10,... | collective-permute-start | bytes 393224 | tf_op jit(solution)/shard_map/ppermute | solution.py:301
  23.0 2.5 %collective-permute-start.1 = (bf16[128,512]{1,0:T(8,128)(2,1)S(1)}, bf16[128,512]{1,0:T(8,128)(2,1)S(1)}, u32[]{:S(2)}, u32[]{:S(2)}) collective-permute-start(bf16[128,512]{1,0:T(8,128)(2,1)S(1)} %collective-permute-done.refs_0_), channel_id=1, source_target_pairs={{0,2},{1,3},{2,4},{3,5},{4,6},{5,7},{6,0},{7,1},{8,10},{9,11},{10,... | collective-permute-start | bytes 393224 | tf_op jit(solution)/shard_map/ppermute | solution.py:301
  25.5 0.3 fusion
  25.8 0.1 pad_maximum_fusion
  25.9 0.0 all-to-all-done.mine
  25.9 1.9 %shard_map.83.first = f32[128,512]{1,0:T(8,128)S(1)} custom-call(s32[1]{0:T(128)} %bitcast.1.me_ref, bf16[4,128,512]{2,1,0:T(8,128)(2,1)S(1)} %all-to-all-done.mine, bf16[4096,256]{1,0:T(8,128)(2,1)} %wq.3, bf16[4096,128]{1,0:T(8,128)(2,1)} %wk.3, bf16[4096,128]{1,0:T(8,128)(2,1)} %wv.3), custom_call_target="tpu_custom_call" | custom-call | tf_op jit(solution)/shard_map/pallas_call | solution.py:249
  27.8 1.7 %shard_map.85 = (bf16[4,512,256]{2,1,0:T(8,128)(2,1)S(1)}, bf16[4,512,128]{2,1,0:T(8,128)(2,1)S(1)}, bf16[4,512,128]{2,1,0:T(8,128)(2,1)S(1)}) custom-call(s32[1]{0:T(128)} %bitcast.1.me_ref, f32[128,512]{1,0:T(8,128)S(1)} %shard_map.83.first, bf16[4096,256]{1,0:T(8,128)(2,1)} %wq.3, bf16[4096,128]{1,0:T(8,128)(2,1)} %wk.3, bf16[4096,128]{1,0:T(8,128)(2,1)} %wv.3), custom_call_target="tpu_custom_call" | custom-call | tf_op jit(solution)/shard_map/pallas_call | solution.py:249
  29.5 0.0 collective-permute-done.3.refs_3_
  29.5 0.0 collective-permute-done.2.refs_2_
  29.5 0.4 collective-permute-done.1.refs_1_
  29.9 2.2 %shard_map.86 = bf16[512,896]{1,0:T(8,128)(2,1)} custom-call(f32[128,512]{1,0:T(8,128)S(1)} %shard_map.83.first, f32[128,128]{1,0:T(8,128)S(1)} %get-tuple-element.34.cosine, f32[128,128]{1,0:T(8,128)S(1)} %get-tuple-element.35.sine, f32[2,128]{1,0:T(2,128)S(1)} %get-tuple-element.18.gains, bf16[3,512,128]{2,1,0:T(8,128)(2,1)S(1)} %get-tuple-element.19.picks, ...), custom_call_target="tpu_custom_call" | custom-call | tf_op jit(solution)/shard_map/pallas_call | solution.py:249
  32.1 15.3 %all-to-all-start.1 = ((bf16[64,8,896]{2,1,0:T(8,128)(2,1)}), bf16[64,8,896]{2,1,0:T(8,128)(2,1)S(1)}, u32[]{:S(2)}, u32[]{:S(2)}) async-start(bf16[64,8,896]{2,1,0:T(8,128)(2,1)} %bitcast.6), calls=%async_computation.1 | async-start | bytes 1835008 | tf_op jit(solution)/shard_map/all_to_all | solution.py:322
  47.4 25.8 %all-to-all-done.1 = bf16[64,8,896]{2,1,0:T(8,128)(2,1)S(1)} async-done(((bf16[64,8,896]{2,1,0:T(8,128)(2,1)}), bf16[64,8,896]{2,1,0:T(8,128)(2,1)S(1)}, u32[]{:S(2)}, u32[]{:S(2)}) %all-to-all-start.1) | async-done | bytes 917536 | tf_op jit(solution)/shard_map/all_to_all | solution.py:322
  73.3 0.8 %shard_map.87 = (bf16[256,128]{1,0:T(8,128)(2,1)S(1)}, bf16[640,256]{1,0:T(8,128)(2,1)S(1)}, bf16[512,256]{1,0:T(8,128)(2,1)S(1)}, s32[16,128]{1,0:T(8,128)S(1)}, s32[256,1]{1,0:T(8,128)S(1)}) custom-call(s32[1]{0:T(128)} %bitcast.me_ref, bf16[512,896]{1,0:T(8,128)(2,1)S(1)} %bitcast.8), custom_call_target="tpu_custom_call" | custom-call | tf_op jit(solution)/shard_map/pallas_call | solution.py:249
  74.1 2.0 %collective-permute-start.4 = (bf16[512,256]{1,0:T(8,128)(2,1)S(1)}, bf16[512,256]{1,0:T(8,128)(2,1)S(1)}, u32[]{:S(2)}, u32[]{:S(2)}) collective-permute-start(bf16[512,256]{1,0:T(8,128)(2,1)S(1)} %get-tuple-element.27), channel_id=1, source_target_pairs={{0,8},{8,0},{16,24},{24,16},{32,40},{40,32},{48,56},{56,48},{64,72... | collective-permute-start | bytes 786440 | tf_op jit(solution)/shard_map/ppermute | solution.py:339
  76.1 0.4 shard_map.88
  76.5 1.0 %collective-permute-done.4.keyvalues = bf16[512,256]{1,0:T(8,128)(2,1)S(1)} collective-permute-done((bf16[512,256]{1,0:T(8,128)(2,1)S(1)}, bf16[512,256]{1,0:T(8,128)(2,1)S(1)}, u32[]{:S(2)}, u32[]{:S(2)}) %collective-permute-start.4) | collective-permute-done | bytes 262176 | tf_op jit(solution)/shard_map/ppermute | solution.py:339
  77.5 1.0 %shard_map.89 = bf16[128,256]{1,0:T(8,128)(2,1)} custom-call(bf16[256,128]{1,0:T(8,128)(2,1)S(1)} %get-tuple-element.24.queries, s32[256,1]{1,0:T(8,128)S(1)} %get-tuple-element.25.query_docs, s32[16,128]{1,0:T(8,128)S(1)} %get-tuple-element.26.key_docs, bf16[512,256]{1,0:T(8,128)(2,1)S(1)} %collective-permute-done.4.keyvalues, ...), custom_call_target="tpu_custom_call" | custom-call | tf_op jit(solution)/shard_map/pallas_call | solution.py:249
  (2 shorter events, 0.0 us)
Async XLA Ops:
  0.0 15.3 %collective-permute-start = (bf16[128,512]{1,0:T(8,128)(2,1)}, bf16[128,512]{1,0:T(8,128)(2,1)S(1)}, u32[]{:S(2)}, u32[]{:S(2)}) collective-permute-start(bf16[128,512]{1,0:T(8,128)(2,1)} %hidden.1), channel_id=1, source_target_pairs={{0,1},{1,0},{2,3},{3,2},{4,5},{5,4},{6,7},{7,6},{8,9},{9,8},{10,11... | collective-permute-start | bytes 393224 | tf_op jit(solution)/shard_map/ppermute | solution.py:281
  8.3 0.9 %copy-start = (bf16[128,512]{1,0:T(8,128)(2,1)S(1)}, bf16[128,512]{1,0:T(8,128)(2,1)}, u32[]{:S(2)}) copy-start(bf16[128,512]{1,0:T(8,128)(2,1)} %hidden.1) | copy-start | bytes 393220
  10.0 15.9 %all-to-all-start = ((bf16[4,128,512]{2,1,0:T(8,128)(2,1)}), bf16[4,128,512]{2,1,0:T(8,128)(2,1)S(1)}, u32[]{:S(2)}, u32[]{:S(2)}) async-start(bf16[4,128,512]{2,1,0:T(8,128)(2,1)} %shard_map.82), calls=%async_computation | async-start | bytes 1048576 | tf_op jit(solution)/shard_map/all_to_all | solution.py:287
  14.0 1.2 %copy-start.1 = (s32[128]{0:T(128)S(1)}, s32[128]{0:T(128)}, u32[]{:S(2)}) copy-start(s32[128]{0:T(128)} %param.9) | copy-start | bytes 1540
  15.3 14.2 %collective-permute-start.3 = (bf16[128,512]{1,0:T(8,128)(2,1)S(1)}, bf16[128,512]{1,0:T(8,128)(2,1)S(1)}, u32[]{:S(2)}, u32[]{:S(2)}) collective-permute-start(bf16[128,512]{1,0:T(8,128)(2,1)S(1)} %collective-permute-done.refs_0_), channel_id=1, source_target_pairs={{0,4},{1,5},{2,6},{3,7},{4,0},{5,1},{6,2},{7,3},{8,12},{9,13},{10,... | collective-permute-start | bytes 393224 | tf_op jit(solution)/shard_map/ppermute | solution.py:301
  20.2 9.3 %collective-permute-start.2 = (bf16[128,512]{1,0:T(8,128)(2,1)S(1)}, bf16[128,512]{1,0:T(8,128)(2,1)S(1)}, u32[]{:S(2)}, u32[]{:S(2)}) collective-permute-start(bf16[128,512]{1,0:T(8,128)(2,1)S(1)} %collective-permute-done.refs_0_), channel_id=1, source_target_pairs={{0,6},{1,7},{2,0},{3,1},{4,2},{5,3},{6,4},{7,5},{8,14},{9,15},{10,... | collective-permute-start | bytes 393224 | tf_op jit(solution)/shard_map/ppermute | solution.py:301
  23.0 6.9 %collective-permute-start.1 = (bf16[128,512]{1,0:T(8,128)(2,1)S(1)}, bf16[128,512]{1,0:T(8,128)(2,1)S(1)}, u32[]{:S(2)}, u32[]{:S(2)}) collective-permute-start(bf16[128,512]{1,0:T(8,128)(2,1)S(1)} %collective-permute-done.refs_0_), channel_id=1, source_target_pairs={{0,2},{1,3},{2,4},{3,5},{4,6},{5,7},{6,0},{7,1},{8,10},{9,11},{10,... | collective-permute-start | bytes 393224 | tf_op jit(solution)/shard_map/ppermute | solution.py:301
  32.1 41.2 %all-to-all-start.1 = ((bf16[64,8,896]{2,1,0:T(8,128)(2,1)}), bf16[64,8,896]{2,1,0:T(8,128)(2,1)S(1)}, u32[]{:S(2)}, u32[]{:S(2)}) async-start(bf16[64,8,896]{2,1,0:T(8,128)(2,1)} %bitcast.6), calls=%async_computation.1 | async-start | bytes 1835008 | tf_op jit(solution)/shard_map/all_to_all | solution.py:322
  74.1 3.4 %collective-permute-start.4 = (bf16[512,256]{1,0:T(8,128)(2,1)S(1)}, bf16[512,256]{1,0:T(8,128)(2,1)S(1)}, u32[]{:S(2)}, u32[]{:S(2)}) collective-permute-start(bf16[512,256]{1,0:T(8,128)(2,1)S(1)} %get-tuple-element.27), channel_id=1, source_target_pairs={{0,8},{8,0},{16,24},{24,16},{32,40},{40,32},{48,56},{56,48},{64,72... | collective-permute-start | bytes 786440 | tf_op jit(solution)/shard_map/ppermute | solution.py:339

commit v5 on v4

--- a/solution.py
+++ b/solution.py
@@ -121,7 +121,11 @@
 def project_kernel(
     first, cosine, sine, gains, picks, notes, wq, wk, wv, *refs
 ):
-    other, out = refs[:-1], refs[-1]
+    other, (out, held, sems) = refs[:-3], refs[-3:]
+    width = held.shape[2]
+    kept = out.at[:, PAIRS * width :]
+    copies = [pltpu.make_async_copy(notes, kept, sems.at[PAIRS])]
+    copies[0].start()
     total = first[...]
     for k, piece in enumerate(other):
         block = jnp.concatenate([w[k] for w in (wq, wk, wv)], 1)
@@ -144,7 +148,6 @@
     heads = [total[:, h : h + head_dim] for h in range(0, total.shape[1], head_dim)]
     top = jnp.concatenate([turned(h, q_cos, q_sin) for h in heads[:-2]], 1)
     low = jnp.concatenate([turned(heads[-2], k_cos, k_sin), heads[-1].astype(BF16)], 1)
-    width = low.shape[1]
     first_half = lax.rem(iota(picks.shape[1:], 0), LINES) < SLOTS
     for g in range(PAIRS):
         picked, lines = picks[g], low
@@ -152,10 +155,12 @@
             zero = jnp.zeros_like(picked)
             parts = [jnp.where(first_half, picked, zero), jnp.where(first_half, zero, picked)]
             picked, lines = jnp.concatenate(parts, 1), jnp.concatenate([top, low], 0)
-        out[:, g * width : (g + 1) * width] = jnp.dot(
-            picked, lines, preferred_element_type=F32
-        ).astype(BF16)
-    out[:, PAIRS * width :] = notes[...]
+        held[g] = jnp.dot(picked, lines, preferred_element_type=F32).astype(BF16)
+        to = out.at[:, g * width : (g + 1) * width]
+        copies.append(pltpu.make_async_copy(held.at[g], to, sems.at[g]))
+        copies[-1].start()
+    for copy in copies:
+        copy.wait()
 
 
 def land_kernel(
@@ -167,17 +172,15 @@
     head_dim = queries.shape[1]
     noted = arrived[:, PAIRS * width :].astype(F32)
     doc_lines[...] = noted
-    shape = noted.shape
-    first = lax.rem(iota(shape, 0), LINES) < SLOTS
-    spot = (iota(shape, 1) + 1).astype(F32)
+    labels = noted.T
+    shape = labels.shape
+    first = lax.rem(iota(shape, 1), LINES) < SLOTS
+    spot = (iota(shape, 0) + 1).astype(F32)
     for g in range(PAIRS):
-        lands = noted[:, g : g + 1] == spot
-        landing = jnp.concatenate([hot(lands & first), hot(lands & ~first)], 1)
-        placed = lax.dot_general(
-            landing,
-            arrived[:, g * width : (g + 1) * width],
-            (((0,), (0,)), ((), ())),
-            preferred_element_type=F32,
+        lands = labels[g : g + 1, :] == spot
+        landing = jnp.concatenate([hot(lands & first), hot(lands & ~first)], 0)
+        placed = jnp.dot(
+            landing, arrived[:, g * width : (g + 1) * width], preferred_element_type=F32
         ).astype(BF16)
         if g == 0:
             for h in range(queries.shape[0] // rows):
@@ -241,16 +244,13 @@
 HBM = pl.BlockSpec(memory_space=pltpu.HBM)
 
 
-def call(kernel, outs, operands, away=(), scratch=(), limit=24, near=(), cost=None):
-    shapes = [
-        pltpu.VMEM(s, t) if i in near else jax.ShapeDtypeStruct(s, t)
-        for i, (s, t) in enumerate(outs)
-    ]
+def call(kernel, outs, operands, away=(), scratch=(), limit=24, cost=None, out_spec=VMEM):
+    shapes = [jax.ShapeDtypeStruct(s, t) for s, t in outs]
     return pl.pallas_call(
         kernel,
         out_shape=shapes,
         in_specs=[SMEM if x.shape == (1,) else VMEM for x in operands] + [HBM] * len(away),
-        out_specs=[VMEM] * len(shapes),
+        out_specs=[out_spec] * len(shapes),
         scratch_shapes=scratch,
         cost_estimate=cost and pl.CostEstimate(flops=cost, bytes_accessed=0, transcendentals=0),
         compiler_params=pltpu.CompilerParams(vmem_limit_bytes=limit * 2**20),
@@ -296,7 +296,7 @@
         scratch=[pltpu.VMEM((1, rows), I32)] * 2 + [pltpu.SemaphoreType.DMA((4,))],
         cost=TABLES_COST,
     )
-    shifts = (0, 1, 3, 2)
+    shifts = (0, 2, 1, 3)
     other = [across] + [
         lax.ppermute(across, "kvh", [(i, (i + 2 * d) % n) for i in range(n)]) for d in shifts[1:]
     ]
@@ -318,6 +318,11 @@
         project_kernel,
         [((lines, columns), BF16)],
         [first, cosine, sine, gains, picks, notes, *ahead, *other],
+        scratch=[
+            pltpu.VMEM((PAIRS, lines, 2 * head_dim), BF16),
+            pltpu.SemaphoreType.DMA((PAIRS + 1,)),
+        ],
+        out_spec=HBM,
     )
     arrived = lax.all_to_all(
         parcel.reshape(blocks, LINES, columns), "ctx", split_axis=0, concat_axis=0, tiled=True

time: 79 us -> 77.6 us (0.982)
  no operation moved by 1% of the time
where the time goes in v5:
time: 77.6 us; the launch traced here: 77.2 us
  starting transfers between devices  39.1 us (50%)
  waiting for transfers between devices  26.9 us (35%)
  Pallas kernels  9.66 us (12%)
  local copies, waits for them, and re-layouts  0.91 us (1%)
    all_to_all x1, waiting for transfers between devices, body(): lax.all_to_all(parcel.reshape(blocks, LINES, columns), 'ctx', split_axis=...  25.8 us
    all_to_all x1, starting transfers between devices, body(): lax.all_to_all(parcel.reshape(blocks, LINES, columns), 'ctx', split_axis=...  14.6 us
    ppermute x3, starting transfers between devices, body(): lax.ppermute(across, 'kvh', [(i, (i + 2 * d) % n) for i in range(n)])  10.2 us
    pallas_call x8, Pallas kernels, call(): pl.pallas_call(kernel, out_shape=shapes, in_specs=[SMEM if x.shape == (1,...  9.66 us
    ppermute x1, starting transfers between devices, body(): across = lax.ppermute(hidden, 'kvh', [(i, i ^ 1) for i in range(n)])  8.27 us
    all_to_all x1, starting transfers between devices, body(): lax.all_to_all(spread, 'kvh', 0, 0, tiled=True, axis_index_groups=along_x)  4.01 us
    ppermute x1, starting transfers between devices, body(): swapped = lax.ppermute(sent, 'ctx', [(i, i ^ 1) for i in range(blocks)])  2.05 us
  transfers between devices with their start and end apart: 7, of which 3 were waited for; matrix products, arithmetic and copies ran while one was open for 1% of the time, Pallas kernels for 8%

profile of v5, /device:TPU:1, one launch (start us, length us, event | category | flops | bytes accessed | tf_op | source)
XLA Modules:
  0.0 77.2 jit_solution(18069213419404570775)
XLA Ops:
  0.0 8.3 %collective-permute-start = (bf16[128,512]{1,0:T(8,128)(2,1)}, bf16[128,512]{1,0:T(8,128)(2,1)S(1)}, u32[]{:S(2)}, u32[]{:S(2)}) collective-permute-start(bf16[128,512]{1,0:T(8,128)(2,1)} %hidden.1), channel_id=1, source_target_pairs={{0,1},{1,0},{2,3},{3,2},{4,5},{5,4},{6,7},{7,6},{8,9},{9,8},{10,11... | collective-permute-start | bytes 393224 | tf_op jit(solution)/shard_map/ppermute | solution.py:281
  8.3 0.0 copy-start
  8.3 0.9 %copy-done = bf16[128,512]{1,0:T(8,128)(2,1)S(1)} copy-done((bf16[128,512]{1,0:T(8,128)(2,1)S(1)}, bf16[128,512]{1,0:T(8,128)(2,1)}, u32[]{:S(2)}) %copy-start) | copy-done | bytes 131096
  9.2 0.8 %shard_map.82 = bf16[4,128,512]{2,1,0:T(8,128)(2,1)} custom-call(bf16[128,512]{1,0:T(8,128)(2,1)S(1)} %copy-done), custom_call_target="tpu_custom_call" | custom-call | tf_op jit(solution)/shard_map/pallas_call | solution.py:249
  10.0 4.0 %all-to-all-start = ((bf16[4,128,512]{2,1,0:T(8,128)(2,1)}), bf16[4,128,512]{2,1,0:T(8,128)(2,1)S(1)}, u32[]{:S(2)}, u32[]{:S(2)}) async-start(bf16[4,128,512]{2,1,0:T(8,128)(2,1)} %shard_map.82), calls=%async_computation | async-start | bytes 1048576 | tf_op jit(solution)/shard_map/all_to_all | solution.py:287
  14.0 0.0 copy-start.1
  14.0 1.2 %shard_map.84 = (bf16[3,512,128]{2,1,0:T(8,128)(2,1)S(1)}, bf16[512,128]{1,0:T(8,128)(2,1)S(1)}, f32[2,128]{1,0:T(2,128)S(1)}) custom-call(s32[1,128]{1,0:T(1,128)} %bitcast.12, s32[1,128]{1,0:T(1,128)} %bitcast.9, f32[1,128]{1,0:T(1,128)} %bitcast.10, f32[1,128]{1,0:T(1,128)} %bitcast.11), custom_call_target="tpu_custom_call" | custom-call | flops 20000000000 | tf_op jit(solution)/shard_map/pallas_call | solution.py:249
  15.2 0.0 copy-done.1
  15.3 0.0 collective-permute-done.refs_0_
  15.3 4.6 %collective-permute-start.3 = (bf16[128,512]{1,0:T(8,128)(2,1)S(1)}, bf16[128,512]{1,0:T(8,128)(2,1)S(1)}, u32[]{:S(2)}, u32[]{:S(2)}) collective-permute-start(bf16[128,512]{1,0:T(8,128)(2,1)S(1)} %collective-permute-done.refs_0_), channel_id=1, source_target_pairs={{0,6},{1,7},{2,0},{3,1},{4,2},{5,3},{6,4},{7,5},{8,14},{9,15},{10,... | collective-permute-start | bytes 393224 | tf_op jit(solution)/shard_map/ppermute | solution.py:301
  19.9 1.9 %collective-permute-start.2 = (bf16[128,512]{1,0:T(8,128)(2,1)S(1)}, bf16[128,512]{1,0:T(8,128)(2,1)S(1)}, u32[]{:S(2)}, u32[]{:S(2)}) collective-permute-start(bf16[128,512]{1,0:T(8,128)(2,1)S(1)} %collective-permute-done.refs_0_), channel_id=1, source_target_pairs={{0,2},{1,3},{2,4},{3,5},{4,6},{5,7},{6,0},{7,1},{8,10},{9,11},{10,... | collective-permute-start | bytes 393224 | tf_op jit(solution)/shard_map/ppermute | solution.py:301
  21.8 3.7 %collective-permute-start.1 = (bf16[128,512]{1,0:T(8,128)(2,1)S(1)}, bf16[128,512]{1,0:T(8,128)(2,1)S(1)}, u32[]{:S(2)}, u32[]{:S(2)}) collective-permute-start(bf16[128,512]{1,0:T(8,128)(2,1)S(1)} %collective-permute-done.refs_0_), channel_id=1, source_target_pairs={{0,4},{1,5},{2,6},{3,7},{4,0},{5,1},{6,2},{7,3},{8,12},{9,13},{10,... | collective-permute-start | bytes 393224 | tf_op jit(solution)/shard_map/ppermute | solution.py:301
  25.5 0.3 fusion
  25.8 0.1 pad_maximum_fusion
  25.9 0.0 all-to-all-done.mine
  25.9 1.9 %shard_map.83.first = f32[128,512]{1,0:T(8,128)S(1)} custom-call(s32[1]{0:T(128)} %bitcast.1.me_ref, bf16[4,128,512]{2,1,0:T(8,128)(2,1)S(1)} %all-to-all-done.mine, bf16[4096,256]{1,0:T(8,128)(2,1)} %wq.3, bf16[4096,128]{1,0:T(8,128)(2,1)} %wk.3, bf16[4096,128]{1,0:T(8,128)(2,1)} %wv.3), custom_call_target="tpu_custom_call" | custom-call | tf_op jit(solution)/shard_map/pallas_call | solution.py:249
  27.8 1.7 %shard_map.85 = (bf16[4,512,256]{2,1,0:T(8,128)(2,1)S(1)}, bf16[4,512,128]{2,1,0:T(8,128)(2,1)S(1)}, bf16[4,512,128]{2,1,0:T(8,128)(2,1)S(1)}) custom-call(s32[1]{0:T(128)} %bitcast.1.me_ref, f32[128,512]{1,0:T(8,128)S(1)} %shard_map.83.first, bf16[4096,256]{1,0:T(8,128)(2,1)} %wq.3, bf16[4096,128]{1,0:T(8,128)(2,1)} %wk.3, bf16[4096,128]{1,0:T(8,128)(2,1)} %wv.3), custom_call_target="tpu_custom_call" | custom-call | tf_op jit(solution)/shard_map/pallas_call | solution.py:249
  29.5 0.0 collective-permute-done.3.refs_3_
  29.5 0.0 collective-permute-done.2.refs_2_
  29.5 0.1 collective-permute-done.1.refs_1_
  29.6 2.1 %shard_map.86 = bf16[512,896]{1,0:T(8,128)(2,1)} custom-call(f32[128,512]{1,0:T(8,128)S(1)} %shard_map.83.first, f32[128,128]{1,0:T(8,128)S(1)} %get-tuple-element.34.cosine, f32[128,128]{1,0:T(8,128)S(1)} %get-tuple-element.35.sine, f32[2,128]{1,0:T(2,128)S(1)} %get-tuple-element.18.gains, bf16[3,512,128]{2,1,0:T(8,128)(2,1)S(1)} %get-tuple-element.19.picks, ...), custom_call_target="tpu_custom_call" | custom-call | tf_op jit(solution)/shard_map/pallas_call | solution.py:249
  31.8 14.6 %all-to-all-start.1 = ((bf16[64,8,896]{2,1,0:T(8,128)(2,1)}), bf16[64,8,896]{2,1,0:T(8,128)(2,1)S(1)}, u32[]{:S(2)}, u32[]{:S(2)}) async-start(bf16[64,8,896]{2,1,0:T(8,128)(2,1)} %bitcast.6), calls=%async_computation.1 | async-start | bytes 1835008 | tf_op jit(solution)/shard_map/all_to_all | solution.py:327
  46.4 25.8 %all-to-all-done.1 = bf16[64,8,896]{2,1,0:T(8,128)(2,1)S(1)} async-done(((bf16[64,8,896]{2,1,0:T(8,128)(2,1)}), bf16[64,8,896]{2,1,0:T(8,128)(2,1)S(1)}, u32[]{:S(2)}, u32[]{:S(2)}) %all-to-all-start.1) | async-done | bytes 917536 | tf_op jit(solution)/shard_map/all_to_all | solution.py:327
  72.2 0.5 shard_map.87
  72.7 2.1 %collective-permute-start.4 = (bf16[512,256]{1,0:T(8,128)(2,1)S(1)}, bf16[512,256]{1,0:T(8,128)(2,1)S(1)}, u32[]{:S(2)}, u32[]{:S(2)}) collective-permute-start(bf16[512,256]{1,0:T(8,128)(2,1)S(1)} %get-tuple-element.27), channel_id=1, source_target_pairs={{0,8},{8,0},{16,24},{24,16},{32,40},{40,32},{48,56},{56,48},{64,72... | collective-permute-start | bytes 786440 | tf_op jit(solution)/shard_map/ppermute | solution.py:344
  74.8 0.4 shard_map.88
  75.2 0.9 %collective-permute-done.4.keyvalues = bf16[512,256]{1,0:T(8,128)(2,1)S(1)} collective-permute-done((bf16[512,256]{1,0:T(8,128)(2,1)S(1)}, bf16[512,256]{1,0:T(8,128)(2,1)S(1)}, u32[]{:S(2)}, u32[]{:S(2)}) %collective-permute-start.4) | collective-permute-done | bytes 262176 | tf_op jit(solution)/shard_map/ppermute | solution.py:344
  76.1 1.0 %shard_map.89 = bf16[128,256]{1,0:T(8,128)(2,1)} custom-call(bf16[256,128]{1,0:T(8,128)(2,1)S(1)} %get-tuple-element.24.queries, s32[256,1]{1,0:T(8,128)S(1)} %get-tuple-element.25.query_docs, s32[16,128]{1,0:T(8,128)S(1)} %get-tuple-element.26.key_docs, bf16[512,256]{1,0:T(8,128)(2,1)S(1)} %collective-permute-done.4.keyvalues, ...), custom_call_target="tpu_custom_call" | custom-call | tf_op jit(solution)/shard_map/pallas_call | solution.py:249
  (2 shorter events, 0.0 us)
Async XLA Ops:
  0.0 15.3 %collective-permute-start = (bf16[128,512]{1,0:T(8,128)(2,1)}, bf16[128,512]{1,0:T(8,128)(2,1)S(1)}, u32[]{:S(2)}, u32[]{:S(2)}) collective-permute-start(bf16[128,512]{1,0:T(8,128)(2,1)} %hidden.1), channel_id=1, source_target_pairs={{0,1},{1,0},{2,3},{3,2},{4,5},{5,4},{6,7},{7,6},{8,9},{9,8},{10,11... | collective-permute-start | bytes 393224 | tf_op jit(solution)/shard_map/ppermute | solution.py:281
  8.3 0.9 %copy-start = (bf16[128,512]{1,0:T(8,128)(2,1)S(1)}, bf16[128,512]{1,0:T(8,128)(2,1)}, u32[]{:S(2)}) copy-start(bf16[128,512]{1,0:T(8,128)(2,1)} %hidden.1) | copy-start | bytes 393220
  10.0 15.9 %all-to-all-start = ((bf16[4,128,512]{2,1,0:T(8,128)(2,1)}), bf16[4,128,512]{2,1,0:T(8,128)(2,1)S(1)}, u32[]{:S(2)}, u32[]{:S(2)}) async-start(bf16[4,128,512]{2,1,0:T(8,128)(2,1)} %shard_map.82), calls=%async_computation | async-start | bytes 1048576 | tf_op jit(solution)/shard_map/all_to_all | solution.py:287
  14.0 1.2 %copy-start.1 = (s32[128]{0:T(128)S(1)}, s32[128]{0:T(128)}, u32[]{:S(2)}) copy-start(s32[128]{0:T(128)} %param.9) | copy-start | bytes 1540
  15.3 14.2 %collective-permute-start.3 = (bf16[128,512]{1,0:T(8,128)(2,1)S(1)}, bf16[128,512]{1,0:T(8,128)(2,1)S(1)}, u32[]{:S(2)}, u32[]{:S(2)}) collective-permute-start(bf16[128,512]{1,0:T(8,128)(2,1)S(1)} %collective-permute-done.refs_0_), channel_id=1, source_target_pairs={{0,6},{1,7},{2,0},{3,1},{4,2},{5,3},{6,4},{7,5},{8,14},{9,15},{10,... | collective-permute-start | bytes 393224 | tf_op jit(solution)/shard_map/ppermute | solution.py:301
  19.9 9.6 %collective-permute-start.2 = (bf16[128,512]{1,0:T(8,128)(2,1)S(1)}, bf16[128,512]{1,0:T(8,128)(2,1)S(1)}, u32[]{:S(2)}, u32[]{:S(2)}) collective-permute-start(bf16[128,512]{1,0:T(8,128)(2,1)S(1)} %collective-permute-done.refs_0_), channel_id=1, source_target_pairs={{0,2},{1,3},{2,4},{3,5},{4,6},{5,7},{6,0},{7,1},{8,10},{9,11},{10,... | collective-permute-start | bytes 393224 | tf_op jit(solution)/shard_map/ppermute | solution.py:301
  21.8 7.8 %collective-permute-start.1 = (bf16[128,512]{1,0:T(8,128)(2,1)S(1)}, bf16[128,512]{1,0:T(8,128)(2,1)S(1)}, u32[]{:S(2)}, u32[]{:S(2)}) collective-permute-start(bf16[128,512]{1,0:T(8,128)(2,1)S(1)} %collective-permute-done.refs_0_), channel_id=1, source_target_pairs={{0,4},{1,5},{2,6},{3,7},{4,0},{5,1},{6,2},{7,3},{8,12},{9,13},{10,... | collective-permute-start | bytes 393224 | tf_op jit(solution)/shard_map/ppermute | solution.py:301
  31.8 40.4 %all-to-all-start.1 = ((bf16[64,8,896]{2,1,0:T(8,128)(2,1)}), bf16[64,8,896]{2,1,0:T(8,128)(2,1)S(1)}, u32[]{:S(2)}, u32[]{:S(2)}) async-start(bf16[64,8,896]{2,1,0:T(8,128)(2,1)} %bitcast.6), calls=%async_computation.1 | async-start | bytes 1835008 | tf_op jit(solution)/shard_map/all_to_all | solution.py:327
  72.7 3.4 %collective-permute-start.4 = (bf16[512,256]{1,0:T(8,128)(2,1)S(1)}, bf16[512,256]{1,0:T(8,128)(2,1)S(1)}, u32[]{:S(2)}, u32[]{:S(2)}) collective-permute-start(bf16[512,256]{1,0:T(8,128)(2,1)S(1)} %get-tuple-element.27), channel_id=1, source_target_pairs={{0,8},{8,0},{16,24},{24,16},{32,40},{40,32},{48,56},{56,48},{64,72... | collective-permute-start | bytes 786440 | tf_op jit(solution)/shard_map/ppermute | solution.py:344

commit v6 on v5

--- a/solution.py
+++ b/solution.py
@@ -95,25 +95,23 @@
     return copies
 
 
-def project_first_kernel(me_ref, mine, wq, wk, wv, first, *room):
-    held, sems = room[:-1], room[-1]
-    total = 0.0
+def project_first_kernel(shifts, me_ref, mine, wq, wk, wv, first, *refs):
+    ahead, held, (sems, ahead_sems) = refs[:3], refs[3:6], refs[6:]
     side = lax.rem(me_ref[0], 2)
     owners = [2 * k + side for k in range(mine.shape[0])]
-    for k, copies in enumerate(weight_copies((wq, wk, wv), held, sems, owners)):
+    steps = weight_copies((wq, wk, wv), held, sems, owners)
+    groups = wq.shape[0] // held[0].shape[1]
+    partner = me_ref[0] + 1 - 2 * side
+    owners = [lax.rem(partner + groups - 2 * d, groups) for d in shifts]
+    later = weight_copies((wq, wk, wv), ahead, ahead_sems, owners)
+    total = 0.0
+    for k, copies in enumerate(steps):
         for copy in copies:
             copy.wait()
         block = jnp.concatenate([to[k] for to in held], 1)
         total = total + jnp.dot(mine[k], block, preferred_element_type=F32)
     first[...] = total
-
-
-def ahead_kernel(shifts, me_ref, first, wq, wk, wv, *refs):
-    held, sems = refs[:-1], refs[-1]
-    groups = wq.shape[0] // held[0].shape[1]
-    partner = me_ref[0] + 1 - 2 * lax.rem(me_ref[0], 2)
-    owners = [lax.rem(partner + groups - 2 * d, groups) for d in shifts]
-    for copies in weight_copies((wq, wk, wv), held, sems, owners):
+    for copies in later:
         for copy in copies:
             copy.wait()
 
@@ -296,7 +294,7 @@
         scratch=[pltpu.VMEM((1, rows), I32)] * 2 + [pltpu.SemaphoreType.DMA((4,))],
         cost=TABLES_COST,
     )
-    shifts = (0, 2, 1, 3)
+    shifts = (0, 3, 2, 1)
     other = [across] + [
         lax.ppermute(across, "kvh", [(i, (i + 2 * d) % n) for i in range(n)]) for d in shifts[1:]
     ]
@@ -306,14 +304,13 @@
     all_heads = q_width + 2 * head_dim
     held = [((members, width, w.shape[1]), BF16) for w in weights]
     sems = pltpu.SemaphoreType.DMA((members, len(weights)))
-    (first,) = call(
-        project_first_kernel,
-        [((rows, all_heads), F32)],
+    first, *ahead = call(
+        functools.partial(project_first_kernel, shifts),
+        [((rows, all_heads), F32), *held],
         [me_kvh, mine],
         weights,
-        scratch=[pltpu.VMEM(*h) for h in held] + [sems],
-    )
-    ahead = call(functools.partial(ahead_kernel, shifts), held, [me_kvh, first], weights, scratch=[sems])
+        scratch=[pltpu.VMEM(*h) for h in held] + [sems, sems],
+    )
     (parcel,) = call(
         project_kernel,
         [((lines, columns), BF16)],

time: 77.6 us -> 77.5 us (level)
  Pallas kernels: 9.66 us -> 8.7 us
    pallas_call x8 -> x7, Pallas kernels: 9.66 us -> 8.7 us  [call(): pl.pallas_call(kernel, out_shape=shapes, in_specs=[SMEM if x.shape == (1,...]
  transfers between devices with their start and end apart: 7 -> 7, of which waited for: 3 -> 3; matrix products, arithmetic and copies ran while one was open for 1% -> 1% of each run, Pallas kernels for 8% -> 7%
where the time goes in v6:
time: 77.5 us; the launch traced here: 77 us
  starting transfers between devices  39.5 us (51%)
  waiting for transfers between devices  27.4 us (35%)
  Pallas kernels  8.7 us (11%)
  local copies, waits for them, and re-layouts  0.91 us (1%)
    all_to_all x1, waiting for transfers between devices, body(): lax.all_to_all(parcel.reshape(blocks, LINES, columns), 'ctx', split_axis=...  25.8 us
    all_to_all x1, starting transfers between devices, body(): lax.all_to_all(parcel.reshape(blocks, LINES, columns), 'ctx', split_axis=...  14.4 us
    ppermute x3, starting transfers between devices, body(): lax.ppermute(across, 'kvh', [(i, (i + 2 * d) % n) for i in range(n)])  10.8 us
    pallas_call x7, Pallas kernels, call(): pl.pallas_call(kernel, out_shape=shapes, in_specs=[SMEM if x.shape == (1,...  8.7 us
    ppermute x1, starting transfers between devices, body(): across = lax.ppermute(hidden, 'kvh', [(i, i ^ 1) for i in range(n)])  8.27 us
    all_to_all x1, starting transfers between devices, body(): lax.all_to_all(spread, 'kvh', 0, 0, tiled=True, axis_index_groups=along_x)  4.01 us
    ppermute x1, starting transfers between devices, body(): swapped = lax.ppermute(sent, 'ctx', [(i, i ^ 1) for i in range(blocks)])  2.04 us
  transfers between devices with their start and end apart: 7, of which 3 were waited for; matrix products, arithmetic and copies ran while one was open for 1% of the time, Pallas kernels for 7%

profile of v6, /device:TPU:1, one launch (start us, length us, event | category | flops | bytes accessed | tf_op | source)
XLA Modules:
  0.0 77.0 jit_solution(16934855199748857889)
XLA Ops:
  0.0 8.3 %collective-permute-start = (bf16[128,512]{1,0:T(8,128)(2,1)}, bf16[128,512]{1,0:T(8,128)(2,1)S(1)}, u32[]{:S(2)}, u32[]{:S(2)}) collective-permute-start(bf16[128,512]{1,0:T(8,128)(2,1)} %hidden.1), channel_id=1, source_target_pairs={{0,1},{1,0},{2,3},{3,2},{4,5},{5,4},{6,7},{7,6},{8,9},{9,8},{10,11... | collective-permute-start | bytes 393224 | tf_op jit(solution)/shard_map/ppermute | solution.py:279
  8.3 0.0 copy-start
  8.3 0.9 %copy-done = bf16[128,512]{1,0:T(8,128)(2,1)S(1)} copy-done((bf16[128,512]{1,0:T(8,128)(2,1)S(1)}, bf16[128,512]{1,0:T(8,128)(2,1)}, u32[]{:S(2)}) %copy-start) | copy-done | bytes 131096
  9.2 0.8 %shard_map.82 = bf16[4,128,512]{2,1,0:T(8,128)(2,1)} custom-call(bf16[128,512]{1,0:T(8,128)(2,1)S(1)} %copy-done), custom_call_target="tpu_custom_call" | custom-call | tf_op jit(solution)/shard_map/pallas_call | solution.py:247
  10.0 4.0 %all-to-all-start = ((bf16[4,128,512]{2,1,0:T(8,128)(2,1)}), bf16[4,128,512]{2,1,0:T(8,128)(2,1)S(1)}, u32[]{:S(2)}, u32[]{:S(2)}) async-start(bf16[4,128,512]{2,1,0:T(8,128)(2,1)} %shard_map.82), calls=%async_computation | async-start | bytes 1048576 | tf_op jit(solution)/shard_map/all_to_all | solution.py:285
  14.0 0.0 copy-start.1
  14.0 1.2 %shard_map.84 = (bf16[3,512,128]{2,1,0:T(8,128)(2,1)S(1)}, bf16[512,128]{1,0:T(8,128)(2,1)S(1)}, f32[2,128]{1,0:T(2,128)S(1)}) custom-call(s32[1,128]{1,0:T(1,128)} %bitcast.12, s32[1,128]{1,0:T(1,128)} %bitcast.9, f32[1,128]{1,0:T(1,128)} %bitcast.10, f32[1,128]{1,0:T(1,128)} %bitcast.11), custom_call_target="tpu_custom_call" | custom-call | flops 20000000000 | tf_op jit(solution)/shard_map/pallas_call | solution.py:247
  15.2 0.0 copy-done.1
  15.3 0.0 collective-permute-done.refs_0_
  15.3 3.4 %collective-permute-start.3 = (bf16[128,512]{1,0:T(8,128)(2,1)S(1)}, bf16[128,512]{1,0:T(8,128)(2,1)S(1)}, u32[]{:S(2)}, u32[]{:S(2)}) collective-permute-start(bf16[128,512]{1,0:T(8,128)(2,1)S(1)} %collective-permute-done.refs_0_), channel_id=1, source_target_pairs={{0,2},{1,3},{2,4},{3,5},{4,6},{5,7},{6,0},{7,1},{8,10},{9,11},{10,... | collective-permute-start | bytes 393224 | tf_op jit(solution)/shard_map/ppermute | solution.py:299
  18.7 4.3 %collective-permute-start.2 = (bf16[128,512]{1,0:T(8,128)(2,1)S(1)}, bf16[128,512]{1,0:T(8,128)(2,1)S(1)}, u32[]{:S(2)}, u32[]{:S(2)}) collective-permute-start(bf16[128,512]{1,0:T(8,128)(2,1)S(1)} %collective-permute-done.refs_0_), channel_id=1, source_target_pairs={{0,4},{1,5},{2,6},{3,7},{4,0},{5,1},{6,2},{7,3},{8,12},{9,13},{10,... | collective-permute-start | bytes 393224 | tf_op jit(solution)/shard_map/ppermute | solution.py:299
  23.0 3.1 %collective-permute-start.1 = (bf16[128,512]{1,0:T(8,128)(2,1)S(1)}, bf16[128,512]{1,0:T(8,128)(2,1)S(1)}, u32[]{:S(2)}, u32[]{:S(2)}) collective-permute-start(bf16[128,512]{1,0:T(8,128)(2,1)S(1)} %collective-permute-done.refs_0_), channel_id=1, source_target_pairs={{0,6},{1,7},{2,0},{3,1},{4,2},{5,3},{6,4},{7,5},{8,14},{9,15},{10,... | collective-permute-start | bytes 393224 | tf_op jit(solution)/shard_map/ppermute | solution.py:299
  26.1 0.3 fusion
  26.4 0.1 pad_maximum_fusion
  26.5 0.0 all-to-all-done.mine
  26.5 2.6 %shard_map.83 = (f32[128,512]{1,0:T(8,128)S(1)}, bf16[4,512,256]{2,1,0:T(8,128)(2,1)S(1)}, bf16[4,512,128]{2,1,0:T(8,128)(2,1)S(1)}, bf16[4,512,128]{2,1,0:T(8,128)(2,1)S(1)}) custom-call(s32[1]{0:T(128)} %bitcast.1.me_ref, bf16[4,128,512]{2,1,0:T(8,128)(2,1)S(1)} %all-to-all-done.mine, bf16[4096,256]{1,0:T(8,128)(2,1)} %wq.1, bf16[4096,128]{1,0:T(8,128)(2,1)} %wk.1, ...), custom_call_target="tpu_custom_call" | custom-call | tf_op jit(solution)/shard_map/pallas_call | solution.py:247
  29.1 0.0 collective-permute-done.3.refs_3_
  29.1 0.0 collective-permute-done.2.refs_2_
  29.1 0.6 collective-permute-done.1.refs_1_
  29.7 2.1 %shard_map.85 = bf16[512,896]{1,0:T(8,128)(2,1)} custom-call(f32[128,512]{1,0:T(8,128)S(1)} %get-tuple-element.19.first, f32[128,128]{1,0:T(8,128)S(1)} %get-tuple-element.36.cosine, f32[128,128]{1,0:T(8,128)S(1)} %get-tuple-element.37.sine, f32[2,128]{1,0:T(2,128)S(1)} %get-tuple-element.20.gains, bf16[3,512,128]{2,1,0:T(8,128)(2,1)S(1)} %get-tuple-element.21.picks, ...), custom_call_target="tpu_custom_call" | custom-call | tf_op jit(solution)/shard_map/pallas_call | solution.py:247
  31.9 14.4 %all-to-all-start.1 = ((bf16[64,8,896]{2,1,0:T(8,128)(2,1)}), bf16[64,8,896]{2,1,0:T(8,128)(2,1)S(1)}, u32[]{:S(2)}, u32[]{:S(2)}) async-start(bf16[64,8,896]{2,1,0:T(8,128)(2,1)} %bitcast.6), calls=%async_computation.1 | async-start | bytes 1835008 | tf_op jit(solution)/shard_map/all_to_all | solution.py:324
  46.2 25.8 %all-to-all-done.1 = bf16[64,8,896]{2,1,0:T(8,128)(2,1)S(1)} async-done(((bf16[64,8,896]{2,1,0:T(8,128)(2,1)}), bf16[64,8,896]{2,1,0:T(8,128)(2,1)S(1)}, u32[]{:S(2)}, u32[]{:S(2)}) %all-to-all-start.1) | async-done | bytes 917536 | tf_op jit(solution)/shard_map/all_to_all | solution.py:324
  72.1 0.5 shard_map.86
  72.6 2.0 %collective-permute-start.4 = (bf16[512,256]{1,0:T(8,128)(2,1)S(1)}, bf16[512,256]{1,0:T(8,128)(2,1)S(1)}, u32[]{:S(2)}, u32[]{:S(2)}) collective-permute-start(bf16[512,256]{1,0:T(8,128)(2,1)S(1)} %get-tuple-element.29), channel_id=1, source_target_pairs={{0,8},{8,0},{16,24},{24,16},{32,40},{40,32},{48,56},{56,48},{64,72... | collective-permute-start | bytes 786440 | tf_op jit(solution)/shard_map/ppermute | solution.py:341
  74.6 0.4 shard_map.87
  75.1 0.9 %collective-permute-done.4.keyvalues = bf16[512,256]{1,0:T(8,128)(2,1)S(1)} collective-permute-done((bf16[512,256]{1,0:T(8,128)(2,1)S(1)}, bf16[512,256]{1,0:T(8,128)(2,1)S(1)}, u32[]{:S(2)}, u32[]{:S(2)}) %collective-permute-start.4) | collective-permute-done | bytes 262176 | tf_op jit(solution)/shard_map/ppermute | solution.py:341
  76.0 1.0 %shard_map.88 = bf16[128,256]{1,0:T(8,128)(2,1)} custom-call(bf16[256,128]{1,0:T(8,128)(2,1)S(1)} %get-tuple-element.26.queries, s32[256,1]{1,0:T(8,128)S(1)} %get-tuple-element.27.query_docs, s32[16,128]{1,0:T(8,128)S(1)} %get-tuple-element.28.key_docs, bf16[512,256]{1,0:T(8,128)(2,1)S(1)} %collective-permute-done.4.keyvalues, ...), custom_call_target="tpu_custom_call" | custom-call | tf_op jit(solution)/shard_map/pallas_call | solution.py:247
  (2 shorter events, 0.0 us)
Async XLA Ops:
  0.0 15.3 %collective-permute-start = (bf16[128,512]{1,0:T(8,128)(2,1)}, bf16[128,512]{1,0:T(8,128)(2,1)S(1)}, u32[]{:S(2)}, u32[]{:S(2)}) collective-permute-start(bf16[128,512]{1,0:T(8,128)(2,1)} %hidden.1), channel_id=1, source_target_pairs={{0,1},{1,0},{2,3},{3,2},{4,5},{5,4},{6,7},{7,6},{8,9},{9,8},{10,11... | collective-permute-start | bytes 393224 | tf_op jit(solution)/shard_map/ppermute | solution.py:279
  8.3 0.9 %copy-start = (bf16[128,512]{1,0:T(8,128)(2,1)S(1)}, bf16[128,512]{1,0:T(8,128)(2,1)}, u32[]{:S(2)}) copy-start(bf16[128,512]{1,0:T(8,128)(2,1)} %hidden.1) | copy-start | bytes 393220
  10.0 16.5 %all-to-all-start = ((bf16[4,128,512]{2,1,0:T(8,128)(2,1)}), bf16[4,128,512]{2,1,0:T(8,128)(2,1)S(1)}, u32[]{:S(2)}, u32[]{:S(2)}) async-start(bf16[4,128,512]{2,1,0:T(8,128)(2,1)} %shard_map.82), calls=%async_computation | async-start | bytes 1048576 | tf_op jit(solution)/shard_map/all_to_all | solution.py:285
  14.0 1.2 %copy-start.1 = (s32[128]{0:T(128)S(1)}, s32[128]{0:T(128)}, u32[]{:S(2)}) copy-start(s32[128]{0:T(128)} %param.9) | copy-start | bytes 1540
  15.3 13.8 %collective-permute-start.3 = (bf16[128,512]{1,0:T(8,128)(2,1)S(1)}, bf16[128,512]{1,0:T(8,128)(2,1)S(1)}, u32[]{:S(2)}, u32[]{:S(2)}) collective-permute-start(bf16[128,512]{1,0:T(8,128)(2,1)S(1)} %collective-permute-done.refs_0_), channel_id=1, source_target_pairs={{0,2},{1,3},{2,4},{3,5},{4,6},{5,7},{6,0},{7,1},{8,10},{9,11},{10,... | collective-permute-start | bytes 393224 | tf_op jit(solution)/shard_map/ppermute | solution.py:299
  18.7 10.5 %collective-permute-start.2 = (bf16[128,512]{1,0:T(8,128)(2,1)S(1)}, bf16[128,512]{1,0:T(8,128)(2,1)S(1)}, u32[]{:S(2)}, u32[]{:S(2)}) collective-permute-start(bf16[128,512]{1,0:T(8,128)(2,1)S(1)} %collective-permute-done.refs_0_), channel_id=1, source_target_pairs={{0,4},{1,5},{2,6},{3,7},{4,0},{5,1},{6,2},{7,3},{8,12},{9,13},{10,... | collective-permute-start | bytes 393224 | tf_op jit(solution)/shard_map/ppermute | solution.py:299
  23.0 6.7 %collective-permute-start.1 = (bf16[128,512]{1,0:T(8,128)(2,1)S(1)}, bf16[128,512]{1,0:T(8,128)(2,1)S(1)}, u32[]{:S(2)}, u32[]{:S(2)}) collective-permute-start(bf16[128,512]{1,0:T(8,128)(2,1)S(1)} %collective-permute-done.refs_0_), channel_id=1, source_target_pairs={{0,6},{1,7},{2,0},{3,1},{4,2},{5,3},{6,4},{7,5},{8,14},{9,15},{10,... | collective-permute-start | bytes 393224 | tf_op jit(solution)/shard_map/ppermute | solution.py:299
  31.9 40.2 %all-to-all-start.1 = ((bf16[64,8,896]{2,1,0:T(8,128)(2,1)}), bf16[64,8,896]{2,1,0:T(8,128)(2,1)S(1)}, u32[]{:S(2)}, u32[]{:S(2)}) async-start(bf16[64,8,896]{2,1,0:T(8,128)(2,1)} %bitcast.6), calls=%async_computation.1 | async-start | bytes 1835008 | tf_op jit(solution)/shard_map/all_to_all | solution.py:324
  72.6 3.4 %collective-permute-start.4 = (bf16[512,256]{1,0:T(8,128)(2,1)S(1)}, bf16[512,256]{1,0:T(8,128)(2,1)S(1)}, u32[]{:S(2)}, u32[]{:S(2)}) collective-permute-start(bf16[512,256]{1,0:T(8,128)(2,1)S(1)} %get-tuple-element.29), channel_id=1, source_target_pairs={{0,8},{8,0},{16,24},{24,16},{32,40},{40,32},{48,56},{56,48},{64,72... | collective-permute-start | bytes 786440 | tf_op jit(solution)/shard_map/ppermute | solution.py:341

commit v7 on v6

--- a/solution.py
+++ b/solution.py
@@ -294,7 +294,7 @@
         scratch=[pltpu.VMEM((1, rows), I32)] * 2 + [pltpu.SemaphoreType.DMA((4,))],
         cost=TABLES_COST,
     )
-    shifts = (0, 3, 2, 1)
+    shifts = (0, 2, 1, 3)
     other = [across] + [
         lax.ppermute(across, "kvh", [(i, (i + 2 * d) % n) for i in range(n)]) for d in shifts[1:]
     ]

time: 77.5 us -> 77.6 us (level)
  no operation moved by 1% of the time
where the time goes in v7:
time: 77.6 us; the launch traced here: 77.2 us
  starting transfers between devices  39.1 us (50%)
  waiting for transfers between devices  27.9 us (36%)
  Pallas kernels  8.69 us (11%)
  local copies, waits for them, and re-layouts  0.91 us (1%)
    all_to_all x1, waiting for transfers between devices, body(): lax.all_to_all(parcel.reshape(blocks, LINES, columns), 'ctx', split_axis=...  25.8 us
    all_to_all x1, starting transfers between devices, body(): lax.all_to_all(parcel.reshape(blocks, LINES, columns), 'ctx', split_axis=...  14.6 us
    ppermute x3, starting transfers between devices, body(): lax.ppermute(across, 'kvh', [(i, (i + 2 * d) % n) for i in range(n)])  10.2 us
    pallas_call x7, Pallas kernels, call(): pl.pallas_call(kernel, out_shape=shapes, in_specs=[SMEM if x.shape == (1,...  8.69 us
    ppermute x1, starting transfers between devices, body(): across = lax.ppermute(hidden, 'kvh', [(i, i ^ 1) for i in range(n)])  8.27 us
    all_to_all x1, starting transfers between devices, body(): lax.all_to_all(spread, 'kvh', 0, 0, tiled=True, axis_index_groups=along_x)  4.01 us
    ppermute x1, starting transfers between devices, body(): swapped = lax.ppermute(sent, 'ctx', [(i, i ^ 1) for i in range(blocks)])  2.04 us
  transfers between devices with their start and end apart: 7, of which 3 were waited for; matrix products, arithmetic and copies ran while one was open for 1% of the time, Pallas kernels for 7%

profile of v7, /device:TPU:1, one launch (start us, length us, event | category | flops | bytes accessed | tf_op | source)
XLA Modules:
  0.0 77.2 jit_solution(2142264281281959371)
XLA Ops:
  0.0 8.3 %collective-permute-start = (bf16[128,512]{1,0:T(8,128)(2,1)}, bf16[128,512]{1,0:T(8,128)(2,1)S(1)}, u32[]{:S(2)}, u32[]{:S(2)}) collective-permute-start(bf16[128,512]{1,0:T(8,128)(2,1)} %hidden.1), channel_id=1, source_target_pairs={{0,1},{1,0},{2,3},{3,2},{4,5},{5,4},{6,7},{7,6},{8,9},{9,8},{10,11... | collective-permute-start | bytes 393224 | tf_op jit(solution)/shard_map/ppermute | solution.py:279
  8.3 0.0 copy-start
  8.3 0.9 %copy-done = bf16[128,512]{1,0:T(8,128)(2,1)S(1)} copy-done((bf16[128,512]{1,0:T(8,128)(2,1)S(1)}, bf16[128,512]{1,0:T(8,128)(2,1)}, u32[]{:S(2)}) %copy-start) | copy-done | bytes 131096
  9.2 0.8 %shard_map.82 = bf16[4,128,512]{2,1,0:T(8,128)(2,1)} custom-call(bf16[128,512]{1,0:T(8,128)(2,1)S(1)} %copy-done), custom_call_target="tpu_custom_call" | custom-call | tf_op jit(solution)/shard_map/pallas_call | solution.py:247
  10.0 4.0 %all-to-all-start = ((bf16[4,128,512]{2,1,0:T(8,128)(2,1)}), bf16[4,128,512]{2,1,0:T(8,128)(2,1)S(1)}, u32[]{:S(2)}, u32[]{:S(2)}) async-start(bf16[4,128,512]{2,1,0:T(8,128)(2,1)} %shard_map.82), calls=%async_computation | async-start | bytes 1048576 | tf_op jit(solution)/shard_map/all_to_all | solution.py:285
  14.0 0.0 copy-start.1
  14.0 1.2 %shard_map.84 = (bf16[3,512,128]{2,1,0:T(8,128)(2,1)S(1)}, bf16[512,128]{1,0:T(8,128)(2,1)S(1)}, f32[2,128]{1,0:T(2,128)S(1)}) custom-call(s32[1,128]{1,0:T(1,128)} %bitcast.12, s32[1,128]{1,0:T(1,128)} %bitcast.9, f32[1,128]{1,0:T(1,128)} %bitcast.10, f32[1,128]{1,0:T(1,128)} %bitcast.11), custom_call_target="tpu_custom_call" | custom-call | flops 20000000000 | tf_op jit(solution)/shard_map/pallas_call | solution.py:247
  15.2 0.0 copy-done.1
  15.3 0.0 collective-permute-done.refs_0_
  15.3 4.6 %collective-permute-start.3 = (bf16[128,512]{1,0:T(8,128)(2,1)S(1)}, bf16[128,512]{1,0:T(8,128)(2,1)S(1)}, u32[]{:S(2)}, u32[]{:S(2)}) collective-permute-start(bf16[128,512]{1,0:T(8,128)(2,1)S(1)} %collective-permute-done.refs_0_), channel_id=1, source_target_pairs={{0,6},{1,7},{2,0},{3,1},{4,2},{5,3},{6,4},{7,5},{8,14},{9,15},{10,... | collective-permute-start | bytes 393224 | tf_op jit(solution)/shard_map/ppermute | solution.py:299
  19.9 1.9 %collective-permute-start.2 = (bf16[128,512]{1,0:T(8,128)(2,1)S(1)}, bf16[128,512]{1,0:T(8,128)(2,1)S(1)}, u32[]{:S(2)}, u32[]{:S(2)}) collective-permute-start(bf16[128,512]{1,0:T(8,128)(2,1)S(1)} %collective-permute-done.refs_0_), channel_id=1, source_target_pairs={{0,2},{1,3},{2,4},{3,5},{4,6},{5,7},{6,0},{7,1},{8,10},{9,11},{10,... | collective-permute-start | bytes 393224 | tf_op jit(solution)/shard_map/ppermute | solution.py:299
  21.8 3.7 %collective-permute-start.1 = (bf16[128,512]{1,0:T(8,128)(2,1)S(1)}, bf16[128,512]{1,0:T(8,128)(2,1)S(1)}, u32[]{:S(2)}, u32[]{:S(2)}) collective-permute-start(bf16[128,512]{1,0:T(8,128)(2,1)S(1)} %collective-permute-done.refs_0_), channel_id=1, source_target_pairs={{0,4},{1,5},{2,6},{3,7},{4,0},{5,1},{6,2},{7,3},{8,12},{9,13},{10,... | collective-permute-start | bytes 393224 | tf_op jit(solution)/shard_map/ppermute | solution.py:299
  25.5 0.3 fusion
  25.8 0.1 pad_maximum_fusion
  25.9 0.0 all-to-all-done.mine
  25.9 2.6 %shard_map.83 = (f32[128,512]{1,0:T(8,128)S(1)}, bf16[4,512,256]{2,1,0:T(8,128)(2,1)S(1)}, bf16[4,512,128]{2,1,0:T(8,128)(2,1)S(1)}, bf16[4,512,128]{2,1,0:T(8,128)(2,1)S(1)}) custom-call(s32[1]{0:T(128)} %bitcast.1.me_ref, bf16[4,128,512]{2,1,0:T(8,128)(2,1)S(1)} %all-to-all-done.mine, bf16[4096,256]{1,0:T(8,128)(2,1)} %wq.1, bf16[4096,128]{1,0:T(8,128)(2,1)} %wk.1, ...), custom_call_target="tpu_custom_call" | custom-call | tf_op jit(solution)/shard_map/pallas_call | solution.py:247
  28.5 0.0 collective-permute-done.3.refs_3_
  28.5 0.0 collective-permute-done.2.refs_2_
  28.5 1.1 %collective-permute-done.1.refs_1_ = bf16[128,512]{1,0:T(8,128)(2,1)S(1)} collective-permute-done((bf16[128,512]{1,0:T(8,128)(2,1)S(1)}, bf16[128,512]{1,0:T(8,128)(2,1)S(1)}, u32[]{:S(2)}, u32[]{:S(2)}) %collective-permute-start.1) | collective-permute-done | bytes 131104 | tf_op jit(solution)/shard_map/ppermute | solution.py:299
  29.6 2.1 %shard_map.85 = bf16[512,896]{1,0:T(8,128)(2,1)} custom-call(f32[128,512]{1,0:T(8,128)S(1)} %get-tuple-element.19.first, f32[128,128]{1,0:T(8,128)S(1)} %get-tuple-element.36.cosine, f32[128,128]{1,0:T(8,128)S(1)} %get-tuple-element.37.sine, f32[2,128]{1,0:T(2,128)S(1)} %get-tuple-element.20.gains, bf16[3,512,128]{2,1,0:T(8,128)(2,1)S(1)} %get-tuple-element.21.picks, ...), custom_call_target="tpu_custom_call" | custom-call | tf_op jit(solution)/shard_map/pallas_call | solution.py:247
  31.8 14.6 %all-to-all-start.1 = ((bf16[64,8,896]{2,1,0:T(8,128)(2,1)}), bf16[64,8,896]{2,1,0:T(8,128)(2,1)S(1)}, u32[]{:S(2)}, u32[]{:S(2)}) async-start(bf16[64,8,896]{2,1,0:T(8,128)(2,1)} %bitcast.6), calls=%async_computation.1 | async-start | bytes 1835008 | tf_op jit(solution)/shard_map/all_to_all | solution.py:324
  46.4 25.8 %all-to-all-done.1 = bf16[64,8,896]{2,1,0:T(8,128)(2,1)S(1)} async-done(((bf16[64,8,896]{2,1,0:T(8,128)(2,1)}), bf16[64,8,896]{2,1,0:T(8,128)(2,1)S(1)}, u32[]{:S(2)}, u32[]{:S(2)}) %all-to-all-start.1) | async-done | bytes 917536 | tf_op jit(solution)/shard_map/all_to_all | solution.py:324
  72.2 0.5 shard_map.86
  72.7 2.0 %collective-permute-start.4 = (bf16[512,256]{1,0:T(8,128)(2,1)S(1)}, bf16[512,256]{1,0:T(8,128)(2,1)S(1)}, u32[]{:S(2)}, u32[]{:S(2)}) collective-permute-start(bf16[512,256]{1,0:T(8,128)(2,1)S(1)} %get-tuple-element.29), channel_id=1, source_target_pairs={{0,8},{8,0},{16,24},{24,16},{32,40},{40,32},{48,56},{56,48},{64,72... | collective-permute-start | bytes 786440 | tf_op jit(solution)/shard_map/ppermute | solution.py:341
  74.8 0.4 shard_map.87
  75.2 0.9 %collective-permute-done.4.keyvalues = bf16[512,256]{1,0:T(8,128)(2,1)S(1)} collective-permute-done((bf16[512,256]{1,0:T(8,128)(2,1)S(1)}, bf16[512,256]{1,0:T(8,128)(2,1)S(1)}, u32[]{:S(2)}, u32[]{:S(2)}) %collective-permute-start.4) | collective-permute-done | bytes 262176 | tf_op jit(solution)/shard_map/ppermute | solution.py:341
  76.2 1.0 %shard_map.88 = bf16[128,256]{1,0:T(8,128)(2,1)} custom-call(bf16[256,128]{1,0:T(8,128)(2,1)S(1)} %get-tuple-element.26.queries, s32[256,1]{1,0:T(8,128)S(1)} %get-tuple-element.27.query_docs, s32[16,128]{1,0:T(8,128)S(1)} %get-tuple-element.28.key_docs, bf16[512,256]{1,0:T(8,128)(2,1)S(1)} %collective-permute-done.4.keyvalues, ...), custom_call_target="tpu_custom_call" | custom-call | tf_op jit(solution)/shard_map/pallas_call | solution.py:247
  (2 shorter events, 0.0 us)
Async XLA Ops:
  0.0 15.3 %collective-permute-start = (bf16[128,512]{1,0:T(8,128)(2,1)}, bf16[128,512]{1,0:T(8,128)(2,1)S(1)}, u32[]{:S(2)}, u32[]{:S(2)}) collective-permute-start(bf16[128,512]{1,0:T(8,128)(2,1)} %hidden.1), channel_id=1, source_target_pairs={{0,1},{1,0},{2,3},{3,2},{4,5},{5,4},{6,7},{7,6},{8,9},{9,8},{10,11... | collective-permute-start | bytes 393224 | tf_op jit(solution)/shard_map/ppermute | solution.py:279
  8.3 0.9 %copy-start = (bf16[128,512]{1,0:T(8,128)(2,1)S(1)}, bf16[128,512]{1,0:T(8,128)(2,1)}, u32[]{:S(2)}) copy-start(bf16[128,512]{1,0:T(8,128)(2,1)} %hidden.1) | copy-start | bytes 393220
  10.0 15.9 %all-to-all-start = ((bf16[4,128,512]{2,1,0:T(8,128)(2,1)}), bf16[4,128,512]{2,1,0:T(8,128)(2,1)S(1)}, u32[]{:S(2)}, u32[]{:S(2)}) async-start(bf16[4,128,512]{2,1,0:T(8,128)(2,1)} %shard_map.82), calls=%async_computation | async-start | bytes 1048576 | tf_op jit(solution)/shard_map/all_to_all | solution.py:285
  14.0 1.2 %copy-start.1 = (s32[128]{0:T(128)S(1)}, s32[128]{0:T(128)}, u32[]{:S(2)}) copy-start(s32[128]{0:T(128)} %param.9) | copy-start | bytes 1540
  15.3 13.2 %collective-permute-start.3 = (bf16[128,512]{1,0:T(8,128)(2,1)S(1)}, bf16[128,512]{1,0:T(8,128)(2,1)S(1)}, u32[]{:S(2)}, u32[]{:S(2)}) collective-permute-start(bf16[128,512]{1,0:T(8,128)(2,1)S(1)} %collective-permute-done.refs_0_), channel_id=1, source_target_pairs={{0,6},{1,7},{2,0},{3,1},{4,2},{5,3},{6,4},{7,5},{8,14},{9,15},{10,... | collective-permute-start | bytes 393224 | tf_op jit(solution)/shard_map/ppermute | solution.py:299
  19.9 8.6 %collective-permute-start.2 = (bf16[128,512]{1,0:T(8,128)(2,1)S(1)}, bf16[128,512]{1,0:T(8,128)(2,1)S(1)}, u32[]{:S(2)}, u32[]{:S(2)}) collective-permute-start(bf16[128,512]{1,0:T(8,128)(2,1)S(1)} %collective-permute-done.refs_0_), channel_id=1, source_target_pairs={{0,2},{1,3},{2,4},{3,5},{4,6},{5,7},{6,0},{7,1},{8,10},{9,11},{10,... | collective-permute-start | bytes 393224 | tf_op jit(solution)/shard_map/ppermute | solution.py:299
  21.8 7.8 %collective-permute-start.1 = (bf16[128,512]{1,0:T(8,128)(2,1)S(1)}, bf16[128,512]{1,0:T(8,128)(2,1)S(1)}, u32[]{:S(2)}, u32[]{:S(2)}) collective-permute-start(bf16[128,512]{1,0:T(8,128)(2,1)S(1)} %collective-permute-done.refs_0_), channel_id=1, source_target_pairs={{0,4},{1,5},{2,6},{3,7},{4,0},{5,1},{6,2},{7,3},{8,12},{9,13},{10,... | collective-permute-start | bytes 393224 | tf_op jit(solution)/shard_map/ppermute | solution.py:299
  31.8 40.4 %all-to-all-start.1 = ((bf16[64,8,896]{2,1,0:T(8,128)(2,1)}), bf16[64,8,896]{2,1,0:T(8,128)(2,1)S(1)}, u32[]{:S(2)}, u32[]{:S(2)}) async-start(bf16[64,8,896]{2,1,0:T(8,128)(2,1)} %bitcast.6), calls=%async_computation.1 | async-start | bytes 1835008 | tf_op jit(solution)/shard_map/all_to_all | solution.py:324
  72.7 3.4 %collective-permute-start.4 = (bf16[512,256]{1,0:T(8,128)(2,1)S(1)}, bf16[512,256]{1,0:T(8,128)(2,1)S(1)}, u32[]{:S(2)}, u32[]{:S(2)}) collective-permute-start(bf16[512,256]{1,0:T(8,128)(2,1)S(1)} %get-tuple-element.29), channel_id=1, source_target_pairs={{0,8},{8,0},{16,24},{24,16},{32,40},{40,32},{48,56},{56,48},{64,72... | collective-permute-start | bytes 786440 | tf_op jit(solution)/shard_map/ppermute | solution.py:341
